TPU v7x, 32 devices: a whole 2x2x4 slice. The times are simulated.
32 devices in a mesh: rep: 8 (over z, y), fsdp: 4 (over x, core).
Axes of the slice: x: 2, y: 2, z: 4, core: 2. Of those that a mesh axis runs over, the one named last changes fastest.
Arguments:
- tokens: bfloat16 [8, 512, 512], P('rep', 'fsdp'), may hold values from -6 to 6
- states: bfloat16 [8, 256, 512], P('rep', 'fsdp'), may hold values from -6 to 6
- query_w: bfloat16 [512, 384], P('fsdp'), may hold values from -0.0625 to 0.0625
- key_w: bfloat16 [512, 384], P('fsdp'), may hold values from -0.25 to 0.25
- value_w: bfloat16 [512, 384], P('fsdp'), may hold values from -0.25 to 0.25
- out_w: bfloat16 [384, 512], P(None, 'fsdp'), may hold values from -0.875 to 0.875
- cross_query_w: bfloat16 [512, 384], P('fsdp'), may hold values from -0.0625 to 0.0625
- cross_key_w: bfloat16 [512, 384], P('fsdp'), may hold values from -0.25 to 0.25
- cross_value_w: bfloat16 [512, 384], P('fsdp'), may hold values from -0.25 to 0.25
- cross_out_w: bfloat16 [384, 512], P(None, 'fsdp'), may hold values from -0.875 to 0.875
- gate_w: bfloat16 [512, 1024], P('fsdp'), may hold values from -0.25 to 0.25
- up_w: bfloat16 [512, 1024], P('fsdp'), may hold values from -0.25 to 0.25
- down_w: bfloat16 [1024, 512], P('fsdp'), may hold values from -0.375 to 0.375
- self_gain: bfloat16 [512], P('fsdp'), may hold values from 0.5 to 1.5
- cross_gain: bfloat16 [512], P('fsdp'), may hold values from 0.5 to 1.5
- mlp_gain: bfloat16 [512], P('fsdp'), may hold values from 0.5 to 1.5
- bias_table: bfloat16 [32, 6], P('fsdp'), may hold values from -4 to 4
- cotangent: bfloat16 [8, 512, 512], P('rep', 'fsdp'), may hold values from -6 to 6
Outputs:
- output: bfloat16 [8, 512, 512], P('rep', 'fsdp')
- grad_tokens: float32 [8, 512, 512], P('rep', 'fsdp')
- grad_states: float32 [8, 256, 512], P('rep', 'fsdp')
- grad_query_w: float32 [512, 384], P('fsdp')
- grad_key_w: float32 [512, 384], P('fsdp')
- grad_value_w: float32 [512, 384], P('fsdp')
- grad_out_w: float32 [384, 512], P(None, 'fsdp')
- grad_cross_query_w: float32 [512, 384], P('fsdp')
- grad_cross_key_w: float32 [512, 384], P('fsdp')
- grad_cross_value_w: float32 [512, 384], P('fsdp')
- grad_cross_out_w: float32 [384, 512], P(None, 'fsdp')
- grad_gate_w: float32 [512, 1024], P('fsdp')
- grad_up_w: float32 [512, 1024], P('fsdp')
- grad_down_w: float32 [1024, 512], P('fsdp')
- grad_self_gain: float32 [512], P('fsdp')
- grad_cross_gain: float32 [512], P('fsdp')
- grad_mlp_gain: float32 [512], P('fsdp')
- grad_bias_table: float32 [32, 6], P('fsdp')
All inputs are finite; a program needn't handle non-finite values.
Results may differ from a plain program's by a relative error of at most 0.028.
The roundings to bfloat16 on the way count: a program that leaves them out, or rounds other values in their place, can miss the bound.
Values may be sent and summed in bfloat16 or wider, within the bound.
No kernel may reach another device: no remote copies, remote signals or barrier semaphores. Data moves between devices by JAX's collectives and lax.ppermute only.
A program may use at most 128 MiB of HBM per device.

v0:
```python
import math

import jax
import jax.numpy as jnp
from jax import lax
from jax.sharding import PartitionSpec as P

H = 6
DH = 64
BUCKETS = 32
MAXDIST = 128


EPSILON = 1e-06
MASKED = -1000000000.0
HIGHEST = lax.Precision.HIGHEST


def rms_norm(row_block, gain_vec):
    inverse_rms = lax.rsqrt(jnp.mean(row_block * row_block, axis=-1, keepdims=True) + EPSILON)
    return row_block * inverse_rms * gain_vec


def gelu_tanh(values_in):
    return (
        0.5
        * values_in
        * (
            1.0
            + jnp.tanh(
                0.7978845608028654 * (values_in + 0.044715 * values_in * values_in * values_in)
            )
        )
    )


def glu_mix(gate_pre, up_pre):
    return gelu_tanh(gate_pre) * up_pre


def bucket_of(distance):
    exact_span = BUCKETS // 2
    bucket = jnp.minimum(distance, exact_span)
    for power in range(1, exact_span):
        threshold = math.ceil(exact_span * (MAXDIST / exact_span) ** (power / exact_span))
        bucket = bucket + (distance >= threshold).astype(jnp.int32)
    return bucket


def project(row_block, weight_full):
    return jnp.dot(row_block, weight_full, preferred_element_type=jnp.float32)


def outer_sum(left_rows, right_rows):
    return lax.dot_general(
        left_rows, right_rows, (((0,), (0,)), ((), ())), preferred_element_type=jnp.float32
    )


def times_transpose(left_rows, right_rows):
    return lax.dot_general(
        left_rows, right_rows, (((1,), (1,)), ((), ())), preferred_element_type=jnp.float32
    )


def split_heads(row_block):
    return row_block.reshape(row_block.shape[0], H, DH)


def offset_table(table_full, row_start, rows_here, keys_total):
    period = rows_here + keys_total - 1
    residue = jnp.arange(period, dtype=jnp.int32)
    distance = jnp.where(residue < keys_total, row_start - residue, row_start + period - residue)
    bucket = bucket_of(jnp.maximum(distance, 0))
    one_hot = (bucket[None, :] == jnp.arange(BUCKETS, dtype=jnp.int32)[:, None]).astype(jnp.float32)
    return lax.dot_general(
        table_full,
        one_hot,
        (((0,), (0,)), ((), ())),
        precision=HIGHEST,
        preferred_element_type=jnp.float32,
    )


def toeplitz_expand(per_offset, rows_here, keys_total):
    period = per_offset.shape[1]
    tiled = jnp.tile(per_offset, (1, rows_here))[:, : rows_here * (period - 1)]
    return tiled.reshape(per_offset.shape[0], rows_here, period - 1)[:, :, :keys_total]


def position_bias(table_low, row_start, rows_here, keys_total):
    per_offset = offset_table(table_low.astype(jnp.float32), row_start, rows_here, keys_total)
    return toeplitz_expand(per_offset.astype(jnp.bfloat16), rows_here, keys_total)


def bucket_onehot(row_start, rows_here, keys_total):
    distance = (
        row_start
        + jnp.arange(rows_here, dtype=jnp.int32)[:, None]
        - jnp.arange(keys_total, dtype=jnp.int32)[None, :]
    )
    bucket = bucket_of(jnp.maximum(distance, 0))
    one_hot = (bucket[:, :, None] == jnp.arange(BUCKETS, dtype=jnp.int32)[None, None, :]).astype(
        jnp.float32
    )
    return one_hot.reshape(rows_here * keys_total, BUCKETS)


def score_block(query_heads, key_heads, bias_block, allowed):
    scores = jnp.einsum("qhd,khd->hqk", query_heads, key_heads, preferred_element_type=jnp.float32)
    if bias_block is None:
        return scores
    return jnp.where(allowed[None], scores + bias_block.astype(jnp.float32), MASKED)


def attend_forward(queries, keys_all, values_all, bias_block, allowed):
    scores = score_block(split_heads(queries), split_heads(keys_all), bias_block, allowed)
    row_max = jnp.max(scores, axis=-1, keepdims=True)
    lifted = jnp.exp(scores - row_max)
    row_sum = jnp.sum(lifted, axis=-1, keepdims=True)
    attn_probs = (lifted / row_sum).astype(jnp.bfloat16)
    mixed_heads = jnp.einsum(
        "hqk,khd->qhd", attn_probs, split_heads(values_all), preferred_element_type=jnp.float32
    )
    return (mixed_heads.reshape(queries.shape).astype(jnp.bfloat16), row_max + jnp.log(row_sum))


def attend_back(queries, keys_all, values_all, grad_mixed, log_total, bias_block, allowed):
    query_heads = split_heads(queries)
    key_heads = split_heads(keys_all)
    grad_heads = split_heads(grad_mixed)
    scores = score_block(query_heads, key_heads, bias_block, allowed)
    attn_probs = jnp.exp(scores - log_total)
    grad_probs = jnp.einsum(
        "qhd,khd->hqk", grad_heads, split_heads(values_all), preferred_element_type=jnp.float32
    )
    grad_values = jnp.einsum(
        "hqk,qhd->khd",
        attn_probs.astype(jnp.bfloat16),
        grad_heads,
        preferred_element_type=jnp.float32,
    )
    grad_scores = attn_probs * (
        grad_probs - jnp.sum(attn_probs * grad_probs, axis=-1, keepdims=True)
    )
    grad_scores_low = grad_scores.astype(jnp.bfloat16)
    grad_queries = jnp.einsum(
        "hqk,khd->qhd", grad_scores_low, key_heads, preferred_element_type=jnp.float32
    )
    grad_keys = jnp.einsum(
        "hqk,qhd->khd", grad_scores_low, query_heads, preferred_element_type=jnp.float32
    )
    return (
        grad_queries.reshape(queries.shape).astype(jnp.bfloat16),
        grad_keys.reshape(keys_all.shape),
        grad_values.reshape(keys_all.shape),
        grad_scores,
    )


def per_device(
    tokens,
    states,
    query_w,
    key_w,
    value_w,
    out_w,
    cross_query_w,
    cross_key_w,
    cross_value_w,
    cross_out_w,
    gate_w,
    up_w,
    down_w,
    self_gain,
    cross_gain,
    mlp_gain,
    bias_table,
    cotangent,
):
    (
        query_full,
        key_full,
        value_full,
        out_full,
        cross_query_full,
        cross_key_full,
        cross_value_full,
        cross_out_full,
        gate_full,
        up_full,
        down_full,
        self_gain_full,
        cross_gain_full,
        mlp_gain_full,
        table_full,
    ) = (
        lax.all_gather(query_w, "fsdp", axis=0, tiled=True),
        lax.all_gather(key_w, "fsdp", axis=0, tiled=True),
        lax.all_gather(value_w, "fsdp", axis=0, tiled=True),
        lax.all_gather(out_w, "fsdp", axis=1, tiled=True),
        lax.all_gather(cross_query_w, "fsdp", axis=0, tiled=True),
        lax.all_gather(cross_key_w, "fsdp", axis=0, tiled=True),
        lax.all_gather(cross_value_w, "fsdp", axis=0, tiled=True),
        lax.all_gather(cross_out_w, "fsdp", axis=1, tiled=True),
        lax.all_gather(gate_w, "fsdp", axis=0, tiled=True),
        lax.all_gather(up_w, "fsdp", axis=0, tiled=True),
        lax.all_gather(down_w, "fsdp", axis=0, tiled=True),
        lax.all_gather(self_gain, "fsdp", axis=0, tiled=True),
        lax.all_gather(cross_gain, "fsdp", axis=0, tiled=True),
        lax.all_gather(mlp_gain, "fsdp", axis=0, tiled=True),
        lax.all_gather(bias_table, "fsdp", axis=0, tiled=True),
    )
    seq_count, rows_here, width = tokens.shape
    enc_here = states.shape[1]
    token_rows = seq_count * rows_here
    keys_total = rows_here * lax.axis_size("fsdp")
    row_start = lax.axis_index("fsdp") * rows_here
    allowed = (
        jnp.arange(keys_total, dtype=jnp.int32)[None, :]
        <= row_start + jnp.arange(rows_here, dtype=jnp.int32)[:, None]
    )
    inputs_f = tokens.reshape(token_rows, width).astype(jnp.float32)
    states_flat = states.reshape(seq_count * enc_here, width)
    self_gain_f = self_gain_full.astype(jnp.float32)
    normed_one = rms_norm(inputs_f, self_gain_f).astype(jnp.bfloat16)
    queries = project(normed_one, query_full).astype(jnp.bfloat16)
    keys_own = project(normed_one, key_full).astype(jnp.bfloat16)
    values_own = project(normed_one, value_full).astype(jnp.bfloat16)
    inner_width = queries.shape[1]
    query_seq = queries.reshape(seq_count, rows_here, inner_width)
    keys_seq, values_seq = (
        lax.all_gather(
            keys_own.reshape(seq_count, rows_here, inner_width), "fsdp", axis=1, tiled=True
        ),
        lax.all_gather(
            values_own.reshape(seq_count, rows_here, inner_width), "fsdp", axis=1, tiled=True
        ),
    )
    bias_block = position_bias(table_full, row_start, rows_here, keys_total)

    def self_step(packed):
        return attend_forward(packed[0], packed[1], packed[2], bias_block, allowed)

    self_mixed, self_log = lax.map(self_step, (query_seq, keys_seq, values_seq))
    self_flat = self_mixed.reshape(token_rows, inner_width)
    hidden_one = inputs_f + project(self_flat, out_full)
    cross_gain_f = cross_gain_full.astype(jnp.float32)
    normed_two = rms_norm(hidden_one, cross_gain_f).astype(jnp.bfloat16)
    cross_queries = project(normed_two, cross_query_full).astype(jnp.bfloat16)
    cross_keys_own = project(states_flat, cross_key_full).astype(jnp.bfloat16)
    cross_values_own = project(states_flat, cross_value_full).astype(jnp.bfloat16)
    cross_query_seq = cross_queries.reshape(seq_count, rows_here, inner_width)
    cross_keys_seq, cross_values_seq = (
        lax.all_gather(
            cross_keys_own.reshape(seq_count, enc_here, inner_width), "fsdp", axis=1, tiled=True
        ),
        lax.all_gather(
            cross_values_own.reshape(seq_count, enc_here, inner_width), "fsdp", axis=1, tiled=True
        ),
    )

    def cross_step(packed):
        return attend_forward(packed[0], packed[1], packed[2], None, None)

    cross_mixed, cross_log = lax.map(
        cross_step, (cross_query_seq, cross_keys_seq, cross_values_seq)
    )
    cross_flat = cross_mixed.reshape(token_rows, inner_width)
    hidden_two = hidden_one + project(cross_flat, cross_out_full)
    mlp_gain_f = mlp_gain_full.astype(jnp.float32)
    normed_three = rms_norm(hidden_two, mlp_gain_f).astype(jnp.bfloat16)
    gate_pre = project(normed_three, gate_full)
    up_pre = project(normed_three, up_full)
    units = glu_mix(gate_pre, up_pre).astype(jnp.bfloat16)
    result = hidden_two + project(units, down_full)
    (
        query_full,
        key_full,
        value_full,
        out_full,
        cross_query_full,
        cross_key_full,
        cross_value_full,
        cross_out_full,
        gate_full,
        up_full,
        down_full,
        self_gain_full,
        cross_gain_full,
        mlp_gain_full,
        table_full,
    ) = (
        lax.all_gather(query_w, "fsdp", axis=0, tiled=True),
        lax.all_gather(key_w, "fsdp", axis=0, tiled=True),
        lax.all_gather(value_w, "fsdp", axis=0, tiled=True),
        lax.all_gather(out_w, "fsdp", axis=1, tiled=True),
        lax.all_gather(cross_query_w, "fsdp", axis=0, tiled=True),
        lax.all_gather(cross_key_w, "fsdp", axis=0, tiled=True),
        lax.all_gather(cross_value_w, "fsdp", axis=0, tiled=True),
        lax.all_gather(cross_out_w, "fsdp", axis=1, tiled=True),
        lax.all_gather(gate_w, "fsdp", axis=0, tiled=True),
        lax.all_gather(up_w, "fsdp", axis=0, tiled=True),
        lax.all_gather(down_w, "fsdp", axis=0, tiled=True),
        lax.all_gather(self_gain, "fsdp", axis=0, tiled=True),
        lax.all_gather(cross_gain, "fsdp", axis=0, tiled=True),
        lax.all_gather(mlp_gain, "fsdp", axis=0, tiled=True),
        lax.all_gather(bias_table, "fsdp", axis=0, tiled=True),
    )
    bias_block = position_bias(table_full, row_start, rows_here, keys_total)
    self_gain_f = self_gain_full.astype(jnp.float32)
    cross_gain_f = cross_gain_full.astype(jnp.float32)
    mlp_gain_f = mlp_gain_full.astype(jnp.float32)
    grad_output = cotangent.reshape(token_rows, width)
    grad_down_w = outer_sum(units, grad_output)
    grad_units = times_transpose(grad_output, down_full)
    unused_mix, glu_pull = jax.vjp(glu_mix, gate_pre, up_pre)
    grad_gate_f, grad_up_f = glu_pull(grad_units)
    grad_gate = grad_gate_f.astype(jnp.bfloat16)
    grad_up = grad_up_f.astype(jnp.bfloat16)
    grad_gate_w = outer_sum(normed_three, grad_gate)
    grad_up_w = outer_sum(normed_three, grad_up)
    grad_normed_three = times_transpose(grad_gate, gate_full) + times_transpose(grad_up, up_full)
    unused_three, norm_pull_three = jax.vjp(rms_norm, hidden_two, mlp_gain_f)
    grad_hidden_part, grad_mlp_gain = norm_pull_three(grad_normed_three)
    grad_hidden_two = grad_output.astype(jnp.float32) + grad_hidden_part
    grad_cross_branch = grad_hidden_two.astype(jnp.bfloat16)
    grad_cross_out_w = outer_sum(cross_flat, grad_cross_branch)
    grad_cross_mixed = times_transpose(grad_cross_branch, cross_out_full).astype(jnp.bfloat16)

    def cross_back_step(packed):
        grad_q, grad_k, grad_v, grad_unused = attend_back(
            packed[0], packed[1], packed[2], packed[3], packed[4], None, None
        )
        return (grad_q, grad_k, grad_v)

    grad_cross_queries, grad_cross_keys_all, grad_cross_values_all = lax.map(
        cross_back_step,
        (
            cross_query_seq,
            cross_keys_seq,
            cross_values_seq,
            grad_cross_mixed.reshape(seq_count, rows_here, inner_width),
            cross_log,
        ),
    )
    own_cross_keys, own_cross_values = (
        lax.psum_scatter(grad_cross_keys_all, "fsdp", scatter_dimension=1, tiled=True),
        lax.psum_scatter(grad_cross_values_all, "fsdp", scatter_dimension=1, tiled=True),
    )
    grad_cross_keys = own_cross_keys.reshape(seq_count * enc_here, inner_width).astype(jnp.bfloat16)
    grad_cross_values = own_cross_values.reshape(seq_count * enc_here, inner_width).astype(
        jnp.bfloat16
    )
    grad_cross_key_w = outer_sum(states_flat, grad_cross_keys)
    grad_cross_value_w = outer_sum(states_flat, grad_cross_values)
    grad_states = times_transpose(grad_cross_keys, cross_key_full) + times_transpose(
        grad_cross_values, cross_value_full
    )
    grad_cross_query_flat = grad_cross_queries.reshape(token_rows, inner_width)
    grad_cross_query_w = outer_sum(normed_two, grad_cross_query_flat)
    grad_normed_two = times_transpose(grad_cross_query_flat, cross_query_full)
    unused_two, norm_pull_two = jax.vjp(rms_norm, hidden_one, cross_gain_f)
    grad_hidden_piece, grad_cross_gain = norm_pull_two(grad_normed_two)
    grad_hidden_one = grad_hidden_two + grad_hidden_piece
    grad_self_branch = grad_hidden_one.astype(jnp.bfloat16)
    grad_out_w = outer_sum(self_flat, grad_self_branch)
    grad_self_mixed = times_transpose(grad_self_branch, out_full).astype(jnp.bfloat16)
    bucket_table = bucket_onehot(row_start, rows_here, keys_total)

    def self_back_step(packed):
        grad_q, grad_k, grad_v, grad_scores = attend_back(
            packed[0], packed[1], packed[2], packed[3], packed[4], bias_block, allowed
        )
        bucket_sums = jnp.dot(
            grad_scores.reshape(grad_scores.shape[0], rows_here * keys_total),
            bucket_table,
            precision=HIGHEST,
            preferred_element_type=jnp.float32,
        )
        return (grad_q, grad_k, grad_v, bucket_sums)

    grad_queries, grad_keys_all, grad_values_all, bucket_all = lax.map(
        self_back_step,
        (
            query_seq,
            keys_seq,
            values_seq,
            grad_self_mixed.reshape(seq_count, rows_here, inner_width),
            self_log,
        ),
    )
    own_keys, own_values = (
        lax.psum_scatter(grad_keys_all, "fsdp", scatter_dimension=1, tiled=True),
        lax.psum_scatter(grad_values_all, "fsdp", scatter_dimension=1, tiled=True),
    )
    grad_keys = own_keys.reshape(token_rows, inner_width).astype(jnp.bfloat16)
    grad_values = own_values.reshape(token_rows, inner_width).astype(jnp.bfloat16)
    grad_query_flat = grad_queries.reshape(token_rows, inner_width)
    grad_bias_table = jnp.transpose(jnp.sum(bucket_all, axis=0))
    grad_query_w = outer_sum(normed_one, grad_query_flat)
    grad_key_w = outer_sum(normed_one, grad_keys)
    grad_value_w = outer_sum(normed_one, grad_values)
    grad_normed_one = (
        times_transpose(grad_query_flat, query_full)
        + times_transpose(grad_keys, key_full)
        + times_transpose(grad_values, value_full)
    )
    unused_one, norm_pull_one = jax.vjp(rms_norm, inputs_f, self_gain_f)
    grad_input_piece, grad_self_gain = norm_pull_one(grad_normed_one)
    grad_tokens = grad_hidden_one + grad_input_piece
    (
        own_query,
        own_key,
        own_value,
        own_out,
        own_cross_query,
        own_cross_key,
        own_cross_value,
        own_cross_out,
        own_gate,
        own_up,
        own_down,
        own_self_gain,
        own_cross_gain,
        own_mlp_gain,
        own_table,
    ) = (
        lax.psum_scatter(
            grad_query_w.astype(jnp.bfloat16), "fsdp", scatter_dimension=0, tiled=True
        ).astype(jnp.float32),
        lax.psum_scatter(
            grad_key_w.astype(jnp.bfloat16), "fsdp", scatter_dimension=0, tiled=True
        ).astype(jnp.float32),
        lax.psum_scatter(
            grad_value_w.astype(jnp.bfloat16), "fsdp", scatter_dimension=0, tiled=True
        ).astype(jnp.float32),
        lax.psum_scatter(
            grad_out_w.astype(jnp.bfloat16), "fsdp", scatter_dimension=1, tiled=True
        ).astype(jnp.float32),
        lax.psum_scatter(
            grad_cross_query_w.astype(jnp.bfloat16), "fsdp", scatter_dimension=0, tiled=True
        ).astype(jnp.float32),
        lax.psum_scatter(
            grad_cross_key_w.astype(jnp.bfloat16), "fsdp", scatter_dimension=0, tiled=True
        ).astype(jnp.float32),
        lax.psum_scatter(
            grad_cross_value_w.astype(jnp.bfloat16), "fsdp", scatter_dimension=0, tiled=True
        ).astype(jnp.float32),
        lax.psum_scatter(
            grad_cross_out_w.astype(jnp.bfloat16), "fsdp", scatter_dimension=1, tiled=True
        ).astype(jnp.float32),
        lax.psum_scatter(
            grad_gate_w.astype(jnp.bfloat16), "fsdp", scatter_dimension=0, tiled=True
        ).astype(jnp.float32),
        lax.psum_scatter(
            grad_up_w.astype(jnp.bfloat16), "fsdp", scatter_dimension=0, tiled=True
        ).astype(jnp.float32),
        lax.psum_scatter(
            grad_down_w.astype(jnp.bfloat16), "fsdp", scatter_dimension=0, tiled=True
        ).astype(jnp.float32),
        lax.psum_scatter(
            grad_self_gain.astype(jnp.bfloat16), "fsdp", scatter_dimension=0, tiled=True
        ).astype(jnp.float32),
        lax.psum_scatter(
            grad_cross_gain.astype(jnp.bfloat16), "fsdp", scatter_dimension=0, tiled=True
        ).astype(jnp.float32),
        lax.psum_scatter(
            grad_mlp_gain.astype(jnp.bfloat16), "fsdp", scatter_dimension=0, tiled=True
        ).astype(jnp.float32),
        lax.psum_scatter(
            grad_bias_table.astype(jnp.bfloat16), "fsdp", scatter_dimension=0, tiled=True
        ).astype(jnp.float32),
    )
    (
        sum_query,
        sum_key,
        sum_value,
        sum_out,
        sum_cross_query,
        sum_cross_key,
        sum_cross_value,
        sum_cross_out,
        sum_gate,
        sum_up,
        sum_down,
        sum_self_gain,
        sum_cross_gain,
        sum_mlp_gain,
        sum_table,
    ) = lax.psum(
        (
            own_query,
            own_key,
            own_value,
            own_out,
            own_cross_query,
            own_cross_key,
            own_cross_value,
            own_cross_out,
            own_gate,
            own_up,
            own_down,
            own_self_gain,
            own_cross_gain,
            own_mlp_gain,
            own_table,
        ),
        "rep",
    )
    return (
        result.reshape(seq_count, rows_here, width).astype(jnp.bfloat16),
        grad_tokens.reshape(seq_count, rows_here, width),
        grad_states.reshape(seq_count, enc_here, width),
        sum_query,
        sum_key,
        sum_value,
        sum_out,
        sum_cross_query,
        sum_cross_key,
        sum_cross_value,
        sum_cross_out,
        sum_gate,
        sum_up,
        sum_down,
        sum_self_gain,
        sum_cross_gain,
        sum_mlp_gain,
        sum_table,
    )


def solution(mesh):
    in_specs = (
        P("rep", "fsdp", None),
        P("rep", "fsdp", None),
        P("fsdp", None),
        P("fsdp", None),
        P("fsdp", None),
        P(None, "fsdp"),
        P("fsdp", None),
        P("fsdp", None),
        P("fsdp", None),
        P(None, "fsdp"),
        P("fsdp", None),
        P("fsdp", None),
        P("fsdp", None),
        P("fsdp"),
        P("fsdp"),
        P("fsdp"),
        P("fsdp", None),
        P("rep", "fsdp", None),
    )
    out_specs = (
        P("rep", "fsdp", None),
        P("rep", "fsdp", None),
        P("rep", "fsdp", None),
        P("fsdp", None),
        P("fsdp", None),
        P("fsdp", None),
        P(None, "fsdp"),
        P("fsdp", None),
        P("fsdp", None),
        P("fsdp", None),
        P(None, "fsdp"),
        P("fsdp", None),
        P("fsdp", None),
        P("fsdp", None),
        P("fsdp"),
        P("fsdp"),
        P("fsdp"),
        P("fsdp", None),
    )
    return jax.shard_map(
        per_device, mesh=mesh, in_specs=in_specs, out_specs=out_specs, check_vma=False
    )
```

profile of v0, /device:TPU:0, one launch (start us, length us, event | category | flops | bytes accessed | tf_op | source)
XLA Modules:
  0.0 669.6 jit_solution(15560784847504156890)
XLA Ops:
  10.6 6.1 all-gather.4
  16.7 8.6 %all_gather.76 = bf16[512,384]{1,0:T(8,128)(2,1)S(1)} all-gather(bf16[128,384]{1,0:T(8,128)(2,1)} %param.21), channel_id=1, replica_groups=mesh['rep'=8,'fsdp'=4] {'fsdp'}, dimensions={0}, use_global_device_ids=true | all-gather | bytes 491520 | tf_op jit(solution)/shard_map/all_gather | solution.py:199
  27.2 7.3 %all-gather.1 = bf16[512,384]{1,0:T(8,128)(2,1)S(1)} all-gather(bf16[128,384]{1,0:T(8,128)(2,1)S(1)} %convolution_convert_fusion.18), channel_id=3, replica_groups=mesh['rep'=8,'fsdp'=4] {'fsdp'}, dimensions={0}, use_global_device_ids=true | all-gather | bytes 491520 | tf_op jit(solution)/shard_map/all_gather | solution.py:233
  34.7 6.6 all_gather.75
  42.6 5.2 all_gather.78
  49.9 3.5 reshape.464
  53.6 6.7 %all_gather.73 = bf16[512,384]{1,0:T(8,128)(2,1)S(1)} all-gather(bf16[128,384]{1,0:T(8,128)(2,1)S(1)} %copy-done.58), channel_id=1, replica_groups=mesh['rep'=8,'fsdp'=4] {'fsdp'}, dimensions={0}, use_global_device_ids=true | all-gather | bytes 491520 | tf_op jit(solution)/shard_map/all_gather | solution.py:200
  61.3 8.0 %all-gather = bf16[512,384]{1,0:T(8,128)(2,1)S(1)} all-gather(bf16[128,384]{1,0:T(8,128)(2,1)S(1)} %convolution_convert_fusion.20), channel_id=2, replica_groups=mesh['rep'=8,'fsdp'=4] {'fsdp'}, dimensions={0}, use_global_device_ids=true | all-gather | bytes 491520 | tf_op jit(solution)/shard_map/all_gather | solution.py:236
  70.3 6.6 all_gather.79
  79.0 5.0 all-gather.5
  84.1 6.5 all_gather.83
  91.8 6.7 %all_gather.84 = bf16[512,384]{1,0:T(8,128)(2,1)S(1)} all-gather(bf16[128,384]{1,0:T(8,128)(2,1)S(1)} %copy-done.61), channel_id=1, replica_groups=mesh['rep'=8,'fsdp'=4] {'fsdp'}, dimensions={0}, use_global_device_ids=true | all-gather | bytes 491520 | tf_op jit(solution)/shard_map/all_gather | solution.py:203
  99.5 5.6 all-gather.3
  105.3 6.6 all_gather.80
  112.9 5.6 all-gather.2
  118.7 6.6 all_gather.86
  125.3 5.2 all-gather.6
  132.7 2.4 fusion.121
  137.4 3.2 multiply_convert_fusion.1
  161.8 118.4 %all-reduce.11 = (bf16[1,256,384]{2,0,1:T(2,128)(2,1)}, bf16[1,256,384]{2,0,1:T(2,128)(2,1)S(1)}) all-reduce(f32[1,256,384]{2,0,1:T(1,128)S(1)} %copy.87, f32[1,256,384]{2,0,1:T(1,128)S(1)} %copy.89), channel_id=8, replica_groups=mesh['rep'=8,'fsdp'=4] {'fsdp'}, use_global_device_ids=true, to_apply=%region_14.15.clone | all-reduce | flops 196608 | bytes 1179648
  305.0 4.3 fusion.13
  312.6 15.2 %reduce-scatter.44.cloned.1.call-done = bf16[128,384]{1,0:T(8,128)(2,1)} async-done(((bf16[512,384]{1,0:T(8,128)(2,1)}), bf16[128,384]{1,0:T(8,128)(2,1)}) %reduce-scatter.44.cloned.1.call-update) | async-done | bytes 98320
  328.8 22.5 %reduce-scatter.32.cloned.1.call-done = bf16[128,384]{1,0:T(8,128)(2,1)} async-done(((bf16[512,384]{1,0:T(8,128)(2,1)}), bf16[128,384]{1,0:T(8,128)(2,1)}) %reduce-scatter.32.cloned.1.call-update) | async-done | bytes 98320 | tf_op jit(solution)/shard_map/reduce_scatter | solution.py:441
  351.3 23.9 %reduce-scatter.26.cloned.1.call-done = bf16[128,384]{1,0:T(8,128)(2,1)} async-done(((bf16[512,384]{1,0:T(8,128)(2,1)}), bf16[128,384]{1,0:T(8,128)(2,1)}) %reduce-scatter.26.cloned.1.call-update) | async-done | bytes 98320 | tf_op jit(solution)/shard_map/reduce_scatter | solution.py:429
  375.2 26.0 %reduce-scatter.22.cloned.1.call-done = f32[1,128,384]{1,2,0:T(8,128)} async-done(((f32[1,512,384]{1,2,0:T(8,128)}), f32[1,128,384]{1,2,0:T(8,128)}) %reduce-scatter.22.cloned.1.call-update) | async-done | bytes 196624 | tf_op jit(solution)/shard_map/reduce_scatter | solution.py:394
  405.0 10.1 %all-reduce.8 = (bf16[512]{0:T(512)(128)(2,1)S(1)}, bf16[512]{0:T(512)(128)(2,1)S(1)}, bf16[512]{0:T(512)(128)(2,1)S(1)}, bf16[32,6]{1,0:T(8,128)(2,1)S(1)}) all-reduce(bf16[512]{0:T(512)(128)(2,1)S(1)} %get-tuple-element.202, bf16[512]{0:T(512)(128)(2,1)S(1)} %copy-done.76, ...), channel_id=21, replica_groups=mesh['rep'=8,'fsdp'=4] {'fsdp'}, use_global_device_ids=true, to_apply=%region_39.40.clone | all-reduce | flops 1728 | bytes 6912
  416.1 12.4 %reduce-scatter.34.cloned.1.call-done = bf16[128,1024]{1,0:T(8,128)(2,1)} async-done(((bf16[512,1024]{1,0:T(8,128)(2,1)}), bf16[128,1024]{1,0:T(8,128)(2,1)}) %reduce-scatter.34.cloned.1.call-update) | async-done | bytes 262160 | tf_op jit(solution)/shard_map/reduce_scatter | solution.py:453
  428.5 27.7 %reduce-scatter.36.cloned.1.call-done = bf16[128,1024]{1,0:T(8,128)(2,1)} async-done(((bf16[512,1024]{1,0:T(8,128)(2,1)}), bf16[128,1024]{1,0:T(8,128)(2,1)}) %reduce-scatter.36.cloned.1.call-update) | async-done | bytes 262160 | tf_op jit(solution)/shard_map/reduce_scatter | solution.py:456
  456.2 27.3 %reduce-scatter.38.cloned.1.call-done = bf16[256,512]{1,0:T(8,128)(2,1)} async-done(((bf16[1024,512]{1,0:T(8,128)(2,1)}), bf16[256,512]{1,0:T(8,128)(2,1)}) %reduce-scatter.38.cloned.1.call-update) | async-done | bytes 262160 | tf_op jit(solution)/shard_map/reduce_scatter | solution.py:459
  483.5 23.9 %reduce-scatter.30.cloned.1.call-done = bf16[128,384]{1,0:T(8,128)(2,1)} async-done(((bf16[512,384]{1,0:T(8,128)(2,1)}), bf16[128,384]{1,0:T(8,128)(2,1)}) %reduce-scatter.30.cloned.1.call-update) | async-done | bytes 98320 | tf_op jit(solution)/shard_map/reduce_scatter | solution.py:435
  507.4 24.0 %reduce-scatter.28.cloned.1.call-done = bf16[128,384]{1,0:T(8,128)(2,1)} async-done(((bf16[512,384]{1,0:T(8,128)(2,1)}), bf16[128,384]{1,0:T(8,128)(2,1)}) %reduce-scatter.28.cloned.1.call-update) | async-done | bytes 98320 | tf_op jit(solution)/shard_map/reduce_scatter | solution.py:432
  531.3 130.1 %all-reduce.12 = (f32[128,384]{1,0:T(8,128)}, f32[128,384]{1,0:T(8,128)}, f32[128,384]{1,0:T(8,128)}, f32[384,128]{1,0:T(8,128)}, f32[128,384]{1,0:T(8,128)}, /*...) all-reduce(bf16[128,384]{1,0:T(8,128)(2,1)S(1)} %copy-done.56, ...), channel_id=1, replica_groups=mesh['rep'=8,'fsdp'=4] {'rep'}, use_global_device_ids=true, to_apply=%region_17.18 | all-reduce | flops 786864 | bytes 4722048 | tf_op jit(solution)/shard_map/psum | solution.py:491
  (312 shorter events, 74.7 us)
Async XLA Ops:
  7.2 92.1 %copy-start = (bf16[1,64,512]{2,1,0:T(8,128)(2,1)S(1)}, bf16[1,64,512]{2,1,0:T(8,128)(2,1)}, u32[]{:S(2)}) copy-start(bf16[1,64,512]{2,1,0:T(8,128)(2,1)} %param.19) | copy-start | bytes 196612
  7.2 125.5 %all-gather.11.cloned.1.call-start = ((), (), s32[]{:S(2)}) async-start(), calls=%async_computation.13 | async-start | bytes 1310720 | tf_op jit(solution)/shard_map/all_gather | solution.py:206
  7.9 127.1 %all-gather.13.cloned.1.call-start = ((), (), s32[]{:S(2)}) async-start(), calls=%async_computation.14 | async-start | bytes 1310720 | tf_op jit(solution)/shard_map/all_gather | solution.py:207
  8.7 128.7 %all-gather.15.cloned.1.call-start = ((), (), s32[]{:S(2)}) async-start(), calls=%async_computation.15 | async-start | bytes 1310720 | tf_op jit(solution)/shard_map/all_gather | solution.py:208
  9.4 32.7 %copy-start.1 = (bf16[1,128,512]{2,1,0:T(8,128)(2,1)S(1)}, bf16[1,128,512]{2,1,0:T(8,128)(2,1)}, u32[]{:S(2)}) copy-start(bf16[1,128,512]{2,1,0:T(8,128)(2,1)} %param.18) | copy-start | bytes 393220
  9.4 292.2 %reduce-scatter.24.cloned.1.call-start = ((), (), s32[]{:S(2)}) async-start(), calls=%async_computation.17 | async-start | bytes 983040 | tf_op jit(solution)/shard_map/reduce_scatter | solution.py:395
  10.5 31.8 %copy-start.82 = (f32[128]{0:T(128)}, f32[128]{0:T(128)S(1)}, u32[]{:S(2)}) copy-start(f32[128]{0:T(128)S(1)} %fusion.42) | copy-start | bytes 1540
  10.6 49.7 %copy-start.66 = (f32[128]{0:T(128)}, f32[128]{0:T(128)S(1)}, u32[]{:S(2)}) copy-start(f32[128]{0:T(128)S(1)} %fusion.110) | copy-start | bytes 1540
  34.7 42.1 %copy-start.26 = (bf16[512,384]{0,1:T(8,128)(2,1)}, bf16[512,384]{0,1:T(8,128)(2,1)S(1)}, u32[]{:S(2)}) copy-start(bf16[512,384]{0,1:T(8,128)(2,1)S(1)} %copy.81) | copy-start | bytes 1179652
  42.5 34.3 %copy-start.38 = (bf16[128,384]{0,1:T(8,128)(2,1)}, bf16[128,384]{0,1:T(8,128)(2,1)S(1)}, u32[]{:S(2)}) copy-start(bf16[128,384]{0,1:T(8,128)(2,1)S(1)} %copy.80) | copy-start | bytes 294916
  79.0 32.9 %copy-start.70 = (f32[128]{0:T(128)}, f32[128]{0:T(128)S(1)}, u32[]{:S(2)}) copy-start(f32[128]{0:T(128)S(1)} %fusion.111) | copy-start | bytes 1540
  91.8 38.7 %copy-start.41 = (bf16[128,384]{0,1:T(8,128)(2,1)}, bf16[128,384]{0,1:T(8,128)(2,1)S(1)}, u32[]{:S(2)}) copy-start(bf16[128,384]{0,1:T(8,128)(2,1)S(1)} %copy.83) | copy-start | bytes 294916
  91.8 26.8 %copy-start.63 = (bf16[384,128]{1,0:T(8,128)(2,1)S(1)}, bf16[384,128]{1,0:T(8,128)(2,1)}, u32[]{:S(2)}) copy-start(bf16[384,128]{1,0:T(8,128)(2,1)} %param.27) | copy-start | bytes 294916
  148.9 160.4 %reduce-scatter.46.cloned.1.call-start = ((), (), s32[]{:S(2)}) async-start(), calls=%async_computation.28 | async-start | bytes 491520
  151.9 158.5 %reduce-scatter.40.cloned.1.call-start = ((), (), s32[]{:S(2)}) async-start(), calls=%async_computation.25 | async-start | bytes 491520
  159.9 151.7 %reduce-scatter.42.cloned.1.call-start = ((), (), s32[]{:S(2)}) async-start(), calls=%async_computation.26 | async-start | bytes 491520
  282.5 45.3 %reduce-scatter.44.cloned.1.call-start = ((), (), s32[]{:S(2)}) async-start(), calls=%async_computation.27 | async-start | bytes 491520
  283.9 67.4 %reduce-scatter.32.cloned.1.call-start = ((), (), s32[]{:S(2)}) async-start(), calls=%async_computation.21 | async-start | bytes 491520 | tf_op jit(solution)/shard_map/reduce_scatter | solution.py:441
  286.7 88.5 %reduce-scatter.26.cloned.1.call-start = ((), (), s32[]{:S(2)}) async-start(), calls=%async_computation.18 | async-start | bytes 491520 | tf_op jit(solution)/shard_map/reduce_scatter | solution.py:429
  290.4 110.8 %reduce-scatter.22.cloned.1.call-start = ((), (), s32[]{:S(2)}) async-start(), calls=%async_computation.16 | async-start | bytes 983040 | tf_op jit(solution)/shard_map/reduce_scatter | solution.py:394
  291.7 136.8 %reduce-scatter.34.cloned.1.call-start = ((), (), s32[]{:S(2)}) async-start(), calls=%async_computation.22 | async-start | bytes 1310720 | tf_op jit(solution)/shard_map/reduce_scatter | solution.py:453
  293.2 162.9 %reduce-scatter.36.cloned.1.call-start = ((), (), s32[]{:S(2)}) async-start(), calls=%async_computation.23 | async-start | bytes 1310720 | tf_op jit(solution)/shard_map/reduce_scatter | solution.py:456
  294.8 188.7 %reduce-scatter.38.cloned.1.call-start = ((), (), s32[]{:S(2)}) async-start(), calls=%async_computation.24 | async-start | bytes 1310720 | tf_op jit(solution)/shard_map/reduce_scatter | solution.py:459
  296.3 211.1 %reduce-scatter.30.cloned.1.call-start = ((), (), s32[]{:S(2)}) async-start(), calls=%async_computation.20 | async-start | bytes 491520 | tf_op jit(solution)/shard_map/reduce_scatter | solution.py:435
  303.7 227.6 %reduce-scatter.28.cloned.1.call-start = ((), (), s32[]{:S(2)}) async-start(), calls=%async_computation.19 | async-start | bytes 491520 | tf_op jit(solution)/shard_map/reduce_scatter | solution.py:432
  309.3 94.0 %copy-start.15 = (bf16[512,384]{1,0:T(8,128)(2,1)S(1)}, bf16[512,384]{1,0:T(8,128)(2,1)}, u32[]{:S(2)}) copy-start(bf16[512,384]{1,0:T(8,128)(2,1)} %copy-done.14) | copy-start | bytes 1179652
  309.3 95.2 %copy-start.9 = (bf16[512,384]{1,0:T(8,128)(2,1)S(1)}, bf16[512,384]{1,0:T(8,128)(2,1)}, u32[]{:S(2)}) copy-start(bf16[512,384]{1,0:T(8,128)(2,1)} %copy-done.8) | copy-start | bytes 1179652
  309.3 95.2 %copy-start.48 = (f32[1,128,384]{1,2,0:T(8,128)S(1)}, f32[1,128,384]{1,2,0:T(8,128)}, u32[]{:S(2)}) copy-start(f32[1,128,384]{1,2,0:T(8,128)} %reduce-scatter.24.cloned.1.call-done) | copy-start | bytes 589828
  328.8 76.2 %copy-start.75 = (bf16[512]{0:T(512)(128)(2,1)S(1)}, bf16[512]{0:T(512)(128)(2,1)}, u32[]{:S(2)}) copy-start(bf16[512]{0:T(512)(128)(2,1)} %get-tuple-element.198) | copy-start | bytes 3076
  328.8 76.2 %copy-start.76 = (bf16[512]{0:T(512)(128)(2,1)S(1)}, bf16[512]{0:T(512)(128)(2,1)}, u32[]{:S(2)}) copy-start(bf16[512]{0:T(512)(128)(2,1)} %get-tuple-element.200) | copy-start | bytes 3076
  403.3 128.1 %copy-start.55 = (bf16[128,384]{1,0:T(8,128)(2,1)S(1)}, bf16[128,384]{1,0:T(8,128)(2,1)}, u32[]{:S(2)}) copy-start(bf16[128,384]{1,0:T(8,128)(2,1)} %reduce-scatter.32.cloned.1.call-done) | copy-start | bytes 294916
  403.3 128.1 %copy-start.56 = (bf16[128,384]{1,0:T(8,128)(2,1)S(1)}, bf16[128,384]{1,0:T(8,128)(2,1)}, u32[]{:S(2)}) copy-start(bf16[128,384]{1,0:T(8,128)(2,1)} %reduce-scatter.26.cloned.1.call-done) | copy-start | bytes 294916
  (72 other events, 375.1 us)
Sparse Core Ops, SparseCore 0:
  9.6 20.4 all-gather.10
  31.7 17.8 all-gather.12
  51.1 18.1 all-gather.14
  149.1 27.3 reduce-scatter.23
  179.0 23.0 reduce-scatter.45
  204.6 22.4 reduce-scatter.39
  282.6 21.6 reduce-scatter.41
  306.9 20.8 reduce-scatter.43
  330.4 20.8 reduce-scatter.31
  354.3 20.8 reduce-scatter.25
  377.9 23.2 reduce-scatter.21
  403.6 24.8 reduce-scatter.33
  431.2 24.9 reduce-scatter.35
  458.5 24.8 reduce-scatter.37
  486.5 20.8 reduce-scatter.29
  510.5 20.8 reduce-scatter.27
where the time goes:
time: 671 us; the launch traced here: 670 us
  blocking collectives  361 us (54%)
  waiting for transfers between devices  205 us (31%)
  matrix products  48.2 us (7%)
  local copies, waits for them, and re-layouts  30 us (4%)
  between operations  17.2 us (3%)
    psum x1, blocking collectives, per_device(): lax.psum((own_query, own_key, own_value, own_out, own_cross_query, own_cr...  130 us
    unnamed x2, blocking collectives  128 us
    reduce_scatter x1, waiting for transfers between devices, per_device(): lax.psum_scatter(grad_up_w.astype(jnp.bfloat16), 'fsdp', scatter_dimensio...  27.7 us
    reduce_scatter x1, waiting for transfers between devices, per_device(): lax.psum_scatter(grad_down_w.astype(jnp.bfloat16), 'fsdp', scatter_dimens...  27.3 us
    reduce_scatter x1, waiting for transfers between devices, per_device(): lax.psum_scatter(grad_keys_all, 'fsdp', scatter_dimension=1, tiled=True)  26 us
    reduce_scatter x1, waiting for transfers between devices, per_device(): lax.psum_scatter(grad_key_w.astype(jnp.bfloat16), 'fsdp', scatter_dimensi...  24 us
    reduce_scatter x1, waiting for transfers between devices, per_device(): lax.psum_scatter(grad_query_w.astype(jnp.bfloat16), 'fsdp', scatter_dimen...  23.9 us
    reduce_scatter x1, waiting for transfers between devices, per_device(): lax.psum_scatter(grad_value_w.astype(jnp.bfloat16), 'fsdp', scatter_dimen...  23.9 us
  transfers between devices with their start and end apart: 16, of which 9 were waited for; matrix products, arithmetic and copies ran while one was open for 10% of the time, Pallas kernels for 0%

commit v1 on v0

v1 whole, which is shorter than its diff:
```python
import functools
import math

import jax
import jax.numpy as jnp
from jax import lax
from jax.experimental import pallas as pl
from jax.experimental.pallas import tpu as pltpu
from jax.sharding import PartitionSpec as P

H = 6
DH = 64
PAIRS = H // 2
BUCKETS = 32
MAXDIST = 128
EPSILON = 1e-06
MASKED = -1000000000.0
BLOCK = 128
HALF = 256
GROUP = 4
HIGHEST = lax.Precision.HIGHEST
F32 = jnp.float32
BF16 = jnp.bfloat16


def dot(a, b):
    return jnp.dot(a, b, preferred_element_type=F32)


def dot_t(a, b):
    return lax.dot_general(a, b, (((1,), (1,)), ((), ())), preferred_element_type=F32)


def t_dot(a, b):
    return lax.dot_general(a, b, (((0,), (0,)), ((), ())), preferred_element_type=F32)


def own(f, size):
    return pl.ds(pl.multiple_of(f * size, size), size)


def place_rows(dst, pieces, f, first, size):
    for k, piece in enumerate(pieces):
        dst[own(f ^ k, size), :] = piece[first : first + size, :].astype(dst.dtype)


def place_columns(dst, pieces, f, first, rows):
    for k, piece in enumerate(pieces):
        dst[:, own(f ^ k, piece.shape[1])] = piece[first : first + rows, :]


def bucket_of(distance):
    exact_span = BUCKETS // 2
    bucket = jnp.minimum(distance, exact_span)
    for power in range(1, exact_span):
        threshold = math.ceil(exact_span * (MAXDIST / exact_span) ** (power / exact_span))
        bucket = bucket + (distance >= threshold).astype(jnp.int32)
    return bucket


def offset_onehot(rows, axis):
    shape = (rows, 4 * BLOCK) if axis == 1 else (4 * BLOCK, rows)
    m = lax.broadcasted_iota(jnp.int32, shape, axis)
    n = jnp.where(m < 2 * BLOCK, BLOCK - m, 5 * BLOCK - m)
    bucket = bucket_of(jnp.maximum(n, 0))
    return (bucket == lax.broadcasted_iota(jnp.int32, shape, 1 - axis)).astype(F32)


def rms(v):
    return lax.rsqrt(jnp.mean(v * v, axis=-1, keepdims=True) + EPSILON)


def head_lanes(rows):
    lane = lax.broadcasted_iota(jnp.int32, (rows, 2 * DH), 1)
    return lane < DH


def only_head(pair, hd):
    low = head_lanes(pair.shape[0])
    zero = jnp.zeros_like(pair)
    return jnp.where(low, pair, zero) if hd == 0 else jnp.where(low, zero, pair)


def softmax(s):
    lifted = jnp.exp(s - jnp.max(s, axis=-1, keepdims=True))
    return lifted * (1.0 / jnp.sum(lifted, axis=-1, keepdims=True))


def norm_back(v, gain, q):
    r = rms(v)
    u = q * gain
    vr = v * r
    return r * (u - vr * jnp.mean(vr * u, axis=-1, keepdims=True)), q * vr


def self_forward(
    f_ref, t0, t1, t2, t3, w0, w1, w2, w3,
    normed_ref, qkv_ref, probs_ref, mixed_ref, aux_ref,
    x_s, w_s, band_s,
):
    f = f_ref[0]
    tokens, weights = (t0, t1, t2, t3), (w0, w1, w2, w3)
    length = x_s.shape[0]
    rows = length // GROUP
    inner = H * DH
    place_rows(x_s, tokens, f, 0, rows)
    place_rows(w_s, weights, f, 0, w0.shape[0])
    aux = sum(t[rows : rows + 16, :].astype(F32) for t in tokens)
    aux_ref[...] = aux
    for hb in range(length // HALF):
        at = slice(hb * HALF, (hb + 1) * HALF)
        x = x_s[at, :].astype(F32)
        normed = (x * rms(x) * aux[0:1, :]).astype(BF16)
        normed_ref[at, :] = normed
        qkv_ref[at, :] = dot(normed, w_s[...]).astype(BF16)
    per_offset = jnp.dot(
        aux[8:16, 0:BLOCK], offset_onehot(BLOCK, 1), precision=HIGHEST, preferred_element_type=F32
    )
    row = lax.broadcasted_iota(jnp.int32, (BLOCK, 2 * BLOCK), 0)
    col = lax.broadcasted_iota(jnp.int32, (BLOCK, 2 * BLOCK), 1)
    for h in range(H):
        spread = jnp.broadcast_to(per_offset[h : h + 1, :], (BLOCK, 4 * BLOCK))
        skewed = pltpu.roll(spread, 0, 1, stride=1, stride_axis=0)[:, : 2 * BLOCK]
        band_s[h] = jnp.where(col - BLOCK > row, MASKED, skewed)
    for p in range(PAIRS):
        k2 = qkv_ref[:, inner + p * BLOCK : inner + (p + 1) * BLOCK]
        v2 = qkv_ref[:, 2 * inner + p * BLOCK : 2 * inner + (p + 1) * BLOCK]
        v_only = [only_head(v2, hd) for hd in range(2)]
        for hb in range(length // HALF):
            q2 = qkv_ref[hb * HALF : (hb + 1) * HALF, p * BLOCK : (p + 1) * BLOCK]
            scores = [dot_t(only_head(q2, hd), k2[: (hb + 1) * HALF, :]) for hd in range(2)]
            for sub in range(2):
                rb = 2 * hb + sub
                seen = (rb + 1) * BLOCK
                out = jnp.zeros((BLOCK, BLOCK), F32)
                for hd in range(2):
                    h = 2 * p + hd
                    s = scores[hd][sub * BLOCK : (sub + 1) * BLOCK, :seen]
                    if rb == 0:
                        s = s + band_s[h, :, BLOCK:]
                    elif rb == 1:
                        s = s + band_s[h]
                    else:
                        far = seen - 2 * BLOCK
                        s = jnp.concatenate(
                            [s[:, :far] + per_offset[h : h + 1, 0:1], s[:, far:] + band_s[h]], axis=1
                        )
                    probs = softmax(s).astype(BF16)
                    probs_ref[h, rb * BLOCK : seen, :seen] = probs
                    out = out + dot(probs, v_only[hd][:seen, :])
                mixed_ref[rb * BLOCK : seen, p * BLOCK : (p + 1) * BLOCK] = out.astype(BF16)


def cross_forward(
    f_ref, t0, t1, t2, t3, mixed_ref, aux_ref, w0, w1, w2, w3, o0, o1, o2, o3, s0, s1, s2, s3,
    h1_ref, n2_ref, cq_ref, ckv_ref, probs_ref, cmixed_ref, h2_ref, n3_ref,
    x_s, w_s, out_s, co_s, states_s,
):
    f = f_ref[0]
    length = x_s.shape[0]
    inner = H * DH
    place_rows(x_s, (t0, t1, t2, t3), f, 0, length // GROUP)
    place_rows(w_s, (w0, w1, w2, w3), f, 0, w0.shape[0])
    place_columns(out_s, (o0, o1, o2, o3), f, 0, inner)
    place_columns(co_s, (o0, o1, o2, o3), f, inner, inner)
    place_rows(states_s, (s0, s1, s2, s3), f, 0, s0.shape[0])
    ckv_ref[...] = dot(states_s[...], w_s[:, inner:]).astype(BF16)
    for hb in range(length // HALF):
        at = slice(hb * HALF, (hb + 1) * HALF)
        hidden = x_s[at, :].astype(F32) + dot(mixed_ref[at, :], out_s[...])
        h1_ref[at, :] = hidden
        normed = (hidden * rms(hidden) * aux_ref[1:2, :]).astype(BF16)
        n2_ref[at, :] = normed
        cq_ref[at, :] = dot(normed, w_s[:, :inner]).astype(BF16)
    for p in range(PAIRS):
        k2 = ckv_ref[:, p * BLOCK : (p + 1) * BLOCK]
        v2 = ckv_ref[:, inner + p * BLOCK : inner + (p + 1) * BLOCK]
        v_only = [only_head(v2, hd) for hd in range(2)]
        for hb in range(length // HALF):
            at = slice(hb * HALF, (hb + 1) * HALF)
            q2 = cq_ref[at, p * BLOCK : (p + 1) * BLOCK]
            out = jnp.zeros((HALF, BLOCK), F32)
            for hd in range(2):
                probs = softmax(dot_t(only_head(q2, hd), k2)).astype(BF16)
                probs_ref[2 * p + hd, at, :] = probs
                out = out + dot(probs, v_only[hd])
            cmixed_ref[at, p * BLOCK : (p + 1) * BLOCK] = out.astype(BF16)
    for hb in range(length // HALF):
        at = slice(hb * HALF, (hb + 1) * HALF)
        hidden = h1_ref[at, :] + dot(cmixed_ref[at, :], co_s[...])
        h2_ref[at, :] = hidden
        n3_ref[at, :] = (hidden * rms(hidden) * aux_ref[2:3, :]).astype(BF16)


def feed_forward(
    f_ref, h2_ref, n3_ref, aux_ref, g0, g1, g2, g3, d0, d1, d2, d3,
    result_ref, grad_h2_ref, pack_ref, gain_ref,
    gu_s, down_s, cot_s, units_s, gate_s, up_s,
):
    f = f_ref[0]
    length, width = h2_ref.shape
    rows = length // GROUP
    hidden_units = down_s.shape[0]
    own_units = hidden_units // GROUP
    place_rows(gu_s, (g0, g1, g2, g3), f, 0, g0.shape[0])
    place_rows(down_s, (d0, d1, d2, d3), f, 0, own_units)
    place_rows(cot_s, (d0, d1, d2, d3), f, own_units, rows)
    gain = aux_ref[2:3, :]
    gain_sum = jnp.zeros((1, width), F32)
    for rb in range(length // BLOCK):
        at = slice(rb * BLOCK, (rb + 1) * BLOCK)
        pre = dot(n3_ref[at, :], gu_s[...])
        gate, up = pre[:, :hidden_units], pre[:, hidden_units:]
        grad_units = dot_t(cot_s[at, :], down_s[...])
        square = gate * gate
        tanh = jnp.tanh(0.7978845608028654 * (gate + 0.044715 * square * gate))
        half_gate = 0.5 * gate
        gelu = half_gate + half_gate * tanh
        slope = 0.5 + 0.5 * tanh + half_gate * (1.0 - tanh * tanh) * (
            0.7978845608028654 + (3 * 0.044715 * 0.7978845608028654) * square
        )
        units_s[at, :] = (gelu * up).astype(BF16)
        grad_gate = (grad_units * up * slope).astype(BF16)
        grad_up = (grad_units * gelu).astype(BF16)
        gate_s[at, :] = grad_gate
        up_s[at, :] = grad_up
        grad_normed = dot_t(grad_gate, gu_s[:, :hidden_units]) + dot_t(grad_up, gu_s[:, hidden_units:])
        piece, gain_part = norm_back(h2_ref[at, :], gain, grad_normed)
        grad_h2_ref[at, :] = cot_s[at, :].astype(F32) + piece
        gain_sum = gain_sum + jnp.sum(gain_part, axis=0, keepdims=True)
    gain_ref[...] = jnp.broadcast_to(gain_sum, gain_ref.shape)
    mine = own(f, rows)
    result_ref[...] = (h2_ref[mine, :] + dot(units_s[mine, :], down_s[...])).astype(BF16)
    own_rows = g0.shape[0]
    normed_own = n3_ref[:, own(f, own_rows)]
    pack_ref[:, :hidden_units] = t_dot(normed_own, gate_s[...]).astype(BF16)
    pack_ref[:, hidden_units : 2 * hidden_units] = t_dot(normed_own, up_s[...]).astype(BF16)
    grad_down = t_dot(units_s[:, own(f, own_units)], cot_s[...]).astype(BF16)
    for part in range(own_units // own_rows):
        first = 2 * hidden_units + part * width
        pack_ref[:, first : first + width] = grad_down[part * own_rows : (part + 1) * own_rows, :]


def cross_backward(
    f_ref, grad_h2_ref, h1_ref, n2_ref, cq_ref, ckv_ref, probs_ref, cmixed_ref, aux_ref,
    w0, w1, w2, w3, o0, o1, o2, o3, s0, s1, s2, s3,
    grad_h1_ref, grad_states_ref, pack_ref, gain_ref,
    w_s, co_s, states_s, low_s, mix_s, dq_s, dkv_s, ds_s,
):
    f = f_ref[0]
    length, width = h1_ref.shape
    inner = H * DH
    own_rows = w0.shape[0]
    place_rows(w_s, (w0, w1, w2, w3), f, 0, own_rows)
    place_columns(co_s, (o0, o1, o2, o3), f, inner, inner)
    place_rows(states_s, (s0, s1, s2, s3), f, 0, s0.shape[0])
    low = grad_h2_ref[...].astype(BF16)
    low_s[...] = low
    mix_s[...] = dot_t(low, co_s[...]).astype(BF16)
    grad_out = t_dot(cmixed_ref[...], low_s[:, own(f, o0.shape[1])]).astype(BF16)
    for part in range(inner // own_rows):
        first = inner * 3 + part * o0.shape[1]
        pack_ref[:, first : first + o0.shape[1]] = grad_out[part * own_rows : (part + 1) * own_rows, :]
    for p in range(PAIRS):
        lanes = slice(p * BLOCK, (p + 1) * BLOCK)
        k2 = ckv_ref[:, lanes]
        v2 = ckv_ref[:, inner + p * BLOCK : inner + (p + 1) * BLOCK]
        dq = jnp.zeros((length, BLOCK), F32)
        dk = jnp.zeros((k2.shape[0], BLOCK), F32)
        dv = jnp.zeros((k2.shape[0], BLOCK), F32)
        for hd in range(2):
            h = 2 * p + hd
            grad_mixed = only_head(mix_s[:, lanes], hd)
            for hb in range(length // HALF):
                at = slice(hb * HALF, (hb + 1) * HALF)
                probs = probs_ref[h, at, :].astype(F32)
                weighted = probs * dot_t(grad_mixed[at, :], v2)
                ds_s[at, :] = (weighted - probs * jnp.sum(weighted, axis=-1, keepdims=True)).astype(BF16)
            grad_scores = ds_s[...]
            dq = dq + dot(grad_scores, only_head(k2, hd))
            dk = dk + t_dot(grad_scores, only_head(cq_ref[:, lanes], hd))
            dv = dv + t_dot(probs_ref[h], grad_mixed)
        dq_s[:, lanes] = dq.astype(BF16)
        dkv_s[:, lanes] = dk.astype(BF16)
        dkv_s[:, inner + p * BLOCK : inner + (p + 1) * BLOCK] = dv.astype(BF16)
    gain = aux_ref[1:2, :]
    gain_sum = jnp.zeros((1, width), F32)
    for hb in range(length // HALF):
        at = slice(hb * HALF, (hb + 1) * HALF)
        grad_normed = dot_t(dq_s[at, :], w_s[:, :inner])
        piece, gain_part = norm_back(h1_ref[at, :], gain, grad_normed)
        grad_h1_ref[at, :] = grad_h2_ref[at, :] + piece
        gain_sum = gain_sum + jnp.sum(gain_part, axis=0, keepdims=True)
    gain_ref[...] = jnp.broadcast_to(gain_sum, gain_ref.shape)
    pack_ref[:, :inner] = t_dot(n2_ref[:, own(f, own_rows)], dq_s[...]).astype(BF16)
    pack_ref[:, inner : 3 * inner] = t_dot(states_s[:, own(f, own_rows)], dkv_s[...]).astype(BF16)
    grad_states_ref[...] = dot_t(dkv_s[own(f, s0.shape[0]), :], w_s[:, inner:])


def self_backward(
    f_ref, grad_h1_ref, normed_ref, qkv_ref, probs_ref, mixed_ref, aux_ref, gain2_ref, gain3_ref,
    t0, t1, t2, t3, w0, w1, w2, w3, o0, o1, o2, o3,
    grad_tokens_ref, pack_ref,
    x_s, w_s, out_s, low_s, mix_s, dqkv_s, ds_s, gain_s,
):
    f = f_ref[0]
    length, width = x_s.shape
    rows = length // GROUP
    inner = H * DH
    own_rows = w0.shape[0]
    place_rows(x_s, (t0, t1, t2, t3), f, 0, rows)
    place_rows(w_s, (w0, w1, w2, w3), f, 0, own_rows)
    place_columns(out_s, (o0, o1, o2, o3), f, 0, inner)
    low = grad_h1_ref[...].astype(BF16)
    low_s[...] = low
    mix_s[...] = dot_t(low, out_s[...]).astype(BF16)
    grad_out = t_dot(mixed_ref[...], low_s[:, own(f, o0.shape[1])]).astype(BF16)
    for part in range(inner // own_rows):
        first = inner * 3 + part * o0.shape[1]
        pack_ref[:, first : first + o0.shape[1]] = grad_out[part * own_rows : (part + 1) * own_rows, :]
    blocks = length // BLOCK
    row = lax.broadcasted_iota(jnp.int32, (BLOCK, 4 * BLOCK), 0)
    offset_sums, far_sums = [], []
    for p in range(PAIRS):
        lanes = slice(p * BLOCK, (p + 1) * BLOCK)
        k2 = qkv_ref[:, inner + p * BLOCK : inner + (p + 1) * BLOCK]
        v2 = qkv_ref[:, 2 * inner + p * BLOCK : 2 * inner + (p + 1) * BLOCK]
        q2 = qkv_ref[:, lanes]
        dq = [jnp.zeros((BLOCK, BLOCK), F32) for _ in range(blocks)]
        dk = [jnp.zeros((BLOCK, BLOCK), F32) for _ in range(blocks)]
        dv = [jnp.zeros((BLOCK, BLOCK), F32) for _ in range(blocks)]
        for hd in range(2):
            h = 2 * p + hd
            grad_mixed = only_head(mix_s[:, lanes], hd)
            k_only, q_only = only_head(k2, hd), only_head(q2, hd)
            near = jnp.zeros((BLOCK, BLOCK), F32)
            next_to = jnp.zeros((BLOCK, BLOCK), F32)
            far = jnp.zeros((BLOCK, BLOCK), F32)
            for rb in range(blocks):
                seen = (rb + 1) * BLOCK
                at = slice(rb * BLOCK, seen)
                probs = probs_ref[h, at, :seen].astype(F32)
                weighted = probs * dot_t(grad_mixed[at, :], v2[:seen, :])
                ds = weighted - probs * jnp.sum(weighted, axis=-1, keepdims=True)
                near = near + ds[:, rb * BLOCK :]
                if rb >= 1:
                    next_to = next_to + ds[:, (rb - 1) * BLOCK : rb * BLOCK]
                for c in range(rb - 1):
                    far = far + ds[:, c * BLOCK : (c + 1) * BLOCK]
                low_ds = ds.astype(BF16)
                ds_s[at, :seen] = low_ds
                dq[rb] = dq[rb] + dot(low_ds, k_only[:seen, :])
            for c in range(blocks):
                below, keys = slice(c * BLOCK, length), slice(c * BLOCK, (c + 1) * BLOCK)
                dk[c] = dk[c] + t_dot(ds_s[below, keys], q_only[below, :])
                dv[c] = dv[c] + t_dot(probs_ref[h, below, keys], grad_mixed[below, :])
            skew = jnp.concatenate([next_to, near, jnp.zeros((BLOCK, 2 * BLOCK), F32)], axis=1)
            for bit in range(BLOCK.bit_length() - 1):
                moved = pltpu.roll(skew, 4 * BLOCK - (1 << bit), 1)
                skew = jnp.where((row & (1 << bit)) != 0, moved, skew)
            offset_sums.append(jnp.sum(skew, axis=0, keepdims=True))
            far_sums.append(jnp.sum(jnp.sum(far, axis=0, keepdims=True), axis=1, keepdims=True))
        for c in range(blocks):
            at = slice(c * BLOCK, (c + 1) * BLOCK)
            dqkv_s[at, lanes] = dq[c].astype(BF16)
            dqkv_s[at, inner + p * BLOCK : inner + (p + 1) * BLOCK] = dk[c].astype(BF16)
            dqkv_s[at, 2 * inner + p * BLOCK : 2 * inner + (p + 1) * BLOCK] = dv[c].astype(BF16)
    per_offset = jnp.concatenate(offset_sums + [jnp.zeros((2, 4 * BLOCK), F32)], axis=0)
    per_bucket = jnp.dot(
        per_offset, offset_onehot(BLOCK, 0), precision=HIGHEST, preferred_element_type=F32
    )
    far_all = jnp.concatenate(far_sums + [jnp.zeros((2, 1), F32)], axis=0)
    lane = lax.broadcasted_iota(jnp.int32, (8, BLOCK), 1)
    per_bucket = per_bucket + jnp.where(lane == BUCKETS - 1, far_all, 0.0)

    gain = aux_ref[0:1, :]
    mine = own(f, rows)
    grad_normed = dot_t(dqkv_s[mine, :], w_s[...])
    piece, _ = norm_back(x_s[mine, :].astype(F32), gain, grad_normed)
    grad_tokens_ref[...] = grad_h1_ref[mine, :] + piece
    own_columns = own(f, own_rows)
    x = x_s[...].astype(F32)
    grad_own = dot_t(dqkv_s[...], w_s[own_columns, :])
    gain_own = jnp.sum(grad_own * x_s[:, own_columns].astype(F32) * rms(x), axis=0, keepdims=True)
    pack_ref[:, : 3 * inner] = t_dot(normed_ref[:, own_columns], dqkv_s[...]).astype(BF16)
    gain_s[0:8, :] = gain2_ref[...]
    gain_s[8:16, :] = gain3_ref[...]
    small = jnp.concatenate(
        [per_bucket, gain_own, gain_s[0:1, own_columns], gain_s[8:9, own_columns],
         jnp.zeros((BLOCK - 11, BLOCK), F32)], axis=0,
    )
    pack_ref[:, 4 * inner :] = small.astype(BF16)


VMEM = pl.BlockSpec(memory_space=pltpu.VMEM)


def call(kernel, name, out_shapes, scratch, args, flops):
    moved = sum(a.size * a.dtype.itemsize for a in args)
    return pl.pallas_call(
        kernel,
        name=name,
        out_shape=[jax.ShapeDtypeStruct(s, d) for s, d in out_shapes],
        in_specs=[pl.BlockSpec(memory_space=pltpu.SMEM)] + [VMEM] * (len(args) - 1),
        out_specs=[VMEM] * len(out_shapes),
        scratch_shapes=[pltpu.VMEM(s, d) for s, d in scratch],
        compiler_params=pltpu.CompilerParams(vmem_limit_bytes=56 * 1024 * 1024),
        cost_estimate=pl.CostEstimate(flops=flops, bytes_accessed=moved, transcendentals=0),
    )(*args)


def hop(x, axis, bits):
    size = lax.axis_size(axis)
    return lax.ppermute(x, axis, [(i, i ^ bits) for i in range(size)])


def gather_group(packs):
    across = [hop(pack, "fsdp", 2) for pack in packs]
    beside = [hop(pack, "fsdp", 1) for pack in packs]
    return [
        (pack, near, far, hop(far, "fsdp", 1)) for pack, near, far in zip(packs, beside, across)
    ]


def rep_stages():
    size = lax.axis_size("rep")
    stages, stride = [], 1
    while stride < size:
        ways = min(8, size // stride)
        stages.append((stride, ways))
        stride *= ways
    return stages


def sum_over_rep(pack):
    me = lax.axis_index("rep")
    part = pack
    stages = rep_stages()
    for stride, ways in stages:
        digit = (me // stride) % ways
        pieces = part.reshape((ways, part.shape[0] // ways) + part.shape[1:])
        total = lax.dynamic_index_in_dim(pieces, digit, 0, keepdims=False).astype(F32)
        arrived = [
            hop(lax.dynamic_index_in_dim(pieces, digit ^ k, 0, keepdims=False), "rep", k * stride)
            for k in range(1, ways)
        ]
        for piece in arrived:
            total = total + piece.astype(F32)
        part = total.astype(BF16)
    for stride, ways in reversed(stages):
        digit = (me // stride) % ways
        arrived = [part] + [hop(part, "rep", k * stride) for k in range(1, ways)]
        whole = jnp.zeros((ways,) + part.shape, BF16)
        for k, piece in enumerate(arrived):
            whole = lax.dynamic_update_index_in_dim(whole, piece, digit ^ k, 0)
        part = whole.reshape((ways * part.shape[0],) + part.shape[1:])
    return part.astype(F32)


def per_device(
    tokens,
    states,
    query_w,
    key_w,
    value_w,
    out_w,
    cross_query_w,
    cross_key_w,
    cross_value_w,
    cross_out_w,
    gate_w,
    up_w,
    down_w,
    self_gain,
    cross_gain,
    mlp_gain,
    bias_table,
    cotangent,
):
    seq_count, rows, width = tokens.shape
    enc = states.shape[1]
    own_rows, inner = query_w.shape
    hidden_units = gate_w.shape[1]
    length, enc_all = rows * GROUP, enc * GROUP
    f = lax.axis_index("fsdp")
    f_arg = f.astype(jnp.int32).reshape(1)

    gains = jnp.stack([self_gain, cross_gain, mlp_gain])
    aux = jnp.zeros((16, width), BF16)
    aux = lax.dynamic_update_slice(aux, gains, (0, f * own_rows))
    aux = lax.dynamic_update_slice(aux, bias_table.T, (8, f * bias_table.shape[0]))
    token_pack = jnp.concatenate([tokens[0], aux], axis=0)
    self_pack = jnp.concatenate([query_w, key_w, value_w], axis=1)
    out_pack = jnp.concatenate([out_w, cross_out_w], axis=0)
    cross_pack = jnp.concatenate([cross_query_w, cross_key_w, cross_value_w], axis=1)
    gate_pack = jnp.concatenate([gate_w, up_w], axis=1)
    down_pack = jnp.concatenate([down_w, cotangent[0]], axis=0)
    tok, self_ws, cross_ws, states_all, outs_ws, gates, downs = gather_group(
        [token_pack, self_pack, cross_pack, states[0], out_pack, gate_pack, down_pack]
    )

    normed_one, qkv, probs, mixed, aux_all = call(
        self_forward,
        "self_forward",
        [
            ((length, width), BF16),
            ((length, 3 * inner), BF16),
            ((H, length, length), BF16),
            ((length, inner), BF16),
            ((16, width), F32),
        ],
        [((length, width), BF16), ((width, 3 * inner), BF16), ((H, BLOCK, 2 * BLOCK), F32)],
        [f_arg, *tok, *self_ws],
        2 * 10**9,
    )
    hidden_one, normed_two, cross_q, cross_kv, cross_probs, cross_mixed, hidden_two, normed_three = call(
        cross_forward,
        "cross_forward",
        [
            ((length, width), F32),
            ((length, width), BF16),
            ((length, inner), BF16),
            ((enc_all, 2 * inner), BF16),
            ((H, length, enc_all), BF16),
            ((length, inner), BF16),
            ((length, width), F32),
            ((length, width), BF16),
        ],
        [
            ((length, width), BF16),
            ((width, 3 * inner), BF16),
            ((inner, width), BF16),
            ((inner, width), BF16),
            ((enc_all, width), BF16),
        ],
        [f_arg, *tok, mixed, aux_all, *cross_ws, *outs_ws, *states_all],
        2 * 10**9,
    )
    result, grad_hidden_two, ff_pack, mlp_gain_all = call(
        feed_forward,
        "feed_forward",
        [
            ((rows, width), BF16),
            ((length, width), F32),
            ((own_rows, 2 * hidden_units + down_w.size // own_rows), BF16),
            ((8, width), F32),
        ],
        [
            ((width, 2 * hidden_units), BF16),
            ((hidden_units, width), BF16),
            ((length, width), BF16),
            ((length, hidden_units), BF16),
            ((length, hidden_units), BF16),
            ((length, hidden_units), BF16),
        ],
        [f_arg, hidden_two, normed_three, aux_all, *gates, *downs],
        4 * 10**9,
    )
    grad_hidden_one, grad_states, cross_grads, cross_gain_all = call(
        cross_backward,
        "cross_backward",
        [
            ((length, width), F32),
            ((enc, width), F32),
            ((own_rows, 4 * inner), BF16),
            ((8, width), F32),
        ],
        [
            ((width, 3 * inner), BF16),
            ((inner, width), BF16),
            ((enc_all, width), BF16),
            ((length, width), BF16),
            ((length, inner), BF16),
            ((length, inner), BF16),
            ((enc_all, 2 * inner), BF16),
            ((length, enc_all), BF16),
        ],
        [
            f_arg, grad_hidden_two, hidden_one, normed_two, cross_q, cross_kv, cross_probs, cross_mixed,
            aux_all, *cross_ws, *outs_ws, *states_all,
        ],
        2 * 10**9,
    )
    grad_tokens, self_grads = call(
        self_backward,
        "self_backward",
        [((rows, width), F32), ((own_rows, 4 * inner + BLOCK), BF16)],
        [
            ((length, width), BF16),
            ((width, 3 * inner), BF16),
            ((inner, width), BF16),
            ((length, width), BF16),
            ((length, inner), BF16),
            ((length, 3 * inner), BF16),
            ((length, length), BF16),
            ((16, width), F32),
        ],
        [
            f_arg, grad_hidden_one, normed_one, qkv, probs, mixed, aux_all, cross_gain_all, mlp_gain_all,
            *tok, *self_ws, *outs_ws,
        ],
        3 * 10**9,
    )

    ff_sum = sum_over_rep(ff_pack)
    cross_sum = sum_over_rep(cross_grads)
    self_sum = sum_over_rep(self_grads)

    def down_grad():
        return jnp.concatenate(
            [ff_sum[:, 2 * hidden_units + i * width :][:, :width] for i in range(down_w.shape[0] // own_rows)]
        )

    def out_grad(total):
        return jnp.concatenate(
            [total[:, 3 * inner + i * own_rows :][:, :own_rows] for i in range(inner // own_rows)]
        )

    small = self_sum[:, 4 * inner :]
    table = lax.dynamic_slice(small[:H, :], (0, f * bias_table.shape[0]), (H, bias_table.shape[0]))
    return (
        result[None],
        grad_tokens[None],
        grad_states[None],
        self_sum[:, :inner],
        self_sum[:, inner : 2 * inner],
        self_sum[:, 2 * inner : 3 * inner],
        out_grad(self_sum),
        cross_sum[:, :inner],
        cross_sum[:, inner : 2 * inner],
        cross_sum[:, 2 * inner : 3 * inner],
        out_grad(cross_sum),
        ff_sum[:, :hidden_units],
        ff_sum[:, hidden_units : 2 * hidden_units],
        down_grad(),
        small[8],
        small[9],
        small[10],
        table.T,
    )


def solution(mesh):
    whole = P("rep", "fsdp", None)
    rows, columns, vector = P("fsdp", None), P(None, "fsdp"), P("fsdp")
    weights = (rows, rows, rows, columns, rows, rows, rows, columns, rows, rows, rows)
    small = (vector, vector, vector, rows)
    return jax.shard_map(
        per_device,
        mesh=mesh,
        in_specs=(whole, whole) + weights + small + (whole,),
        out_specs=(whole, whole, whole) + weights + small,
        check_vma=False,
    )
```

time: 671 us -> 211 us (0.31)
  blocking collectives: 361 us -> 0 us
  waiting for transfers between devices: 205 us -> 68.1 us
  starting transfers between devices: 0.87 us -> 76.7 us
  matrix products: 48.2 us -> 0 us
  Pallas kernels: 0 us -> 45.1 us
  local copies, waits for them, and re-layouts: 30 us -> 14 us
  between operations: 17.2 us -> 1.37 us
    reduce_scatter x9 -> x0, waiting for transfers between devices: 188 us -> none  [the longest x1 27.7 us: per_device(): lax.psum_scatter(grad_up_w.astype(jnp.bfloat16), 'fsdp', scatter_dimensio...]
    psum x1 -> x0, blocking collectives: 130 us -> none  [per_device(): lax.psum((own_query, own_key, own_value, own_out, own_cross_query, own_cr...]
    unnamed x2 -> x0, blocking collectives: 128 us -> none
    all_gather x16 -> x0, blocking collectives: 103 us -> none  [the longest x1 8.59 us: per_device(): lax.all_gather(key_w, 'fsdp', axis=0, tiled=True)]
    ppermute x0 -> x63, starting transfers between devices: none -> 76.7 us  [hop(): return lax.ppermute(x, axis, [(i, i ^ bits) for i in range(size)])]
    ppermute x0 -> x63, waiting for transfers between devices: none -> 68.1 us  [hop(): return lax.ppermute(x, axis, [(i, i ^ bits) for i in range(size)])]
    dot_general x47 -> x0, matrix products: 48.2 us -> none  [the longest x11 14.2 us: outer_sum(): lax.dot_general(left_rows, right_rows, (((0,), (0,)), ((), ())), preferre...]
    pallas_call x0 -> x5, Pallas kernels: none -> 45.1 us  [call(): pl.pallas_call(kernel, name=name, out_shape=[jax.ShapeDtypeStruct(s, d) f...]
  transfers between devices with their start and end apart: 16 -> 63, of which waited for: 9 -> 19; matrix products, arithmetic and copies ran while one was open for 10% -> 5% of each run, Pallas kernels for 0% -> 13%
where the time goes in v1:
time: 211 us
  starting transfers between devices  76.7 us (36%)
  waiting for transfers between devices  68.1 us (32%)
  Pallas kernels  45.1 us (21%)
  local copies, waits for them, and re-layouts  14 us (7%)
  other arithmetic  5.49 us (3%)
    ppermute x63, starting transfers between devices, hop(): return lax.ppermute(x, axis, [(i, i ^ bits) for i in range(size)])  76.7 us
    ppermute x63, waiting for transfers between devices, hop(): return lax.ppermute(x, axis, [(i, i ^ bits) for i in range(size)])  68.1 us
    pallas_call x5, Pallas kernels, call(): pl.pallas_call(kernel, name=name, out_shape=[jax.ShapeDtypeStruct(s, d) f...  45.1 us
    unnamed x66, local copies, waits for them, and re-layouts  7.28 us
  transfers between devices with their start and end apart: 63, of which 19 were waited for; matrix products, arithmetic and copies ran while one was open for 5% of the time, Pallas kernels for 13%

profile of v1, /device:TPU:0, one launch (start us, length us, event | category | flops | bytes accessed | tf_op | source)
XLA Modules:
  0.0 210.8 jit_solution(2551881535805209207)
XLA Ops:
  3.9 3.2 %collective-permute-start.1 = (bf16[144,512]{1,0:T(8,128)(2,1)S(1)}, bf16[144,512]{1,0:T(8,128)(2,1)S(1)}, u32[]{:S(2)}, u32[]{:S(2)}) collective-permute-start(bf16[144,512]{1,0:T(8,128)(2,1)S(1)} %pad_maximum_fusion.4.t0), channel_id=1, source_target_pairs={{0,2},{1,3},{2,0},{3,1},{4,6},{5,7},{6,4},{7,5},{8,10},{9,11},{10,... | collective-permute-start | bytes 442376 | tf_op jit(solution)/shard_map/ppermute | solution.py:414
  20.0 5.6 %collective-permute-done.4.w2 = bf16[128,1152]{1,0:T(8,128)(2,1)S(1)} collective-permute-done((bf16[128,1152]{1,0:T(8,128)(2,1)S(1)}, bf16[128,1152]{1,0:T(8,128)(2,1)S(1)}, u32[]{:S(2)}, u32[]{:S(2)}) %collective-permute-start.4) | collective-permute-done | bytes 294944 | tf_op jit(solution)/shard_map/ppermute | solution.py:414
  25.9 17.3 %collective-permute-done.7.w2 = bf16[128,1152]{1,0:T(8,128)(2,1)S(1)} collective-permute-done((bf16[128,1152]{1,0:T(8,128)(2,1)S(1)}, bf16[128,1152]{1,0:T(8,128)(2,1)S(1)}, u32[]{:S(2)}, u32[]{:S(2)}) %collective-permute-start.7) | collective-permute-done | bytes 294944 | tf_op jit(solution)/shard_map/ppermute | solution.py:414
  44.8 6.3 %collective-permute-done.19.d2 = bf16[384,512]{1,0:T(8,128)(2,1)} collective-permute-done((bf16[384,512]{1,0:T(8,128)(2,1)S(1)}, bf16[384,512]{1,0:T(8,128)(2,1)}, u32[]{:S(2)}, u32[]{:S(2)}) %collective-permute-start.19) | collective-permute-done | bytes 393248 | tf_op jit(solution)/shard_map/ppermute | solution.py:414
  52.3 7.6 %self_forward.1 = (bf16[512,512]{1,0:T(8,128)(2,1)}, bf16[512,1152]{1,0:T(8,128)(2,1)}, bf16[6,512,512]{2,1,0:T(8,128)(2,1)}, bf16[512,384]{1,0:T(8,128)(2,1)}, f32[16,512]{1,0:T(8,128)}) custom-call(s32[1]{0:T(128)} %bitcast.f_ref, bf16[144,512]{1,0:T(8,128)(2,1)} %copy-done.12, bf16[144,512]{1,0:T(8,128)(2,1)} %copy-done.27, bf16[144,512]{1,0:T(8,128)(2,1)} %copy-done.26, ...), custom_call_target="tpu_custom_call" | custom-call | flops 2000000000 | bytes 1769476 | tf_op jit(solution)/shard_map/self_forward/pallas_call | solution.py:400
  60.7 7.4 %cross_forward.1 = (f32[512,512]{1,0:T(8,128)}, bf16[512,512]{1,0:T(8,128)(2,1)}, bf16[512,384]{1,0:T(8,128)(2,1)}, bf16[256,768]{1,0:T(8,128)(2,1)}, bf16[6,512...) custom-call(s32[1]{0:T(128)} %bitcast.f_ref, ...), custom_call_target="tpu_custom_call" | custom-call | flops 2000000000 | bytes 3244036 | tf_op jit(solution)/shard_map/cross_forward/pallas_call | solution.py:400
  68.2 10.2 %feed_forward.1 = (bf16[128,512]{1,0:T(8,128)(2,1)}, f32[512,512]{1,0:T(8,128)}, bf16[128,3072]{1,0:T(8,128)(2,1)}, f32[8,512]{1,0:T(8,128)}) custom-call(s32[1]{0:T(128)} %bitcast.f_ref, f32[512,512]{1,0:T(8,128)} %get-tuple-element.43.h2_ref, bf16[512,512]{1,0:T(8,128)(2,1)} %get-tuple-element.44.n3_ref, f32[16,512]{1,0:T(8,128)} %get-tuple-element.42.aux_ref, ...), custom_call_target="tpu_custom_call" | custom-call | flops 4000000000 | bytes 5275652 | tf_op jit(solution)/shard_map/feed_forward/pallas_call | solution.py:400
  78.4 8.0 %cross_backward.1 = (f32[512,512]{1,0:T(8,128)}, f32[64,512]{1,0:T(8,128)}, bf16[128,1536]{1,0:T(8,128)(2,1)}, f32[8,512]{1,0:T(8,128)}) custom-call(s32[1]{0:T(128)} %bitcast.f_ref, f32[512,512]{1,0:T(8,128)} %get-tuple-element.46.grad_h2_ref, f32[512,512]{1,0:T(8,128)} %get-tuple-element.47.h1_ref, bf16[512,512]{1,0:T(8,128)(2,1)} %get-tuple-element.48.n2_ref, ...), custom_call_target="tpu_custom_call" | custom-call | flops 2000000000 | bytes 7634948 | tf_op jit(solution)/shard_map/cross_backward/pallas_call | solution.py:400
  90.9 2.6 %collective-permute-start.38 = (bf16[16,1536]{1,0:T(8,128)(2,1)S(1)}, bf16[16,1536]{1,0:T(8,128)(2,1)S(1)}, u32[]{:S(2)}, u32[]{:S(2)}) collective-permute-start(bf16[16,1536]{1,0:T(8,128)(2,1)S(1)} %get-tuple-element.143), channel_id=1, source_target_pairs={{0,16},{4,20},{8,24},{12,28},{16,0},{20,4},{24,8},{28,12},{1,17},{... | collective-permute-start | bytes 147464 | tf_op jit(solution)/shard_map/ppermute | solution.py:414
  94.8 11.9 %self_backward.1 = (f32[128,512]{1,0:T(8,128)}, bf16[128,1664]{1,0:T(8,128)(2,1)}) custom-call(s32[1]{0:T(128)} %bitcast.f_ref, f32[512,512]{1,0:T(8,128)} %get-tuple-element.53.grad_h1_ref, bf16[512,512]{1,0:T(8,128)(2,1)} %get-tuple-element.54.normed_ref, bf16[512,1152]{1,0:T(8,128)(2,1)} %get-tuple-element.55.qkv_ref, ...), custom_call_target="tpu_custom_call" | custom-call | flops 3000000000 | bytes 8912900 | tf_op jit(solution)/shard_map/self_backward/pallas_call | solution.py:400
  107.7 3.7 %collective-permute-start.40 = (bf16[16,1536]{1,0:T(8,128)(2,1)S(1)}, bf16[16,1536]{1,0:T(8,128)(2,1)S(1)}, u32[]{:S(2)}, u32[]{:S(2)}) collective-permute-start(bf16[16,1536]{1,0:T(8,128)(2,1)S(1)} %get-tuple-element.141), channel_id=1, source_target_pairs={{0,24},{4,28},{8,16},{12,20},{16,8},{20,12},{24,0},{28,4},{1,25},{... | collective-permute-start | bytes 147464 | tf_op jit(solution)/shard_map/ppermute | solution.py:414
  115.2 2.3 %collective-permute-start.24 = (bf16[16,1664]{1,0:T(8,128)(2,1)S(1)}, bf16[16,1664]{1,0:T(8,128)(2,1)S(1)}, u32[]{:S(2)}, u32[]{:S(2)}) collective-permute-start(bf16[16,1664]{1,0:T(8,128)(2,1)S(1)} %get-tuple-element.136), channel_id=1, source_target_pairs={{0,16},{4,20},{8,24},{12,28},{16,0},{20,4},{24,8},{28,12},{1,17},{... | collective-permute-start | bytes 159752 | tf_op jit(solution)/shard_map/ppermute | solution.py:414
  119.1 3.6 %collective-permute-start.26 = (bf16[16,1664]{1,0:T(8,128)(2,1)S(1)}, bf16[16,1664]{1,0:T(8,128)(2,1)S(1)}, u32[]{:S(2)}, u32[]{:S(2)}) collective-permute-start(bf16[16,1664]{1,0:T(8,128)(2,1)S(1)} %get-tuple-element.134), channel_id=1, source_target_pairs={{0,24},{4,28},{8,16},{12,20},{16,8},{20,12},{24,0},{28,4},{1,25},{... | collective-permute-start | bytes 159752 | tf_op jit(solution)/shard_map/ppermute | solution.py:414
  127.3 2.3 %collective-permute-start.52 = (bf16[16,3072]{1,0:T(8,128)(2,1)S(1)}, bf16[16,3072]{1,0:T(8,128)(2,1)S(1)}, u32[]{:S(2)}, u32[]{:S(2)}) collective-permute-start(bf16[16,3072]{1,0:T(8,128)(2,1)S(1)} %get-tuple-element.123), channel_id=1, source_target_pairs={{0,16},{4,20},{8,24},{12,28},{16,0},{20,4},{24,8},{28,12},{1,17},{... | collective-permute-start | bytes 294920 | tf_op jit(solution)/shard_map/ppermute | solution.py:414
  132.0 2.2 %collective-permute-done.42 = bf16[16,1536]{1,0:T(8,128)(2,1)S(1)} collective-permute-done((bf16[16,1536]{1,0:T(8,128)(2,1)S(1)}, bf16[16,1536]{1,0:T(8,128)(2,1)S(1)}, u32[]{:S(2)}, u32[]{:S(2)}) %collective-permute-start.42) | collective-permute-done | bytes 49184 | tf_op jit(solution)/shard_map/ppermute | solution.py:414
  135.6 2.7 %collective-permute-done.43 = bf16[16,1536]{1,0:T(8,128)(2,1)S(1)} collective-permute-done((bf16[16,1536]{1,0:T(8,128)(2,1)S(1)}, bf16[16,1536]{1,0:T(8,128)(2,1)S(1)}, u32[]{:S(2)}, u32[]{:S(2)}) %collective-permute-start.43) | collective-permute-done | bytes 49184 | tf_op jit(solution)/shard_map/ppermute | solution.py:414
  138.2 2.4 %collective-permute-start.44 = (bf16[16,1536]{1,0:T(8,128)(2,1)S(1)}, bf16[16,1536]{1,0:T(8,128)(2,1)S(1)}, u32[]{:S(2)}, u32[]{:S(2)}) collective-permute-start(bf16[16,1536]{1,0:T(8,128)(2,1)S(1)} %get-tuple-element.103), channel_id=1, source_target_pairs={{0,12},{4,8},{8,4},{12,0},{16,28},{20,24},{24,20},{28,16},{1,13},{... | collective-permute-start | bytes 147464 | tf_op jit(solution)/shard_map/ppermute | solution.py:414
  140.6 2.6 %collective-permute-done.44 = bf16[16,1536]{1,0:T(8,128)(2,1)S(1)} collective-permute-done((bf16[16,1536]{1,0:T(8,128)(2,1)S(1)}, bf16[16,1536]{1,0:T(8,128)(2,1)S(1)}, u32[]{:S(2)}, u32[]{:S(2)}) %collective-permute-start.44) | collective-permute-done | bytes 49184 | tf_op jit(solution)/shard_map/ppermute | solution.py:414
  144.5 3.8 %collective-permute-done.45 = bf16[16,1536]{1,0:T(8,128)(2,1)S(1)} collective-permute-done((bf16[16,1536]{1,0:T(8,128)(2,1)S(1)}, bf16[16,1536]{1,0:T(8,128)(2,1)S(1)}, u32[]{:S(2)}, u32[]{:S(2)}) %collective-permute-start.45) | collective-permute-done | bytes 49184 | tf_op jit(solution)/shard_map/ppermute | solution.py:414
  149.6 4.5 %collective-permute-done.46 = bf16[16,1536]{1,0:T(8,128)(2,1)S(1)} collective-permute-done((bf16[16,1536]{1,0:T(8,128)(2,1)S(1)}, bf16[16,1536]{1,0:T(8,128)(2,1)S(1)}, u32[]{:S(2)}, u32[]{:S(2)}) %collective-permute-start.46) | collective-permute-done | bytes 49184 | tf_op jit(solution)/shard_map/ppermute | solution.py:414
  155.2 5.4 %collective-permute-done.47 = bf16[16,1536]{1,0:T(8,128)(2,1)S(1)} collective-permute-done((bf16[16,1536]{1,0:T(8,128)(2,1)S(1)}, bf16[16,1536]{1,0:T(8,128)(2,1)S(1)}, u32[]{:S(2)}, u32[]{:S(2)}) %collective-permute-start.47) | collective-permute-done | bytes 49184 | tf_op jit(solution)/shard_map/ppermute | solution.py:414
  160.6 3.0 %collective-permute-start.48 = (bf16[16,1536]{1,0:T(8,128)(2,1)S(1)}, bf16[16,1536]{1,0:T(8,128)(2,1)S(1)}, u32[]{:S(2)}, u32[]{:S(2)}) collective-permute-start(bf16[16,1536]{1,0:T(8,128)(2,1)S(1)} %get-tuple-element.103), channel_id=1, source_target_pairs={{0,28},{4,24},{8,20},{12,16},{16,12},{20,8},{24,4},{28,0},{1,29},{... | collective-permute-start | bytes 147464 | tf_op jit(solution)/shard_map/ppermute | solution.py:414
  163.5 3.9 %collective-permute-done.48 = bf16[16,1536]{1,0:T(8,128)(2,1)S(1)} collective-permute-done((bf16[16,1536]{1,0:T(8,128)(2,1)S(1)}, bf16[16,1536]{1,0:T(8,128)(2,1)S(1)}, u32[]{:S(2)}, u32[]{:S(2)}) %collective-permute-start.48) | collective-permute-done | bytes 49184 | tf_op jit(solution)/shard_map/ppermute | solution.py:414
  167.5 2.7 %collective-permute-start.54 = (bf16[16,3072]{1,0:T(8,128)(2,1)S(1)}, bf16[16,3072]{1,0:T(8,128)(2,1)S(1)}, u32[]{:S(2)}, u32[]{:S(2)}) collective-permute-start(bf16[16,3072]{1,0:T(8,128)(2,1)S(1)} %get-tuple-element.121), channel_id=1, source_target_pairs={{0,24},{4,28},{8,16},{12,20},{16,8},{20,12},{24,0},{28,4},{1,25},{... | collective-permute-start | bytes 294920 | tf_op jit(solution)/shard_map/ppermute | solution.py:414
  170.2 2.2 %collective-permute-start.55 = (bf16[16,3072]{1,0:T(8,128)(2,1)S(1)}, bf16[16,3072]{1,0:T(8,128)(2,1)S(1)}, u32[]{:S(2)}, u32[]{:S(2)}) collective-permute-start(bf16[16,3072]{1,0:T(8,128)(2,1)S(1)} %get-tuple-element.120), channel_id=1, source_target_pairs={{0,28},{4,24},{8,20},{12,16},{16,12},{20,8},{24,4},{28,0},{1,29},{... | collective-permute-start | bytes 294920 | tf_op jit(solution)/shard_map/ppermute | solution.py:414
  174.7 3.8 %collective-permute-done.53 = bf16[16,3072]{1,0:T(8,128)(2,1)S(1)} collective-permute-done((bf16[16,3072]{1,0:T(8,128)(2,1)S(1)}, bf16[16,3072]{1,0:T(8,128)(2,1)S(1)}, u32[]{:S(2)}, u32[]{:S(2)}) %collective-permute-start.53) | collective-permute-done | bytes 98336 | tf_op jit(solution)/shard_map/ppermute | solution.py:414
  178.5 3.0 %collective-permute-start.31 = (bf16[16,1664]{1,0:T(8,128)(2,1)S(1)}, bf16[16,1664]{1,0:T(8,128)(2,1)S(1)}, u32[]{:S(2)}, u32[]{:S(2)}) collective-permute-start(bf16[16,1664]{1,0:T(8,128)(2,1)S(1)} %get-tuple-element.105), channel_id=1, source_target_pairs={{0,16},{4,20},{8,24},{12,28},{16,0},{20,4},{24,8},{28,12},{1,17},{... | collective-permute-start | bytes 159752 | tf_op jit(solution)/shard_map/ppermute | solution.py:414
  181.5 3.2 %collective-permute-start.32 = (bf16[16,1664]{1,0:T(8,128)(2,1)S(1)}, bf16[16,1664]{1,0:T(8,128)(2,1)S(1)}, u32[]{:S(2)}, u32[]{:S(2)}) collective-permute-start(bf16[16,1664]{1,0:T(8,128)(2,1)S(1)} %get-tuple-element.105), channel_id=1, source_target_pairs={{0,20},{4,16},{8,28},{12,24},{16,4},{20,0},{24,12},{28,8},{1,21},{... | collective-permute-start | bytes 159752 | tf_op jit(solution)/shard_map/ppermute | solution.py:414
  193.9 2.6 %collective-permute-start.60 = (bf16[16,3072]{1,0:T(8,128)(2,1)S(1)}, bf16[16,3072]{1,0:T(8,128)(2,1)S(1)}, u32[]{:S(2)}, u32[]{:S(2)}) collective-permute-start(bf16[16,3072]{1,0:T(8,128)(2,1)S(1)} %get-tuple-element.101), channel_id=1, source_target_pairs={{0,20},{4,16},{8,28},{12,24},{16,4},{20,0},{24,12},{28,8},{1,21},{... | collective-permute-start | bytes 294920 | tf_op jit(solution)/shard_map/ppermute | solution.py:414
  201.2 2.1 %collective-permute-start.62 = (bf16[16,3072]{1,0:T(8,128)(2,1)S(1)}, bf16[16,3072]{1,0:T(8,128)(2,1)S(1)}, u32[]{:S(2)}, u32[]{:S(2)}) collective-permute-start(bf16[16,3072]{1,0:T(8,128)(2,1)S(1)} %get-tuple-element.101), channel_id=1, source_target_pairs={{0,28},{4,24},{8,20},{12,16},{16,12},{20,8},{24,4},{28,0},{1,29},{... | collective-permute-start | bytes 294920 | tf_op jit(solution)/shard_map/ppermute | solution.py:414
  203.5 2.8 %collective-permute-done.61 = bf16[16,3072]{1,0:T(8,128)(2,1)S(1)} collective-permute-done((bf16[16,3072]{1,0:T(8,128)(2,1)S(1)}, bf16[16,3072]{1,0:T(8,128)(2,1)S(1)}, u32[]{:S(2)}, u32[]{:S(2)}) %collective-permute-start.61) | collective-permute-done | bytes 98336 | tf_op jit(solution)/shard_map/ppermute | solution.py:414
  206.3 2.4 %collective-permute-done.62 = bf16[16,3072]{1,0:T(8,128)(2,1)S(1)} collective-permute-done((bf16[16,3072]{1,0:T(8,128)(2,1)S(1)}, bf16[16,3072]{1,0:T(8,128)(2,1)S(1)}, u32[]{:S(2)}, u32[]{:S(2)}) %collective-permute-start.62) | collective-permute-done | bytes 98336 | tf_op jit(solution)/shard_map/ppermute | solution.py:414
  (218 shorter events, 62.5 us)
Async XLA Ops:
  3.9 12.2 %collective-permute-start.1 = (bf16[144,512]{1,0:T(8,128)(2,1)S(1)}, bf16[144,512]{1,0:T(8,128)(2,1)S(1)}, u32[]{:S(2)}, u32[]{:S(2)}) collective-permute-start(bf16[144,512]{1,0:T(8,128)(2,1)S(1)} %pad_maximum_fusion.4.t0), channel_id=1, source_target_pairs={{0,2},{1,3},{2,0},{3,1},{4,6},{5,7},{6,4},{7,5},{8,10},{9,11},{10,... | collective-permute-start | bytes 442376 | tf_op jit(solution)/shard_map/ppermute | solution.py:414
  16.1 27.6 %collective-permute-start.16 = (bf16[128,2048]{1,0:T(8,128)(2,1)S(1)}, bf16[128,2048]{1,0:T(8,128)(2,1)}, u32[]{:S(2)}, u32[]{:S(2)}) collective-permute-start(bf16[128,2048]{1,0:T(8,128)(2,1)S(1)} %constant_dynamic-update-slice_fusion.8.g0), channel_id=1, source_target_pairs={{0,2},{1,3},{2,0},{3,1},{4,6},{5,7},{6,4},{7,5},{8,10},{9,11},{10,... | collective-permute-start | bytes 1572872 | tf_op jit(solution)/shard_map/ppermute | solution.py:414
  18.1 25.1 %collective-permute-start.7 = (bf16[128,1152]{1,0:T(8,128)(2,1)S(1)}, bf16[128,1152]{1,0:T(8,128)(2,1)S(1)}, u32[]{:S(2)}, u32[]{:S(2)}) collective-permute-start(bf16[128,1152]{1,0:T(8,128)(2,1)S(1)} %constant_dynamic-update-slice_fusion.3.w0), channel_id=1, source_target_pairs={{0,2},{1,3},{2,0},{3,1},{4,6},{5,7},{6,4},{7,5},{8,10},{9,11},{10,... | collective-permute-start | bytes 884744 | tf_op jit(solution)/shard_map/ppermute | solution.py:414
  19.3 23.9 %collective-permute-start.6 = (bf16[128,1152]{1,0:T(8,128)(2,1)S(1)}, bf16[128,1152]{1,0:T(8,128)(2,1)S(1)}, u32[]{:S(2)}, u32[]{:S(2)}) collective-permute-start(bf16[128,1152]{1,0:T(8,128)(2,1)S(1)} %constant_dynamic-update-slice_fusion.3.w0), channel_id=1, source_target_pairs={{0,1},{1,0},{2,3},{3,2},{4,5},{5,4},{6,7},{7,6},{8,9},{9,8},{10,11... | collective-permute-start | bytes 884744 | tf_op jit(solution)/shard_map/ppermute | solution.py:414
  25.6 25.4 %collective-permute-start.19 = (bf16[384,512]{1,0:T(8,128)(2,1)S(1)}, bf16[384,512]{1,0:T(8,128)(2,1)}, u32[]{:S(2)}, u32[]{:S(2)}) collective-permute-start(bf16[384,512]{1,0:T(8,128)(2,1)S(1)} %pad_maximum_fusion.1.d0), channel_id=1, source_target_pairs={{0,2},{1,3},{2,0},{3,1},{4,6},{5,7},{6,4},{7,5},{8,10},{9,11},{10,... | collective-permute-start | bytes 1179656 | tf_op jit(solution)/shard_map/ppermute | solution.py:414
  25.9 25.1 %collective-permute-start.5 = (bf16[128,1152]{1,0:T(8,128)(2,1)S(1)}, bf16[128,1152]{1,0:T(8,128)(2,1)S(1)}, u32[]{:S(2)}, u32[]{:S(2)}) collective-permute-start(bf16[128,1152]{1,0:T(8,128)(2,1)S(1)} %collective-permute-done.4.w2), channel_id=1, source_target_pairs={{0,1},{1,0},{2,3},{3,2},{4,5},{5,4},{6,7},{7,6},{8,9},{9,8},{10,11... | collective-permute-start | bytes 884744 | tf_op jit(solution)/shard_map/ppermute | solution.py:414
  43.2 24.9 %collective-permute-start.15 = (bf16[128,2048]{1,0:T(8,128)(2,1)S(1)}, bf16[128,2048]{1,0:T(8,128)(2,1)}, u32[]{:S(2)}, u32[]{:S(2)}) collective-permute-start(bf16[128,2048]{1,0:T(8,128)(2,1)S(1)} %constant_dynamic-update-slice_fusion.8.g0), channel_id=1, source_target_pairs={{0,1},{1,0},{2,3},{3,2},{4,5},{5,4},{6,7},{7,6},{8,9},{9,8},{10,11... | collective-permute-start | bytes 1572872 | tf_op jit(solution)/shard_map/ppermute | solution.py:414
  43.7 24.4 %collective-permute-start.17 = (bf16[128,2048]{1,0:T(8,128)(2,1)}, bf16[128,2048]{1,0:T(8,128)(2,1)}, u32[]{:S(2)}, u32[]{:S(2)}) collective-permute-start(bf16[128,2048]{1,0:T(8,128)(2,1)} %collective-permute-done.16.g2), channel_id=1, source_target_pairs={{0,1},{1,0},{2,3},{3,2},{4,5},{5,4},{6,7},{7,6},{8,9},{9,8},{10,11... | collective-permute-start | bytes 1572872 | tf_op jit(solution)/shard_map/ppermute | solution.py:414
  44.6 15.3 %collective-permute-start.8 = (bf16[128,1152]{1,0:T(8,128)(2,1)S(1)}, bf16[128,1152]{1,0:T(8,128)(2,1)S(1)}, u32[]{:S(2)}, u32[]{:S(2)}) collective-permute-start(bf16[128,1152]{1,0:T(8,128)(2,1)S(1)} %collective-permute-done.7.w2), channel_id=1, source_target_pairs={{0,1},{1,0},{2,3},{3,2},{4,5},{5,4},{6,7},{7,6},{8,9},{9,8},{10,11... | collective-permute-start | bytes 884744 | tf_op jit(solution)/shard_map/ppermute | solution.py:414
  51.0 17.1 %collective-permute-start.18 = (bf16[384,512]{1,0:T(8,128)(2,1)S(1)}, bf16[384,512]{1,0:T(8,128)(2,1)}, u32[]{:S(2)}, u32[]{:S(2)}) collective-permute-start(bf16[384,512]{1,0:T(8,128)(2,1)S(1)} %pad_maximum_fusion.1.d0), channel_id=1, source_target_pairs={{0,1},{1,0},{2,3},{3,2},{4,5},{5,4},{6,7},{7,6},{8,9},{9,8},{10,11... | collective-permute-start | bytes 1179656 | tf_op jit(solution)/shard_map/ppermute | solution.py:414
  51.8 16.4 %collective-permute-start.20 = (bf16[384,512]{1,0:T(8,128)(2,1)}, bf16[384,512]{1,0:T(8,128)(2,1)}, u32[]{:S(2)}, u32[]{:S(2)}) collective-permute-start(bf16[384,512]{1,0:T(8,128)(2,1)} %collective-permute-done.19.d2), channel_id=1, source_target_pairs={{0,1},{1,0},{2,3},{3,2},{4,5},{5,4},{6,7},{7,6},{8,9},{9,8},{10,11... | collective-permute-start | bytes 1179656 | tf_op jit(solution)/shard_map/ppermute | solution.py:414
  87.4 20.4 %collective-permute-start.35 = (bf16[16,1536]{1,0:T(8,128)(2,1)S(1)}, bf16[16,1536]{1,0:T(8,128)(2,1)S(1)}, u32[]{:S(2)}, u32[]{:S(2)}) collective-permute-start(bf16[16,1536]{1,0:T(8,128)(2,1)S(1)} %get-tuple-element.139), channel_id=1, source_target_pairs={{0,4},{4,0},{8,12},{12,8},{16,20},{20,16},{24,28},{28,24},{1,5},{5... | collective-permute-start | bytes 147464 | tf_op jit(solution)/shard_map/ppermute | solution.py:414
  89.0 22.4 %collective-permute-start.36 = (bf16[16,1536]{1,0:T(8,128)(2,1)S(1)}, bf16[16,1536]{1,0:T(8,128)(2,1)S(1)}, u32[]{:S(2)}, u32[]{:S(2)}) collective-permute-start(bf16[16,1536]{1,0:T(8,128)(2,1)S(1)} %get-tuple-element.145), channel_id=1, source_target_pairs={{0,8},{4,12},{8,0},{12,4},{16,24},{20,28},{24,16},{28,20},{1,9},{5... | collective-permute-start | bytes 147464 | tf_op jit(solution)/shard_map/ppermute | solution.py:414
  90.5 21.0 %collective-permute-start.37 = (bf16[16,1536]{1,0:T(8,128)(2,1)S(1)}, bf16[16,1536]{1,0:T(8,128)(2,1)S(1)}, u32[]{:S(2)}, u32[]{:S(2)}) collective-permute-start(bf16[16,1536]{1,0:T(8,128)(2,1)S(1)} %get-tuple-element.144), channel_id=1, source_target_pairs={{0,12},{4,8},{8,4},{12,0},{16,28},{20,24},{24,20},{28,16},{1,13},{... | collective-permute-start | bytes 147464 | tf_op jit(solution)/shard_map/ppermute | solution.py:414
  90.9 22.2 %collective-permute-start.38 = (bf16[16,1536]{1,0:T(8,128)(2,1)S(1)}, bf16[16,1536]{1,0:T(8,128)(2,1)S(1)}, u32[]{:S(2)}, u32[]{:S(2)}) collective-permute-start(bf16[16,1536]{1,0:T(8,128)(2,1)S(1)} %get-tuple-element.143), channel_id=1, source_target_pairs={{0,16},{4,20},{8,24},{12,28},{16,0},{20,4},{24,8},{28,12},{1,17},{... | collective-permute-start | bytes 147464 | tf_op jit(solution)/shard_map/ppermute | solution.py:414
  93.5 19.7 %collective-permute-start.39 = (bf16[16,1536]{1,0:T(8,128)(2,1)S(1)}, bf16[16,1536]{1,0:T(8,128)(2,1)S(1)}, u32[]{:S(2)}, u32[]{:S(2)}) collective-permute-start(bf16[16,1536]{1,0:T(8,128)(2,1)S(1)} %get-tuple-element.142), channel_id=1, source_target_pairs={{0,20},{4,16},{8,28},{12,24},{16,4},{20,0},{24,12},{28,8},{1,21},{... | collective-permute-start | bytes 147464 | tf_op jit(solution)/shard_map/ppermute | solution.py:414
  113.2 10.6 %collective-permute-start.23 = (bf16[16,1664]{1,0:T(8,128)(2,1)S(1)}, bf16[16,1664]{1,0:T(8,128)(2,1)S(1)}, u32[]{:S(2)}, u32[]{:S(2)}) collective-permute-start(bf16[16,1664]{1,0:T(8,128)(2,1)S(1)} %get-tuple-element.137), channel_id=1, source_target_pairs={{0,12},{4,8},{8,4},{12,0},{16,28},{20,24},{24,20},{28,16},{1,13},{... | collective-permute-start | bytes 159752 | tf_op jit(solution)/shard_map/ppermute | solution.py:414
  115.2 10.2 %collective-permute-start.24 = (bf16[16,1664]{1,0:T(8,128)(2,1)S(1)}, bf16[16,1664]{1,0:T(8,128)(2,1)S(1)}, u32[]{:S(2)}, u32[]{:S(2)}) collective-permute-start(bf16[16,1664]{1,0:T(8,128)(2,1)S(1)} %get-tuple-element.136), channel_id=1, source_target_pairs={{0,16},{4,20},{8,24},{12,28},{16,0},{20,4},{24,8},{28,12},{1,17},{... | collective-permute-start | bytes 159752 | tf_op jit(solution)/shard_map/ppermute | solution.py:414
  123.7 43.7 %collective-permute-start.49 = (bf16[16,3072]{1,0:T(8,128)(2,1)S(1)}, bf16[16,3072]{1,0:T(8,128)(2,1)S(1)}, u32[]{:S(2)}, u32[]{:S(2)}) collective-permute-start(bf16[16,3072]{1,0:T(8,128)(2,1)S(1)} %get-tuple-element.119), channel_id=1, source_target_pairs={{0,4},{4,0},{8,12},{12,8},{16,20},{20,16},{24,28},{28,24},{1,5},{5... | collective-permute-start | bytes 294920 | tf_op jit(solution)/shard_map/ppermute | solution.py:414
  125.3 44.8 %collective-permute-start.50 = (bf16[16,3072]{1,0:T(8,128)(2,1)S(1)}, bf16[16,3072]{1,0:T(8,128)(2,1)S(1)}, u32[]{:S(2)}, u32[]{:S(2)}) collective-permute-start(bf16[16,3072]{1,0:T(8,128)(2,1)S(1)} %get-tuple-element.125), channel_id=1, source_target_pairs={{0,8},{4,12},{8,0},{12,4},{16,24},{20,28},{24,16},{28,20},{1,9},{5... | collective-permute-start | bytes 294920 | tf_op jit(solution)/shard_map/ppermute | solution.py:414
  126.2 46.3 %collective-permute-start.51 = (bf16[16,3072]{1,0:T(8,128)(2,1)S(1)}, bf16[16,3072]{1,0:T(8,128)(2,1)S(1)}, u32[]{:S(2)}, u32[]{:S(2)}) collective-permute-start(bf16[16,3072]{1,0:T(8,128)(2,1)S(1)} %get-tuple-element.124), channel_id=1, source_target_pairs={{0,12},{4,8},{8,4},{12,0},{16,28},{20,24},{24,20},{28,16},{1,13},{... | collective-permute-start | bytes 294920 | tf_op jit(solution)/shard_map/ppermute | solution.py:414
  127.3 45.7 %collective-permute-start.52 = (bf16[16,3072]{1,0:T(8,128)(2,1)S(1)}, bf16[16,3072]{1,0:T(8,128)(2,1)S(1)}, u32[]{:S(2)}, u32[]{:S(2)}) collective-permute-start(bf16[16,3072]{1,0:T(8,128)(2,1)S(1)} %get-tuple-element.123), channel_id=1, source_target_pairs={{0,16},{4,20},{8,24},{12,28},{16,0},{20,4},{24,8},{28,12},{1,17},{... | collective-permute-start | bytes 294920 | tf_op jit(solution)/shard_map/ppermute | solution.py:414
  167.4 11.1 %collective-permute-start.53 = (bf16[16,3072]{1,0:T(8,128)(2,1)S(1)}, bf16[16,3072]{1,0:T(8,128)(2,1)S(1)}, u32[]{:S(2)}, u32[]{:S(2)}) collective-permute-start(bf16[16,3072]{1,0:T(8,128)(2,1)S(1)} %get-tuple-element.122), channel_id=1, source_target_pairs={{0,20},{4,16},{8,28},{12,24},{16,4},{20,0},{24,12},{28,8},{1,21},{... | collective-permute-start | bytes 294920 | tf_op jit(solution)/shard_map/ppermute | solution.py:414
  167.5 11.0 %collective-permute-start.54 = (bf16[16,3072]{1,0:T(8,128)(2,1)S(1)}, bf16[16,3072]{1,0:T(8,128)(2,1)S(1)}, u32[]{:S(2)}, u32[]{:S(2)}) collective-permute-start(bf16[16,3072]{1,0:T(8,128)(2,1)S(1)} %get-tuple-element.121), channel_id=1, source_target_pairs={{0,24},{4,28},{8,16},{12,20},{16,8},{20,12},{24,0},{28,4},{1,25},{... | collective-permute-start | bytes 294920 | tf_op jit(solution)/shard_map/ppermute | solution.py:414
  170.2 11.3 %collective-permute-start.55 = (bf16[16,3072]{1,0:T(8,128)(2,1)S(1)}, bf16[16,3072]{1,0:T(8,128)(2,1)S(1)}, u32[]{:S(2)}, u32[]{:S(2)}) collective-permute-start(bf16[16,3072]{1,0:T(8,128)(2,1)S(1)} %get-tuple-element.120), channel_id=1, source_target_pairs={{0,28},{4,24},{8,20},{12,16},{16,12},{20,8},{24,4},{28,0},{1,29},{... | collective-permute-start | bytes 294920 | tf_op jit(solution)/shard_map/ppermute | solution.py:414
  172.5 12.3 %collective-permute-start.28 = (bf16[16,1664]{1,0:T(8,128)(2,1)S(1)}, bf16[16,1664]{1,0:T(8,128)(2,1)S(1)}, u32[]{:S(2)}, u32[]{:S(2)}) collective-permute-start(bf16[16,1664]{1,0:T(8,128)(2,1)S(1)} %get-tuple-element.105), channel_id=1, source_target_pairs={{0,4},{4,0},{8,12},{12,8},{16,20},{20,16},{24,28},{28,24},{1,5},{5... | collective-permute-start | bytes 159752 | tf_op jit(solution)/shard_map/ppermute | solution.py:414
  173.0 13.4 %collective-permute-start.29 = (bf16[16,1664]{1,0:T(8,128)(2,1)S(1)}, bf16[16,1664]{1,0:T(8,128)(2,1)S(1)}, u32[]{:S(2)}, u32[]{:S(2)}) collective-permute-start(bf16[16,1664]{1,0:T(8,128)(2,1)S(1)} %get-tuple-element.105), channel_id=1, source_target_pairs={{0,8},{4,12},{8,0},{12,4},{16,24},{20,28},{24,16},{28,20},{1,9},{5... | collective-permute-start | bytes 159752 | tf_op jit(solution)/shard_map/ppermute | solution.py:414
  178.5 11.9 %collective-permute-start.31 = (bf16[16,1664]{1,0:T(8,128)(2,1)S(1)}, bf16[16,1664]{1,0:T(8,128)(2,1)S(1)}, u32[]{:S(2)}, u32[]{:S(2)}) collective-permute-start(bf16[16,1664]{1,0:T(8,128)(2,1)S(1)} %get-tuple-element.105), channel_id=1, source_target_pairs={{0,16},{4,20},{8,24},{12,28},{16,0},{20,4},{24,8},{28,12},{1,17},{... | collective-permute-start | bytes 159752 | tf_op jit(solution)/shard_map/ppermute | solution.py:414
  188.6 11.1 %collective-permute-start.56 = (bf16[16,3072]{1,0:T(8,128)(2,1)S(1)}, bf16[16,3072]{1,0:T(8,128)(2,1)S(1)}, u32[]{:S(2)}, u32[]{:S(2)}) collective-permute-start(bf16[16,3072]{1,0:T(8,128)(2,1)S(1)} %get-tuple-element.101), channel_id=1, source_target_pairs={{0,4},{4,0},{8,12},{12,8},{16,20},{20,16},{24,28},{28,24},{1,5},{5... | collective-permute-start | bytes 294920 | tf_op jit(solution)/shard_map/ppermute | solution.py:414
  190.4 10.8 %collective-permute-start.57 = (bf16[16,3072]{1,0:T(8,128)(2,1)S(1)}, bf16[16,3072]{1,0:T(8,128)(2,1)S(1)}, u32[]{:S(2)}, u32[]{:S(2)}) collective-permute-start(bf16[16,3072]{1,0:T(8,128)(2,1)S(1)} %get-tuple-element.101), channel_id=1, source_target_pairs={{0,8},{4,12},{8,0},{12,4},{16,24},{20,28},{24,16},{28,20},{1,9},{5... | collective-permute-start | bytes 294920 | tf_op jit(solution)/shard_map/ppermute | solution.py:414
  190.5 12.9 %collective-permute-start.58 = (bf16[16,3072]{1,0:T(8,128)(2,1)S(1)}, bf16[16,3072]{1,0:T(8,128)(2,1)S(1)}, u32[]{:S(2)}, u32[]{:S(2)}) collective-permute-start(bf16[16,3072]{1,0:T(8,128)(2,1)S(1)} %get-tuple-element.101), channel_id=1, source_target_pairs={{0,12},{4,8},{8,4},{12,0},{16,28},{20,24},{24,20},{28,16},{1,13},{... | collective-permute-start | bytes 294920 | tf_op jit(solution)/shard_map/ppermute | solution.py:414
  192.3 11.1 %collective-permute-start.59 = (bf16[16,3072]{1,0:T(8,128)(2,1)S(1)}, bf16[16,3072]{1,0:T(8,128)(2,1)S(1)}, u32[]{:S(2)}, u32[]{:S(2)}) collective-permute-start(bf16[16,3072]{1,0:T(8,128)(2,1)S(1)} %get-tuple-element.101), channel_id=1, source_target_pairs={{0,16},{4,20},{8,24},{12,28},{16,0},{20,4},{24,8},{28,12},{1,17},{... | collective-permute-start | bytes 294920 | tf_op jit(solution)/shard_map/ppermute | solution.py:414
  (60 other events, 895.7 us)

commit v2 on v1

v2 whole, which is shorter than its diff:
```python
import functools
import math

import jax
import jax.numpy as jnp
from jax import lax
from jax.experimental import pallas as pl
from jax.experimental.pallas import tpu as pltpu
from jax.sharding import PartitionSpec as P

H = 6
DH = 64
PAIRS = H // 2
BUCKETS = 32
MAXDIST = 128
EPSILON = 1e-06
MASKED = -1000000000.0
BLOCK = 128
HALF = 256
GROUP = 4
PIECES = 8
VMEM_BYTES = 32 * 1024 * 1024
HIGHEST = lax.Precision.HIGHEST
F32 = jnp.float32
BF16 = jnp.bfloat16


def dot(a, b):
    return jnp.dot(a, b, preferred_element_type=F32)


def dot_t(a, b):
    return lax.dot_general(a, b, (((1,), (1,)), ((), ())), preferred_element_type=F32)


def t_dot(a, b):
    return lax.dot_general(a, b, (((0,), (0,)), ((), ())), preferred_element_type=F32)


def own(f, size):
    return pl.ds(pl.multiple_of(f * size, size), size)


def place_rows(dst, pieces, f, first, size):
    for k, piece in enumerate(pieces):
        dst[own(f ^ k, size), :] = piece[first : first + size, :].astype(dst.dtype)


def place_mine(ref, f):
    return jnp.concatenate([ref[own(b, BLOCK), :] for b in my_blocks(f)], axis=0)


def my_blocks(f):
    a = (f ^ (f >> 1)) & 1
    return a, 3 - a


def split_pieces(pieces, f, half):
    for k, piece in enumerate(pieces[:2]):
        rows = piece.shape[0] // 2
        for h in range(2):
            yield f ^ k, h, piece, h * rows, rows
    for i, piece in enumerate(pieces[2:]):
        yield f ^ (2 + i // 2), half ^ (i % 2), piece, 0, piece.shape[0]


def place_split_rows(dst, pieces, f, half):
    for owner, h, piece, first, rows in split_pieces(pieces, f, half):
        dst[own(2 * owner + h, rows), :] = piece[first : first + rows, :]


def place_split_columns(dst, pieces, f, half):
    for owner, h, piece, first, rows in split_pieces(pieces, f, half):
        dst[own(h, rows), own(owner, piece.shape[1])] = piece[first : first + rows, :]


def bucket_of(distance):
    exact_span = BUCKETS // 2
    bucket = jnp.minimum(distance, exact_span)
    for power in range(1, exact_span):
        threshold = math.ceil(exact_span * (MAXDIST / exact_span) ** (power / exact_span))
        bucket = bucket + (distance >= threshold).astype(jnp.int32)
    return bucket


def offset_onehot(rows, axis):
    shape = (rows, 4 * BLOCK) if axis == 1 else (4 * BLOCK, rows)
    m = lax.broadcasted_iota(jnp.int32, shape, axis)
    n = jnp.where(m < 2 * BLOCK, BLOCK - m, 5 * BLOCK - m)
    bucket = bucket_of(jnp.maximum(n, 0))
    return (bucket == lax.broadcasted_iota(jnp.int32, shape, 1 - axis)).astype(F32)


def rms(v):
    return lax.rsqrt(jnp.mean(v * v, axis=-1, keepdims=True) + EPSILON)


def head_lanes(rows):
    lane = lax.broadcasted_iota(jnp.int32, (rows, 2 * DH), 1)
    return lane < DH


def only_head(pair, hd):
    low = head_lanes(pair.shape[0])
    zero = jnp.zeros_like(pair)
    return jnp.where(low, pair, zero) if hd == 0 else jnp.where(low, zero, pair)


def softmax(s):
    lifted = jnp.exp(s - jnp.max(s, axis=-1, keepdims=True))
    return lifted * (1.0 / jnp.sum(lifted, axis=-1, keepdims=True))


def norm_back(v, gain, q):
    r = rms(v)
    u = q * gain
    vr = v * r
    return r * (u - vr * jnp.mean(vr * u, axis=-1, keepdims=True)), q * vr


def stack_heads(pair):
    low = head_lanes(pair.shape[0])
    zero = jnp.zeros_like(pair)
    return jnp.concatenate([jnp.where(low, pair, zero), jnp.where(low, zero, pair)], axis=0)


def unstack_heads(stacked):
    rows = stacked.shape[0] // 2
    return jnp.where(head_lanes(rows), stacked[:rows, :], stacked[rows:, :])


def emit(keep_ref, send_ref, chip_s, first, f, order):
    core = f & 1
    rows = keep_ref.shape[0]
    piece = rows // PIECES
    columns = chip_s.shape[1]
    for q in range(PIECES):
        to = pl.ds(pl.multiple_of((q ^ order) * piece, piece), piece)
        for ref, which in ((keep_ref, core), (send_ref, 1 - core)):
            at = pl.ds(pl.multiple_of(which * rows + q * piece, piece), piece)
            ref[to, first : first + columns] = chip_s[at, :]


def pack_first(tokens_ref, q_ref, k_ref, v_ref, pack_ref, pack_s, sems):
    width, inner = tokens_ref.shape[1], q_ref.shape[1]
    copies, first = [], 0
    for i, ref in enumerate((tokens_ref, q_ref, k_ref, v_ref)):
        copies.append(pltpu.make_async_copy(ref, pack_s.at[:, first : first + ref.shape[1]], sems.at[i]))
        copies[-1].start()
        first += ref.shape[1]
    for c in copies:
        c.wait()
    out = pltpu.make_async_copy(pack_s, pack_ref, sems.at[4])
    out.start()
    out.wait()


def run_copies(pairs, sems):
    copies = [pltpu.make_async_copy(a, b, sems.at[i]) for i, (a, b) in enumerate(pairs)]
    for c in copies:
        c.start()
    for c in copies:
        c.wait()


def half_of(ref, half):
    rows = ref.shape[0] // 2
    return ref.at[pl.ds(pl.multiple_of(half * rows, rows), rows), :]


def pack_second(
    ids_ref, cq_ref, ck_ref, cv_ref, out_ref, co_ref, cross_ref, outs_ref, cross_half, out_half,
    cross_s, outs_s, in_sems, out_sems,
):
    half, inner = ids_ref[2], cq_ref.shape[1]
    run_copies(
        [(ref, cross_s.at[:, i * inner : (i + 1) * inner]) for i, ref in enumerate((cq_ref, ck_ref, cv_ref))]
        + [(ref, outs_s.at[i * inner : (i + 1) * inner, :]) for i, ref in enumerate((out_ref, co_ref))],
        in_sems,
    )
    run_copies(
        [(half_of(cross_s, half), cross_half), (half_of(outs_s, half), out_half), (cross_s, cross_ref), (outs_s, outs_ref)],
        out_sems,
    )


def pack_third(ids_ref, gate_ref, up_ref, down_ref, gu_ref, gu_half, down_half, gu_s, down_s, in_sems, out_sems):
    half, units = ids_ref[2], gate_ref.shape[1]
    run_copies([(gate_ref, gu_s.at[:, :units]), (up_ref, gu_s.at[:, units:]), (down_ref, down_s)], in_sems)
    run_copies([(half_of(gu_s, half), gu_half), (half_of(down_s, half), down_half), (gu_s, gu_ref)], out_sems)


def self_forward(
    ids_ref, w0, w1, w2, w3, a0, a1, a2, a3,
    x_ref, normed_ref, q_ref, kv_ref, pa_ref, pb_ref, mixed_ref, aux_ref,
    w_s, bias_a, bias_b,
):
    f = ids_ref[0]
    length, width = x_ref.shape
    inner = H * DH
    for k, piece in enumerate((w0, w1, w2, w3)):
        x_ref[own(f ^ k, w0.shape[0]), :] = piece[:, :width]
        w_s[own(f ^ k, w0.shape[0]), :] = piece[:, width:]
    aux = sum(a[...].astype(F32) for a in (a0, a1, a2, a3))
    aux_ref[...] = aux
    for hb in range(length // HALF):
        at = slice(hb * HALF, (hb + 1) * HALF)
        x = x_ref[at, :].astype(F32)
        normed = (x * rms(x) * aux[0:1, :]).astype(BF16)
        normed_ref[at, :] = normed
        kv_ref[at, :] = dot(normed, w_s[:, inner:]).astype(BF16)
    q_ref[...] = dot(place_mine(normed_ref, f), w_s[:, :inner]).astype(BF16)
    per_offset = jnp.dot(
        aux[8:16, 0:BLOCK], offset_onehot(BLOCK, 1), precision=HIGHEST, preferred_element_type=F32
    )
    first, second = my_blocks(f)
    row = lax.broadcasted_iota(jnp.int32, (BLOCK, 2 * BLOCK), 0)
    col = lax.broadcasted_iota(jnp.int32, (BLOCK, 2 * BLOCK), 1)
    lane = lax.broadcasted_iota(jnp.int32, (BLOCK, length), 1)
    is_far = lane < (second - 1) * BLOCK
    bias_a[:, :, 2 * BLOCK :] = jnp.full((PAIRS, 2 * BLOCK, BLOCK), MASKED, F32)
    for h in range(H):
        at = slice((h % 2) * BLOCK, (h % 2 + 1) * BLOCK)
        spread = jnp.broadcast_to(per_offset[h : h + 1, :], (BLOCK, 4 * BLOCK))
        skewed = pltpu.roll(spread, 0, 1, stride=1, stride_axis=0)[:, : 2 * BLOCK]
        band = jnp.where(col - BLOCK > row, MASKED, skewed)
        bias_a[h // 2, at, pl.ds(pl.multiple_of(first * BLOCK, BLOCK), 2 * BLOCK)] = band
        bias_b[h // 2, at, :] = jnp.where(is_far, per_offset[h : h + 1, 0:1], MASKED)
        bias_b[h // 2, at, pl.ds(pl.multiple_of((second - 1) * BLOCK, BLOCK), 2 * BLOCK)] = band
    for p in range(PAIRS):
        lanes = slice(p * BLOCK, (p + 1) * BLOCK)
        k2 = kv_ref[:, lanes]
        v2 = kv_ref[:, inner + p * BLOCK : inner + (p + 1) * BLOCK]
        for slot in range(2):
            at = slice(slot * BLOCK, (slot + 1) * BLOCK)
            bias = bias_a[p, :, BLOCK:] if slot == 0 else bias_b[p]
            seen = bias.shape[1]
            s = dot_t(stack_heads(q_ref[at, lanes]), k2[:seen, :]) + bias
            probs = softmax(s).astype(BF16)
            (pa_ref, pb_ref)[slot][p] = probs
            mixed_ref[at, lanes] = unstack_heads(dot(probs, v2[:seen, :])).astype(BF16)


def cross_forward(
    ids_ref, x_ref, mixed_ref, aux_ref,
    w0, w1, w2, w3, w4, w5, o0, o1, o2, o3, o4, o5, s0, s1, s2, s3,
    h1_ref, n2_ref, cq_ref, ckv_ref, probs_ref, cmixed_ref, h2_ref, n3_ref,
    w_s, outs_s, states_s,
):
    f = ids_ref[0]
    inner = H * DH
    half = ids_ref[2]
    place_split_rows(w_s, (w0, w1, w2, w3, w4, w5), f, half)
    place_split_columns(outs_s, (o0, o1, o2, o3, o4, o5), f, half)
    place_rows(states_s, (s0, s1, s2, s3), f, 0, s0.shape[0])
    hidden = place_mine(x_ref, f).astype(F32) + dot(mixed_ref[...], outs_s[:inner, :])
    h1_ref[...] = hidden
    normed = (hidden * rms(hidden) * aux_ref[1:2, :]).astype(BF16)
    n2_ref[...] = normed
    cq_ref[...] = dot(normed, w_s[:, :inner]).astype(BF16)
    ckv_ref[...] = dot(states_s[...], w_s[:, inner:]).astype(BF16)
    for p in range(PAIRS):
        lanes = slice(p * BLOCK, (p + 1) * BLOCK)
        v2 = ckv_ref[:, inner + p * BLOCK : inner + (p + 1) * BLOCK]
        probs = softmax(dot_t(stack_heads(cq_ref[:, lanes]), ckv_ref[:, lanes])).astype(BF16)
        probs_ref[p] = probs
        cmixed_ref[:, lanes] = unstack_heads(dot(probs, v2)).astype(BF16)
    hidden = h1_ref[...] + dot(cmixed_ref[...], outs_s[inner:, :])
    h2_ref[...] = hidden
    n3_ref[...] = (hidden * rms(hidden) * aux_ref[2:3, :]).astype(BF16)


def feed_forward(
    ids_ref, h2_ref, n3_ref, aux_ref,
    g0, g1, g2, g3, g4, g5, d0, d1, d2, d3, d4, d5, c0, c1, c2, c3,
    result_ref, grad_h2_ref, keep_ref, send_ref, gain_ref,
    gu_s, down_s, cot_s, cot_mine, units_s, gate_s, up_s, chip_s, down_chip_s,
):
    f, order = ids_ref[0], ids_ref[1]
    chip = f >> 1
    mine_rows, width = h2_ref.shape
    rows = cot_s.shape[0] // GROUP
    hidden_units = down_s.shape[0]
    own_units = hidden_units // GROUP
    half = ids_ref[2]
    place_split_rows(gu_s, (g0, g1, g2, g3, g4, g5), f, half)
    place_split_rows(down_s, (d0, d1, d2, d3, d4, d5), f, half)
    place_rows(cot_s, (c0, c1, c2, c3), f, 0, rows)
    cot_mine[...] = place_mine(cot_s, f)
    grad_normed = jnp.zeros((mine_rows, width), F32)
    chunk = 256
    for c in range(hidden_units // chunk):
        gate_at, up_at = slice(c * chunk, (c + 1) * chunk), slice(hidden_units + c * chunk, hidden_units + (c + 1) * chunk)
        gate, up = dot(n3_ref[...], gu_s[:, gate_at]), dot(n3_ref[...], gu_s[:, up_at])
        grad_units = dot_t(cot_mine[...], down_s[gate_at, :])
        square = gate * gate
        tanh = jnp.tanh(0.7978845608028654 * (gate + 0.044715 * square * gate))
        half_gate = 0.5 * gate
        gelu = half_gate + half_gate * tanh
        slope = 0.5 + 0.5 * tanh + half_gate * (1.0 - tanh * tanh) * (
            0.7978845608028654 + (3 * 0.044715 * 0.7978845608028654) * square
        )
        units_s[:, gate_at] = (gelu * up).astype(BF16)
        grad_gate = (grad_units * up * slope).astype(BF16)
        grad_up = (grad_units * gelu).astype(BF16)
        gate_s[:, gate_at] = grad_gate
        up_s[:, gate_at] = grad_up
        grad_normed = grad_normed + dot_t(grad_gate, gu_s[:, gate_at]) + dot_t(grad_up, gu_s[:, up_at])
    piece, gain_part = norm_back(h2_ref[...], aux_ref[2:3, :], grad_normed)
    grad_h2_ref[...] = cot_mine[...].astype(F32) + piece
    gain_ref[...] = jnp.broadcast_to(jnp.sum(gain_part, axis=0, keepdims=True), gain_ref.shape)
    mine = own(chip, rows)
    result_ref[...] = (h2_ref[mine, :] + dot(units_s[mine, :], down_s[...])).astype(BF16)
    chip_rows = 2 * g0.shape[0]
    normed_chip = n3_ref[:, own(chip, chip_rows)]
    chip_s[:, :hidden_units] = t_dot(normed_chip, gate_s[...]).astype(BF16)
    chip_s[:, hidden_units:] = t_dot(normed_chip, up_s[...]).astype(BF16)
    emit(keep_ref, send_ref, chip_s, 0, f, order)
    grad_down = t_dot(units_s[:, own(chip, 2 * own_units)], cot_mine[...]).astype(BF16)
    parts = own_units // g0.shape[0]
    for which in range(2):
        for part in range(parts):
            at = slice((which * parts + part) * g0.shape[0], (which * parts + part + 1) * g0.shape[0])
            down_chip_s[which * g0.shape[0] : (which + 1) * g0.shape[0], part * width : (part + 1) * width] = grad_down[at, :]
    emit(keep_ref, send_ref, down_chip_s, 2 * hidden_units, f, order)


def put_columns(chip_s, first, grad, own_rows):
    columns = grad.shape[1] // 2
    for which in range(2):
        for part in range(grad.shape[0] // own_rows):
            chip_s[which * own_rows : (which + 1) * own_rows, first + part * columns : first + (part + 1) * columns] = (
                grad[part * own_rows : (part + 1) * own_rows, which * columns : (which + 1) * columns]
            )


def cross_backward(
    ids_ref, grad_h2_ref, h1_ref, n2_ref, cq_ref, ckv_ref, probs_ref, cmixed_ref, mixed_ref, aux_ref,
    w0, w1, w2, w3, w4, w5, o0, o1, o2, o3, o4, o5, s0, s1, s2, s3,
    grad_h1_ref, mix_ref, states_keep, states_send, keep_ref, send_ref, gain_ref,
    w_s, outs_s, states_s, low_s, dq_s, dkv_s, chip_s, states_chip,
):
    f, order = ids_ref[0], ids_ref[1]
    chip, core = f >> 1, f & 1
    inner = H * DH
    own_rows = w0.shape[0]
    chip_columns = own(chip, 2 * own_rows)
    half = ids_ref[2]
    place_split_rows(w_s, (w0, w1, w2, w3, w4, w5), f, half)
    place_split_columns(outs_s, (o0, o1, o2, o3, o4, o5), f, half)
    place_rows(states_s, (s0, s1, s2, s3), f, 0, s0.shape[0])
    low = grad_h2_ref[...].astype(BF16)
    low_s[...] = low
    grad_mixed = dot_t(low, outs_s[inner:, :]).astype(BF16)
    put_columns(chip_s, 3 * inner, t_dot(cmixed_ref[...], low_s[:, chip_columns]).astype(BF16), own_rows)
    for p in range(PAIRS):
        lanes = slice(p * BLOCK, (p + 1) * BLOCK)
        v_lanes = slice(inner + p * BLOCK, inner + (p + 1) * BLOCK)
        stacked = stack_heads(grad_mixed[:, lanes])
        probs = probs_ref[p].astype(F32)
        weighted = probs * dot_t(stacked, ckv_ref[:, v_lanes])
        ds = (weighted - probs * jnp.sum(weighted, axis=-1, keepdims=True)).astype(BF16)
        dq_s[:, lanes] = unstack_heads(dot(ds, ckv_ref[:, lanes])).astype(BF16)
        dkv_s[:, lanes] = t_dot(ds, stack_heads(cq_ref[:, lanes])).astype(BF16)
        dkv_s[:, v_lanes] = t_dot(probs_ref[p], stacked).astype(BF16)
    grad_normed = dot_t(dq_s[...], w_s[:, :inner])
    piece, gain_part = norm_back(h1_ref[...], aux_ref[1:2, :], grad_normed)
    grad_h1 = grad_h2_ref[...] + piece
    grad_h1_ref[...] = grad_h1
    gain_ref[...] = jnp.broadcast_to(jnp.sum(gain_part, axis=0, keepdims=True), gain_ref.shape)
    low = grad_h1.astype(BF16)
    low_s[...] = low
    mix_ref[...] = dot_t(low, outs_s[:inner, :]).astype(BF16)
    put_columns(chip_s, 4 * inner, t_dot(mixed_ref[...], low_s[:, chip_columns]).astype(BF16), own_rows)
    chip_s[:, :inner] = t_dot(n2_ref[:, chip_columns], dq_s[...]).astype(BF16)
    chip_s[:, inner : 3 * inner] = t_dot(states_s[:, chip_columns], dkv_s[...]).astype(BF16)
    emit(keep_ref, send_ref, chip_s, 0, f, order)
    enc = s0.shape[0]
    states_chip[...] = dot_t(dkv_s[own(chip, 2 * enc), :], w_s[:, inner:])
    states_keep[...] = states_chip[own(core, enc), :]
    states_send[...] = states_chip[own(1 - core, enc), :]


def self_backward(
    ids_ref, grad_h1_ref, mix_ref, x_ref, normed_ref, q_ref, kv_ref, pa_ref, pb_ref, aux_ref, gain2_ref, gain3_ref,
    w0, w1, w2, w3,
    tokens_keep, tokens_send, keep_ref, send_ref,
    w_s, dq_s, dkv_s, ds_a, ds_b, chip_s, small_s, gain_s, table_s,
):
    f, order = ids_ref[0], ids_ref[1]
    chip, core = f >> 1, f & 1
    length, width = x_ref.shape
    rows = length // GROUP
    inner = H * DH
    own_rows = w0.shape[0]
    chip_columns = own(chip, 2 * own_rows)
    for k, piece in enumerate((w0, w1, w2, w3)):
        w_s[own(f ^ k, own_rows), :] = piece[:, width:]
    first, second = my_blocks(f)
    row = lax.broadcasted_iota(jnp.int32, (2 * BLOCK, 4 * BLOCK), 0)
    ds_a[:, 0:BLOCK] = jnp.zeros((2 * BLOCK, BLOCK), F32)
    offset_sums, far_sums = [], []
    for p in range(PAIRS):
        lanes = slice(p * BLOCK, (p + 1) * BLOCK)
        v_lanes = slice(inner + p * BLOCK, inner + (p + 1) * BLOCK)
        k2, v2 = kv_ref[:, lanes], kv_ref[:, v_lanes]
        dk, dv = [], []
        for slot in range(2):
            at = slice(slot * BLOCK, (slot + 1) * BLOCK)
            probs_low = (pa_ref, pb_ref)[slot][p]
            seen = probs_low.shape[1]
            stacked = stack_heads(mix_ref[at, lanes])
            probs = probs_low.astype(F32)
            weighted = probs * dot_t(stacked, v2[:seen, :])
            ds = weighted - probs * jnp.sum(weighted, axis=-1, keepdims=True)
            if slot == 0:
                ds_a[:, BLOCK:] = ds
            else:
                ds_b[...] = ds
            low = ds.astype(BF16)
            dq_s[at, lanes] = unstack_heads(dot(low, k2[:seen, :])).astype(BF16)
            dk.append(t_dot(low, stack_heads(q_ref[at, lanes])))
            dv.append(t_dot(probs_low, stacked))
        for total, to in ((dk, lanes), (dv, v_lanes)):
            seen = total[0].shape[0]
            dkv_s[:seen, to] = (total[0] + total[1][:seen, :]).astype(BF16)
            dkv_s[seen:, to] = total[1][seen:, :].astype(BF16)
        band_b = ds_b[:, pl.ds(pl.multiple_of((second - 1) * BLOCK, BLOCK), 2 * BLOCK)]
        band_a = ds_a[:, pl.ds(pl.multiple_of(first * BLOCK, BLOCK), 2 * BLOCK)]
        far = jnp.sum(ds_b[...], axis=1, keepdims=True) - jnp.sum(band_b, axis=1, keepdims=True)
        skew = jnp.concatenate([band_a + band_b, jnp.zeros((2 * BLOCK, 2 * BLOCK), F32)], axis=1)
        for bit in range(BLOCK.bit_length() - 1):
            moved = pltpu.roll(skew, 4 * BLOCK - (1 << bit), 1)
            skew = jnp.where((row & (1 << bit)) != 0, moved, skew)
        for hd in range(2):
            at = slice(hd * BLOCK, (hd + 1) * BLOCK)
            offset_sums.append(jnp.sum(skew[at, :], axis=0, keepdims=True))
            far_sums.append(jnp.sum(far[at, :], axis=0, keepdims=True))
    per_offset = jnp.concatenate(offset_sums + [jnp.zeros((BLOCK - H, 4 * BLOCK), F32)], axis=0)
    far_all = jnp.concatenate(far_sums + [jnp.zeros((BLOCK - H, 1), F32)], axis=0)
    per_offset = per_offset + jnp.where(
        lax.broadcasted_iota(jnp.int32, (BLOCK, 4 * BLOCK), 1) == 0, far_all, 0.0
    )
    table_s[...] = lax.dot_general(
        offset_onehot(BLOCK, 1), per_offset, (((1,), (1,)), ((), ())),
        precision=HIGHEST, preferred_element_type=F32,
    )

    gain = aux_ref[0:1, :]
    mine, block = own(chip, rows), own(f, rows)
    others = own(f ^ 1, rows)
    grad_normed = dot_t(dq_s[mine, :], w_s[:, :inner]) + dot_t(dkv_s[block, :], w_s[:, inner:])
    piece, _ = norm_back(x_ref[block, :].astype(F32), gain, grad_normed)
    tokens_keep[...] = grad_h1_ref[mine, :] + piece
    piece, _ = norm_back(x_ref[others, :].astype(F32), gain, dot_t(dkv_s[others, :], w_s[:, inner:]))
    tokens_send[...] = piece
    chip_w = w_s[chip_columns, :]
    gain_sum = jnp.zeros((1, 2 * own_rows), F32)
    for hb in range(length // HALF):
        at = slice(hb * HALF, (hb + 1) * HALF)
        scaled = x_ref[at, chip_columns].astype(F32) * rms(x_ref[at, :].astype(F32))
        gain_sum = gain_sum + jnp.sum(dot_t(dkv_s[at, :], chip_w[:, inner:]) * scaled, axis=0, keepdims=True)
    grad_q = dot_t(dq_s[...], chip_w[:, :inner])
    for slot, b in enumerate((first, second)):
        scaled = x_ref[own(b, BLOCK), chip_columns].astype(F32) * rms(x_ref[own(b, BLOCK), :].astype(F32))
        gain_sum = gain_sum + jnp.sum(grad_q[slot * BLOCK : (slot + 1) * BLOCK, :] * scaled, axis=0, keepdims=True)
    normed_mine = jnp.concatenate([normed_ref[own(b, BLOCK), chip_columns] for b in (first, second)], axis=0)
    chip_s[:, :inner] = t_dot(normed_mine, dq_s[...]).astype(BF16)
    chip_s[:, inner:] = t_dot(normed_ref[:, chip_columns], dkv_s[...]).astype(BF16)
    emit(keep_ref, send_ref, chip_s, 0, f, order)
    gain_s[0:8, :] = gain2_ref[...]
    gain_s[8:16, :] = gain3_ref[...]
    buckets = BUCKETS // GROUP
    for which in range(2):
        owner = 2 * chip + which
        small = jnp.concatenate(
            [
                table_s[own(owner, buckets), :],
                gain_sum[:, which * own_rows : (which + 1) * own_rows],
                gain_s[0:1, own(owner, own_rows)],
                gain_s[8:9, own(owner, own_rows)],
                jnp.zeros((own_rows - buckets - 3, BLOCK), F32),
            ],
            axis=0,
        )
        small_s[which * own_rows : (which + 1) * own_rows, :] = small.astype(BF16)
    emit(keep_ref, send_ref, small_s, 3 * inner, f, order)


def fold(keep_ref, arrived_ref, *out_refs):
    total = (keep_ref[...].astype(F32) + arrived_ref[...].astype(F32)).astype(BF16)
    rows = total.shape[0] // len(out_refs)
    for i, ref in enumerate(out_refs):
        ref[...] = total[i * rows : (i + 1) * rows, :]


def pieces_of(ids_ref, halves):
    order = ids_ref[1]
    for i, half in enumerate(halves):
        piece = half.shape[0] * len(halves) // PIECES
        here = PIECES // len(halves)
        for j in range(here):
            q = (i * here + j) ^ order
            yield q * piece, piece, half[j * piece : (j + 1) * piece, :].astype(F32)


def unpack_feed(ids_ref, low_ref, high_ref, gate_ref, up_ref, down_ref):
    units, width, own_rows = gate_ref.shape[1], down_ref.shape[1], gate_ref.shape[0]
    for at, size, rows in pieces_of(ids_ref, (low_ref, high_ref)):
        to = pl.ds(pl.multiple_of(at, size), size)
        gate_ref[to, :] = rows[:, :units]
        up_ref[to, :] = rows[:, units : 2 * units]
        for part in range(down_ref.shape[0] // own_rows):
            first = 2 * units + part * width
            down_ref[pl.ds(pl.multiple_of(part * own_rows + at, size), size), :] = rows[:, first : first + width]


def unpack_cross(ids_ref, low_ref, high_ref, cq_ref, ck_ref, cv_ref, co_ref, out_ref):
    own_rows, inner = cq_ref.shape
    for at, size, rows in pieces_of(ids_ref, (low_ref, high_ref)):
        to = pl.ds(pl.multiple_of(at, size), size)
        for i, ref in enumerate((cq_ref, ck_ref, cv_ref)):
            ref[to, :] = rows[:, i * inner : (i + 1) * inner]
        for i, ref in enumerate((co_ref, out_ref)):
            columns = ref.shape[1]
            for part in range(inner // own_rows):
                first = (3 + i) * inner + part * columns
                ref[pl.ds(pl.multiple_of(part * own_rows + at, size), size), :] = rows[:, first : first + columns]


def unpack_self(ids_ref, low_ref, high_ref, q_ref, k_ref, v_ref, g1_ref, g2_ref, g3_ref, table_ref, small_s):
    inner = q_ref.shape[1]
    for at, size, rows in pieces_of(ids_ref, (low_ref, high_ref)):
        to = pl.ds(pl.multiple_of(at, size), size)
        for i, ref in enumerate((q_ref, k_ref, v_ref)):
            ref[to, :] = rows[:, i * inner : (i + 1) * inner]
        small_s[to, :] = rows[:, 3 * inner :]
    buckets, heads = table_ref.shape
    table_ref[...] = small_s[0:buckets, 0:heads]
    for i, ref in enumerate((g1_ref, g2_ref, g3_ref)):
        ref[...] = small_s[buckets + i : buckets + i + 1, :]


VMEM = pl.BlockSpec(memory_space=pltpu.VMEM)
SMEM = pl.BlockSpec(memory_space=pltpu.SMEM)


def call(kernel, name, out_shapes, scratch, args, flops, with_ids=True, place=VMEM):
    moved = sum(a.size * a.dtype.itemsize for a in args)
    return pl.pallas_call(
        kernel,
        name=name,
        out_shape=[jax.ShapeDtypeStruct(s, d) for s, d in out_shapes],
        in_specs=([SMEM] if with_ids else []) + [place] * (len(args) - with_ids),
        out_specs=[place] * len(out_shapes),
        scratch_shapes=[pltpu.VMEM(*s) if isinstance(s, tuple) else s for s in scratch],
        compiler_params=pltpu.CompilerParams(vmem_limit_bytes=VMEM_BYTES if place is VMEM else 56 * 1024 * 1024),
        cost_estimate=pl.CostEstimate(flops=flops, bytes_accessed=moved, transcendentals=0),
    )(*args)


def hop(x, axis, bits):
    size = lax.axis_size(axis)
    return lax.ppermute(x, axis, [(i, i ^ bits) for i in range(size)])


def all_after(arrays, earlier):
    return lax.optimization_barrier((tuple(arrays), tuple(earlier)))[0]


def beside(pack, far):
    return pack, hop(pack, "fsdp", 1), far, hop(far, "fsdp", 1)


def beside_split(pack, far, far_other):
    return pack, hop(pack, "fsdp", 1), far, far_other, hop(far, "fsdp", 1), hop(far_other, "fsdp", 1)


class Sum:
    def __init__(self, name, keep, send, steps):
        self.name, self.keep, self.steps, self.at = name, keep, steps, 0
        self.arrived = hop(send, "fsdp", 1)

    def fold(self, earlier):
        keep, arrived = all_after((self.keep, self.arrived), earlier)
        halving = self.at < len(self.steps) and (1 << self.at) < PIECES
        shape = (keep.shape[0] // 2, keep.shape[1]) if halving else keep.shape
        out = call(fold, f"{self.name}_fold", [(shape, BF16)] * (1 + halving), [], [keep, arrived], 0, False)
        self.keep = out[0]
        if self.at < len(self.steps):
            self.arrived = hop(out[-1], "rep", self.steps[self.at])
        else:
            self.back = [i for i in range(len(self.steps)) if (1 << i) < PIECES]
            self.arrived = hop(self.keep, "rep", self.steps[self.back[-1]])
        self.at += 1
        return self.keep

    def widen(self, earlier):
        keep, arrived = all_after((self.keep, self.arrived), earlier)
        self.back.pop()
        self.keep = jnp.concatenate((keep, arrived))
        self.arrived = hop(self.keep, "rep", self.steps[self.back[-1]])
        return self.keep

    def halves(self, earlier):
        return all_after((self.keep, self.arrived), earlier)


def per_device(
    tokens,
    states,
    query_w,
    key_w,
    value_w,
    out_w,
    cross_query_w,
    cross_key_w,
    cross_value_w,
    cross_out_w,
    gate_w,
    up_w,
    down_w,
    self_gain,
    cross_gain,
    mlp_gain,
    bias_table,
    cotangent,
):
    seq_count, rows, width = tokens.shape
    enc = states.shape[1]
    own_rows, inner = query_w.shape
    hidden_units = gate_w.shape[1]
    length, enc_all, mine = rows * GROUP, enc * GROUP, 2 * BLOCK
    f = lax.axis_index("fsdp").astype(jnp.int32)
    replica = lax.axis_index("rep").astype(jnp.int32)
    steps = [1 << i for i in range((lax.axis_size("rep") - 1).bit_length())]
    order = ((replica & 1) << 2) | (replica & 2) | ((replica >> 2) & 1)
    half = replica & 1
    ids = jnp.stack([f, order, half])

    hbm = pl.BlockSpec(memory_space=pl.ANY)
    (first_pack,) = call(
        pack_first,
        "pack_first",
        [((rows, width + 3 * inner), BF16)],
        [((rows, width + 3 * inner), BF16), pltpu.SemaphoreType.DMA((5,))],
        [tokens[0], query_w, key_w, value_w],
        0,
        False,
        hbm,
    )
    aux = jnp.zeros((16, width), BF16)
    aux = lax.dynamic_update_slice(aux, jnp.stack([self_gain, cross_gain, mlp_gain]), (0, f * own_rows))
    aux = lax.dynamic_update_slice(aux, bias_table.T, (8, f * bias_table.shape[0]))
    (aux,) = all_after((aux,), (first_pack,))
    (second_ids,) = all_after((ids,), (aux,))
    cross_pack, out_pack, cross_half, out_half = call(
        pack_second,
        "pack_second",
        [
            ((own_rows, 3 * inner), BF16),
            ((2 * inner, own_rows), BF16),
            ((own_rows // 2, 3 * inner), BF16),
            ((inner, own_rows), BF16),
        ],
        [
            ((own_rows, 3 * inner), BF16),
            ((2 * inner, own_rows), BF16),
            pltpu.SemaphoreType.DMA((5,)),
            pltpu.SemaphoreType.DMA((4,)),
        ],
        [second_ids, cross_query_w, cross_key_w, cross_value_w, out_w, cross_out_w],
        0,
        place=hbm,
    )
    third_ids, states_own = all_after((ids, states[0]), (cross_pack,))
    gate_pack, gate_half, down_half = call(
        pack_third,
        "pack_third",
        [
            ((own_rows, 2 * hidden_units), BF16),
            ((own_rows // 2, 2 * hidden_units), BF16),
            ((down_w.shape[0] // 2, width), BF16),
        ],
        [
            ((own_rows, 2 * hidden_units), BF16),
            (down_w.shape, BF16),
            pltpu.SemaphoreType.DMA((3,)),
            pltpu.SemaphoreType.DMA((3,)),
        ],
        [third_ids, gate_w, up_w, down_w],
        0,
        place=hbm,
    )
    (cot_own,) = all_after((cotangent[0],), (gate_pack,))
    first_far = hop(first_pack, "fsdp", 2)
    aux_far = hop(aux, "fsdp", 2)
    out_far, cross_far, states_far = (hop(a, "fsdp", 2) for a in (out_half, cross_half, states_own))
    gate_far, down_far, cot_far = (hop(a, "fsdp", 2) for a in (gate_half, down_half, cot_own))
    first_far, aux_far = all_after((first_far, aux_far), (gate_pack,))
    first_packs, aux_ws = beside(first_pack, first_far), beside(aux, aux_far)

    x, normed_one, q, kv, probs_a, probs_b, mixed, aux = call(
        self_forward,
        "self_forward",
        [
            ((length, width), BF16),
            ((length, width), BF16),
            ((mine, inner), BF16),
            ((length, 2 * inner), BF16),
            ((PAIRS, 2 * BLOCK, 2 * BLOCK), BF16),
            ((PAIRS, 2 * BLOCK, length), BF16),
            ((mine, inner), BF16),
            ((16, width), F32),
        ],
        [
            ((width, 3 * inner), BF16),
            ((PAIRS, 2 * BLOCK, 3 * BLOCK), F32),
            ((PAIRS, 2 * BLOCK, length), F32),
        ],
        [ids, *first_packs, *aux_ws],
        2 * 10**9,
    )
    out_far, cross_far, states_far, gate_far = all_after((out_far, cross_far, states_far, gate_far), (aux,))
    out_other, cross_other, gate_other = (hop(a, "rep", 1) for a in (out_far, cross_far, gate_far))
    outs_ws = beside_split(out_pack, out_far, out_other)
    cross_ws = beside_split(cross_pack, cross_far, cross_other)
    states_all = beside(states[0], states_far)
    hidden_one, normed_two, cross_q, cross_kv, cross_probs, cross_mixed, hidden_two, normed_three = call(
        cross_forward,
        "cross_forward",
        [
            ((mine, width), F32),
            ((mine, width), BF16),
            ((mine, inner), BF16),
            ((enc_all, 2 * inner), BF16),
            ((PAIRS, 2 * mine, enc_all), BF16),
            ((mine, inner), BF16),
            ((mine, width), F32),
            ((mine, width), BF16),
        ],
        [
            ((width, 3 * inner), BF16),
            ((2 * inner, width), BF16),
            ((enc_all, width), BF16),
        ],
        [ids, x, mixed, aux, *cross_ws, *outs_ws, *states_all],
        2 * 10**9,
    )
    gate_far, gate_other, down_far, cot_far = all_after((gate_far, gate_other, down_far, cot_far), (normed_three,))
    down_other = hop(down_far, "rep", 1)
    gates = beside_split(gate_pack, gate_far, gate_other)
    downs = beside_split(down_w, down_far, down_other)
    cots = beside(cotangent[0], cot_far)
    down_columns = down_w.size // own_rows
    result, grad_hidden_two, ff_keep, ff_send, mlp_gain_sum = call(
        feed_forward,
        "feed_forward",
        [
            ((rows, width), BF16),
            ((mine, width), F32),
            ((own_rows, 2 * hidden_units + down_columns), BF16),
            ((own_rows, 2 * hidden_units + down_columns), BF16),
            ((8, width), F32),
        ],
        [
            ((width, 2 * hidden_units), BF16),
            ((hidden_units, width), BF16),
            ((length, width), BF16),
            ((mine, width), BF16),
            ((mine, hidden_units), BF16),
            ((mine, hidden_units), BF16),
            ((mine, hidden_units), BF16),
            ((2 * own_rows, 2 * hidden_units), BF16),
            ((2 * own_rows, down_columns), BF16),
        ],
        [ids, hidden_two, normed_three, aux, *gates, *downs, *cots],
        4 * 10**9,
    )
    ff_sum = Sum("feed", ff_keep, ff_send, steps)
    grad_hidden_one, grad_mixed, states_keep, states_send, cross_keep, cross_send, cross_gain_sum = call(
        cross_backward,
        "cross_backward",
        [
            ((mine, width), F32),
            ((mine, inner), BF16),
            ((enc, width), F32),
            ((enc, width), F32),
            ((own_rows, 5 * inner), BF16),
            ((own_rows, 5 * inner), BF16),
            ((8, width), F32),
        ],
        [
            ((width, 3 * inner), BF16),
            ((2 * inner, width), BF16),
            ((enc_all, width), BF16),
            ((mine, width), BF16),
            ((mine, inner), BF16),
            ((enc_all, 2 * inner), BF16),
            ((2 * own_rows, 5 * inner), BF16),
            ((2 * enc, width), F32),
        ],
        [
            ids, grad_hidden_two, hidden_one, normed_two, cross_q, cross_kv, cross_probs, cross_mixed, mixed,
            aux, *cross_ws, *outs_ws, *states_all,
        ],
        2 * 10**9,
    )
    cross_sum = Sum("cross", cross_keep, cross_send, steps)
    done = ff_sum.fold((grad_hidden_one,))
    done = cross_sum.fold((done,))
    (grad_hidden_one,) = all_after((grad_hidden_one,), (done,))
    tokens_keep, tokens_send, self_keep, self_send = call(
        self_backward,
        "self_backward",
        [
            ((rows, width), F32),
            ((rows, width), F32),
            ((own_rows, 3 * inner + BLOCK), BF16),
            ((own_rows, 3 * inner + BLOCK), BF16),
        ],
        [
            ((width, 3 * inner), BF16),
            ((mine, inner), BF16),
            ((length, 2 * inner), BF16),
            ((2 * BLOCK, 3 * BLOCK), F32),
            ((2 * BLOCK, length), F32),
            ((2 * own_rows, 3 * inner), BF16),
            ((2 * own_rows, BLOCK), BF16),
            ((16, width), F32),
            ((BLOCK, BLOCK), F32),
        ],
        [
            ids, grad_hidden_one, grad_mixed, x, normed_one, q, kv, probs_a, probs_b, aux,
            cross_gain_sum, mlp_gain_sum, *first_packs,
        ],
        3 * 10**9,
    )
    self_sum = Sum("self", self_keep, self_send, steps)
    grad_states = states_keep + hop(states_send, "fsdp", 1)
    grad_tokens = tokens_keep + hop(tokens_send, "fsdp", 1)

    done = ff_sum.fold((tokens_keep,))
    order_of_sums = (self_sum, cross_sum, ff_sum)
    for _ in range(len(steps) - 1):
        for part in order_of_sums:
            done = part.fold((done,))
    for part in (self_sum, cross_sum):
        done = part.fold((done,))
    widenings = len(ff_sum.back) - 1
    done = ff_sum.widen((done,)) if widenings else done
    done = self_sum.fold((done,))
    for i in range(widenings):
        done = cross_sum.widen((done,))
        if i + 1 < widenings:
            done = ff_sum.widen((done,))
        done = self_sum.widen((done,))
    grad_gate, grad_up, grad_down = call(
        unpack_feed,
        "unpack_feed",
        [(gate_w.shape, F32), (up_w.shape, F32), (down_w.shape, F32)],
        [],
        [ids, *ff_sum.halves((done,))],
        0,
    )
    grad_cross_query, grad_cross_key, grad_cross_value, grad_cross_out, grad_out = call(
        unpack_cross,
        "unpack_cross",
        [(query_w.shape, F32)] * 3 + [(out_w.shape, F32)] * 2,
        [],
        [ids, *cross_sum.halves((grad_gate,))],
        0,
    )
    grad_query, grad_key, grad_value, grad_g1, grad_g2, grad_g3, grad_table = call(
        unpack_self,
        "unpack_self",
        [(query_w.shape, F32)] * 3 + [((1, own_rows), F32)] * 3 + [(bias_table.shape, F32)],
        [((own_rows, BLOCK), F32)],
        [ids, *self_sum.halves((grad_cross_query,))],
        0,
    )
    return (
        result[None],
        grad_tokens[None],
        grad_states[None],
        grad_query,
        grad_key,
        grad_value,
        grad_out,
        grad_cross_query,
        grad_cross_key,
        grad_cross_value,
        grad_cross_out,
        grad_gate,
        grad_up,
        grad_down,
        grad_g1[0],
        grad_g2[0],
        grad_g3[0],
        grad_table,
    )


def solution(mesh):
    whole = P("rep", "fsdp", None)
    rows, columns, vector = P("fsdp", None), P(None, "fsdp"), P("fsdp")
    weights = (rows, rows, rows, columns, rows, rows, rows, columns, rows, rows, rows)
    small = (vector, vector, vector, rows)
    return jax.shard_map(
        per_device,
        mesh=mesh,
        in_specs=(whole, whole) + weights + small + (whole,),
        out_specs=(whole, whole, whole) + weights + small,
        check_vma=False,
    )
```

time: 211 us -> 128 us (0.61)
  starting transfers between devices: 76.7 us -> 41.3 us
  waiting for transfers between devices: 68.1 us -> 45.5 us
  local copies, waits for them, and re-layouts: 14 us -> 2.26 us
  Pallas kernels: 45.1 us -> 35.8 us
  other arithmetic: 5.49 us -> 2.01 us
    ppermute x63 -> x55, starting transfers between devices: 76.7 us -> 41.3 us  [hop(): return lax.ppermute(x, axis, [(i, i ^ bits) for i in range(size)])]
    ppermute x63 -> x55, waiting for transfers between devices: 68.1 us -> 45.5 us  [hop(): return lax.ppermute(x, axis, [(i, i ^ bits) for i in range(size)])]
    pallas_call x5 -> x23, Pallas kernels: 45.1 us -> 35.8 us  [call(): pl.pallas_call(kernel, name=name, out_shape=[jax.ShapeDtypeStruct(s, d) f...]
    unnamed x66 -> x33, local copies, waits for them, and re-layouts: 7.28 us -> 1.55 us
    squeeze x4 -> x0, local copies, waits for them, and re-layouts: 2.56 us -> none  [the longest x3 2.04 us: sum_over_rep(): lax.dynamic_index_in_dim(pieces, digit ^ k, 0, keepdims=False)]
    concatenate x4 -> x0, other arithmetic: 2.54 us -> none  [the longest x1 0.92 us: per_device(): token_pack = jnp.concatenate([tokens[0], aux], axis=0)]
    slice x6 -> x0, local copies, waits for them, and re-layouts: 2.16 us -> none  [the longest x1 1.08 us: per_device(): ff_sum[:, hidden_units:2 * hidden_units]]
  transfers between devices with their start and end apart: 63 -> 55, of which waited for: 19 -> 27; matrix products, arithmetic and copies ran while one was open for 5% -> 2% of each run, Pallas kernels for 13% -> 22%
where the time goes in v2:
time: 128 us
  waiting for transfers between devices  45.5 us (36%)
  starting transfers between devices  41.3 us (32%)
  Pallas kernels  35.8 us (28%)
  local copies, waits for them, and re-layouts  2.26 us (2%)
  other arithmetic  2.01 us (2%)
    ppermute x55, waiting for transfers between devices, hop(): return lax.ppermute(x, axis, [(i, i ^ bits) for i in range(size)])  45.5 us
    ppermute x55, starting transfers between devices, hop(): return lax.ppermute(x, axis, [(i, i ^ bits) for i in range(size)])  41.3 us
    pallas_call x23, Pallas kernels, call(): pl.pallas_call(kernel, name=name, out_shape=[jax.ShapeDtypeStruct(s, d) f...  35.8 us
  transfers between devices with their start and end apart: 55, of which 27 were waited for; matrix products, arithmetic and copies ran while one was open for 2% of the time, Pallas kernels for 22%

profile of v2, /device:TPU:0, one launch (start us, length us, event | category | flops | bytes accessed | tf_op | source)
XLA Modules:
  0.0 127.8 jit_solution(12651299877160497859)
XLA Ops:
  0.7 1.9 %pack_first.1.w0 = bf16[128,1664]{1,0:T(8,128)(2,1)} custom-call(bf16[128,512]{1,0:T(8,128)(2,1)} %bitcast.25, bf16[128,384]{1,0:T(8,128)(2,1)} %q_ref.1, bf16[128,384]{1,0:T(8,128)(2,1)} %k_ref.1, bf16[128,384]{1,0:T(8,128)(2,1)} %v_ref.1), custom_call_target="tpu_custom_call" | custom-call | bytes 425984 | tf_op jit(solution)/shard_map/pack_first/pallas_call | solution.py:550
  2.5 3.0 %collective-permute-start.1 = (bf16[128,1664]{1,0:T(8,128)(2,1)}, bf16[128,1664]{1,0:T(8,128)(2,1)S(1)}, u32[]{:S(2)}, u32[]{:S(2)}) collective-permute-start(bf16[128,1664]{1,0:T(8,128)(2,1)} %pack_first.1.w0), channel_id=1, source_target_pairs={{0,2},{1,3},{2,0},{3,1},{4,6},{5,7},{6,4},{7,5},{8,10},{9,11},{10,... | collective-permute-start | bytes 1277960 | tf_op jit(solution)/shard_map/ppermute | solution.py:564
  8.6 2.8 %pack_second.1 = (bf16[128,1152]{1,0:T(8,128)(2,1)}, bf16[768,128]{1,0:T(8,128)(2,1)}, bf16[64,1152]{1,0:T(8,128)(2,1)}, bf16[384,128]{1,0:T(8,128)(2,1)}) custom-call(s32[3]{0:T(128)} %pad_add_fusion.ids_ref, bf16[128,384]{1,0:T(8,128)(2,1)} %cq_ref.1, bf16[128,384]{1,0:T(8,128)(2,1)} %ck_ref.1, bf16[128,384]{1,0:T(8,128)(2,1)} %cv_ref.1, ...), custom_call_target="tpu_custom_call" | custom-call | bytes 491532 | tf_op jit(solution)/shard_map/pack_second/pallas_call | solution.py:550
  11.5 2.9 %pack_third.1 = (bf16[128,2048]{1,0:T(8,128)(2,1)}, bf16[64,2048]{1,0:T(8,128)(2,1)}, bf16[128,512]{1,0:T(8,128)(2,1)}) custom-call(s32[3]{0:T(128)} %pad_add_fusion.ids_ref, bf16[128,1024]{1,0:T(8,128)(2,1)} %gate_ref.1, bf16[128,1024]{1,0:T(8,128)(2,1)} %up_ref.1, bf16[256,512]{1,0:T(8,128)(2,1)} %d0.1), custom_call_target="tpu_custom_call" | custom-call | bytes 786444 | tf_op jit(solution)/shard_map/pack_third/pallas_call | solution.py:550
  14.4 1.5 %collective-permute-done.2.a2 = bf16[16,512]{1,0:T(8,128)(2,1)S(1)} collective-permute-done((bf16[16,512]{1,0:T(8,128)(2,1)S(1)}, bf16[16,512]{1,0:T(8,128)(2,1)S(1)}, u32[]{:S(2)}, u32[]{:S(2)}) %collective-permute-start.2) | collective-permute-done | bytes 16416 | tf_op jit(solution)/shard_map/ppermute | solution.py:564
  15.9 1.7 %collective-permute-start.7 = (bf16[384,128]{1,0:T(8,128)(2,1)}, bf16[384,128]{1,0:T(8,128)(2,1)S(1)}, u32[]{:S(2)}, u32[]{:S(2)}) collective-permute-start(bf16[384,128]{1,0:T(8,128)(2,1)} %get-tuple-element.158), channel_id=1, source_target_pairs={{0,2},{1,3},{2,0},{3,1},{4,6},{5,7},{6,4},{7,5},{8,10},{9,11},{10,... | collective-permute-start | bytes 294920 | tf_op jit(solution)/shard_map/ppermute | solution.py:564
  19.9 3.2 %collective-permute-done.9.s2 = bf16[64,512]{1,0:T(8,128)(2,1)S(1)} collective-permute-done((bf16[64,512]{1,0:T(8,128)(2,1)S(1)}, bf16[64,512]{1,0:T(8,128)(2,1)S(1)}, u32[]{:S(2)}, u32[]{:S(2)}) %collective-permute-start.9) | collective-permute-done | bytes 65568 | tf_op jit(solution)/shard_map/ppermute | solution.py:564
  23.6 1.7 %collective-permute-start.8 = (bf16[64,1152]{1,0:T(8,128)(2,1)}, bf16[64,1152]{1,0:T(8,128)(2,1)S(1)}, u32[]{:S(2)}, u32[]{:S(2)}) collective-permute-start(bf16[64,1152]{1,0:T(8,128)(2,1)} %get-tuple-element.159), channel_id=1, source_target_pairs={{0,2},{1,3},{2,0},{3,1},{4,6},{5,7},{6,4},{7,5},{8,10},{9,11},{10,... | collective-permute-start | bytes 442376 | tf_op jit(solution)/shard_map/ppermute | solution.py:564
  26.3 4.2 %self_forward.1 = (bf16[512,512]{1,0:T(8,128)(2,1)S(1)}, bf16[512,512]{1,0:T(8,128)(2,1)S(1)}, bf16[256,384]{1,0:T(8,128)(2,1)S(1)}, bf16[512,768]{1,0:T(8,128)(...) custom-call(s32[3]{0:T(128)S(1)} %copy-done.2, ...), custom_call_target="tpu_custom_call" | custom-call | flops 2000000000 | bytes 1769484 | tf_op jit(solution)/shard_map/self_forward/pallas_call | solution.py:550
  31.9 1.8 %collective-permute-start.11 = (bf16[64,1152]{1,0:T(8,128)(2,1)S(1)}, bf16[64,1152]{1,0:T(8,128)(2,1)S(1)}, u32[]{:S(2)}, u32[]{:S(2)}) collective-permute-start(bf16[64,1152]{1,0:T(8,128)(2,1)S(1)} %collective-permute-done.8.w2), channel_id=1, source_target_pairs={{0,4},{4,0},{8,12},{12,8},{16,20},{20,16},{24,28},{28,24},{1,5},{5... | collective-permute-start | bytes 442376 | tf_op jit(solution)/shard_map/ppermute | solution.py:564
  37.0 3.3 %collective-permute-done.15.o3 = bf16[384,128]{1,0:T(8,128)(2,1)S(1)} collective-permute-done((bf16[384,128]{1,0:T(8,128)(2,1)S(1)}, bf16[384,128]{1,0:T(8,128)(2,1)S(1)}, u32[]{:S(2)}, u32[]{:S(2)}) %collective-permute-start.15) | collective-permute-done | bytes 98336 | tf_op jit(solution)/shard_map/ppermute | solution.py:564
  43.3 2.9 %cross_forward.1 = (f32[256,512]{1,0:T(8,128)S(1)}, bf16[256,512]{1,0:T(8,128)(2,1)S(1)}, bf16[256,384]{1,0:T(8,128)(2,1)S(1)}, bf16[256,768]{1,0:T(8,128)(2,1)S...) custom-call(s32[3]{0:T(128)S(1)} %copy-done.2, ...), custom_call_target="tpu_custom_call" | custom-call | flops 2000000000 | bytes 2981900 | tf_op jit(solution)/shard_map/cross_forward/pallas_call | solution.py:550
  47.5 1.5 %collective-permute-done.21.g3 = bf16[64,2048]{1,0:T(8,128)(2,1)S(1)} collective-permute-done((bf16[64,2048]{1,0:T(8,128)(2,1)S(1)}, bf16[64,2048]{1,0:T(8,128)(2,1)S(1)}, u32[]{:S(2)}, u32[]{:S(2)}) %collective-permute-start.21) | collective-permute-done | bytes 262176 | tf_op jit(solution)/shard_map/ppermute | solution.py:564
  51.1 3.1 %collective-permute-done.27.d3 = bf16[128,512]{1,0:T(8,128)(2,1)S(1)} collective-permute-done((bf16[128,512]{1,0:T(8,128)(2,1)S(1)}, bf16[128,512]{1,0:T(8,128)(2,1)S(1)}, u32[]{:S(2)}, u32[]{:S(2)}) %collective-permute-start.27) | collective-permute-done | bytes 131104 | tf_op jit(solution)/shard_map/ppermute | solution.py:564
  55.5 3.9 %feed_forward.1 = (bf16[128,512]{1,0:T(8,128)(2,1)}, f32[256,512]{1,0:T(8,128)S(1)}, bf16[128,3072]{1,0:T(8,128)(2,1)S(1)}, bf16[128,3072]{1,0:T(8,128)(2,1)S(1)}, f32[8,512]{1,0:T(8,128)S(1)}) custom-call(s32[3]{0:T(128)S(1)} %copy-done.2, f32[256,512]{1,0:T(8,128)S(1)} %get-tuple-element.166.h2_ref, bf16[256,512]{1,0:T(8,128)(2,1)S(1)} %get-tuple-element.167.n3_ref, ...), custom_call_target="tpu_custom_call" | custom-call | flops 4000000000 | bytes 4489228 | tf_op jit(solution)/shard_map/feed_forward/pallas_call | solution.py:550
  59.6 3.7 %cross_backward.1 = (f32[256,512]{1,0:T(8,128)S(1)}, bf16[256,384]{1,0:T(8,128)(2,1)S(1)}, f32[64,512]{1,0:T(8,128)S(1)}, f32[64,512]{1,0:T(8,128)S(1)}, bf16[12...) custom-call(s32[3]{0:T(128)S(1)} %copy-done.2, ...), custom_call_target="tpu_custom_call" | custom-call | flops 2000000000 | bytes 5341196 | tf_op jit(solution)/shard_map/cross_backward/pallas_call | solution.py:550
  66.4 8.1 %self_backward.1 = (f32[128,512]{1,0:T(8,128)S(1)}, f32[128,512]{1,0:T(8,128)S(1)}, bf16[128,1280]{1,0:T(8,128)(2,1)S(1)}, bf16[128,1280]{1,0:T(8,128)(2,1)S(1)}) custom-call(s32[3]{0:T(128)S(1)} %copy-done.2, f32[256,512]{1,0:T(8,128)S(1)} %get-tuple-element.194.grad_h1_ref, bf16[256,384]{1,0:T(8,128)(2,1)S(1)} %get-tuple-element.195.mix_ref, ...), custom_call_target="tpu_custom_call" | custom-call | flops 3000000000 | bytes 5701644 | tf_op jit(solution)/shard_map/self_backward/pallas_call | solution.py:550
  76.9 1.6 %collective-permute-start.39 = (bf16[32,3072]{1,0:T(8,128)(2,1)S(1)}, bf16[32,3072]{1,0:T(8,128)(2,1)S(1)}, u32[]{:S(2)}, u32[]{:S(2)}) collective-permute-start(bf16[32,3072]{1,0:T(8,128)(2,1)S(1)} %get-tuple-element.217), channel_id=1, source_target_pairs={{0,8},{4,12},{8,0},{12,4},{16,24},{20,28},{24,16},{28,20},{1,9},{5... | collective-permute-start | bytes 589832 | tf_op jit(solution)/shard_map/ppermute | solution.py:564
  79.7 3.7 %collective-permute-done.40.arrived_ref = bf16[64,1920]{1,0:T(8,128)(2,1)S(1)} collective-permute-done((bf16[64,1920]{1,0:T(8,128)(2,1)S(1)}, bf16[64,1920]{1,0:T(8,128)(2,1)S(1)}, u32[]{:S(2)}, u32[]{:S(2)}) %collective-permute-start.40) | collective-permute-done | bytes 245792 | tf_op jit(solution)/shard_map/ppermute | solution.py:564
  83.5 1.6 %collective-permute-start.43 = (bf16[32,1920]{1,0:T(8,128)(2,1)S(1)}, bf16[32,1920]{1,0:T(8,128)(2,1)S(1)}, u32[]{:S(2)}, u32[]{:S(2)}) collective-permute-start(bf16[32,1920]{1,0:T(8,128)(2,1)S(1)} %get-tuple-element.230), channel_id=1, source_target_pairs={{0,8},{4,12},{8,0},{12,4},{16,24},{20,28},{24,16},{28,20},{1,9},{5... | collective-permute-start | bytes 368648 | tf_op jit(solution)/shard_map/ppermute | solution.py:564
  85.2 2.7 %collective-permute-start.42 = (bf16[16,3072]{1,0:T(8,128)(2,1)S(1)}, bf16[16,3072]{1,0:T(8,128)(2,1)S(1)}, u32[]{:S(2)}, u32[]{:S(2)}) collective-permute-start(bf16[16,3072]{1,0:T(8,128)(2,1)S(1)} %get-tuple-element.229), channel_id=1, source_target_pairs={{0,16},{4,20},{8,24},{12,28},{16,0},{20,4},{24,8},{28,12},{1,17},{... | collective-permute-start | bytes 294920 | tf_op jit(solution)/shard_map/ppermute | solution.py:564
  87.9 1.6 %collective-permute-done.43.arrived_ref = bf16[32,1920]{1,0:T(8,128)(2,1)S(1)} collective-permute-done((bf16[32,1920]{1,0:T(8,128)(2,1)S(1)}, bf16[32,1920]{1,0:T(8,128)(2,1)S(1)}, u32[]{:S(2)}, u32[]{:S(2)}) %collective-permute-start.43) | collective-permute-done | bytes 122912 | tf_op jit(solution)/shard_map/ppermute | solution.py:564
  89.5 2.2 %collective-permute-start.46 = (bf16[16,1920]{1,0:T(8,128)(2,1)S(1)}, bf16[16,1920]{1,0:T(8,128)(2,1)S(1)}, u32[]{:S(2)}, u32[]{:S(2)}) collective-permute-start(bf16[16,1920]{1,0:T(8,128)(2,1)S(1)} %get-tuple-element.240), channel_id=1, source_target_pairs={{0,16},{4,20},{8,24},{12,28},{16,0},{20,4},{24,8},{28,12},{1,17},{... | collective-permute-start | bytes 184328 | tf_op jit(solution)/shard_map/ppermute | solution.py:564
  91.7 1.8 %collective-permute-start.41 = (bf16[32,1280]{1,0:T(8,128)(2,1)S(1)}, bf16[32,1280]{1,0:T(8,128)(2,1)S(1)}, u32[]{:S(2)}, u32[]{:S(2)}) collective-permute-start(bf16[32,1280]{1,0:T(8,128)(2,1)S(1)} %get-tuple-element.228), channel_id=1, source_target_pairs={{0,8},{4,12},{8,0},{12,4},{16,24},{20,28},{24,16},{28,20},{1,9},{5... | collective-permute-start | bytes 245768 | tf_op jit(solution)/shard_map/ppermute | solution.py:564
  97.8 1.7 %collective-permute-start.49 = (bf16[16,1920]{1,0:T(8,128)(2,1)S(1)}, bf16[16,1920]{1,0:T(8,128)(2,1)S(1)}, u32[]{:S(2)}, u32[]{:S(2)}) collective-permute-start(bf16[16,1920]{1,0:T(8,128)(2,1)S(1)} %cross_fold.7), channel_id=1, source_target_pairs={{0,16},{4,20},{8,24},{12,28},{16,0},{20,4},{24,8},{28,12},{1,17},{... | collective-permute-start | bytes 184328 | tf_op jit(solution)/shard_map/ppermute | solution.py:564
  101.1 2.2 %collective-permute-done.44.arrived_ref = bf16[16,1280]{1,0:T(8,128)(2,1)S(1)} collective-permute-done((bf16[16,1280]{1,0:T(8,128)(2,1)S(1)}, bf16[16,1280]{1,0:T(8,128)(2,1)S(1)}, u32[]{:S(2)}, u32[]{:S(2)}) %collective-permute-start.44) | collective-permute-done | bytes 40992 | tf_op jit(solution)/shard_map/ppermute | solution.py:564
  106.1 3.0 %collective-permute-done.48 = bf16[32,3072]{1,0:T(8,128)(2,1)S(1)} collective-permute-done((bf16[32,3072]{1,0:T(8,128)(2,1)S(1)}, bf16[32,3072]{1,0:T(8,128)(2,1)S(1)}, u32[]{:S(2)}, u32[]{:S(2)}) %collective-permute-start.48) | collective-permute-done | bytes 196640 | tf_op jit(solution)/shard_map/ppermute | solution.py:564
  112.4 2.4 %collective-permute-done.50 = bf16[32,1280]{1,0:T(8,128)(2,1)S(1)} collective-permute-done((bf16[32,1280]{1,0:T(8,128)(2,1)S(1)}, bf16[32,1280]{1,0:T(8,128)(2,1)S(1)}, u32[]{:S(2)}, u32[]{:S(2)}) %collective-permute-start.50) | collective-permute-done | bytes 81952 | tf_op jit(solution)/shard_map/ppermute | solution.py:564
  116.6 4.7 %collective-permute-done.54.high_ref = bf16[64,3072]{1,0:T(8,128)(2,1)S(1)} collective-permute-done((bf16[64,3072]{1,0:T(8,128)(2,1)S(1)}, bf16[64,3072]{1,0:T(8,128)(2,1)S(1)}, u32[]{:S(2)}, u32[]{:S(2)}) %collective-permute-start.54) | collective-permute-done | bytes 393248 | tf_op jit(solution)/shard_map/ppermute | solution.py:564
  121.3 1.8 %unpack_feed.1 = (f32[128,1024]{1,0:T(8,128)}, f32[128,1024]{1,0:T(8,128)}, f32[256,512]{1,0:T(8,128)}) custom-call(s32[3]{0:T(128)S(1)} %copy-done.2, bf16[64,3072]{1,0:T(8,128)(2,1)S(1)} %constant_dynamic-update-slice_fusion.4.low_ref, bf16[64,3072]{1,0:T(8,128)(2,1)S(1)} %collective-permute-done.54.high_ref), custom_call_target="tpu_custom_call" | custom-call | bytes 786444 | tf_op jit(solution)/shard_map/unpack_feed/pallas_call | solution.py:550
  123.1 1.5 %collective-permute-done.53.high_ref = bf16[64,1920]{1,0:T(8,128)(2,1)S(1)} collective-permute-done((bf16[64,1920]{1,0:T(8,128)(2,1)S(1)}, bf16[64,1920]{1,0:T(8,128)(2,1)S(1)}, u32[]{:S(2)}, u32[]{:S(2)}) %collective-permute-start.53) | collective-permute-done | bytes 245792 | tf_op jit(solution)/shard_map/ppermute | solution.py:564
  124.6 1.5 %unpack_cross.1 = (f32[128,384]{1,0:T(8,128)}, f32[128,384]{1,0:T(8,128)}, f32[128,384]{1,0:T(8,128)}, f32[384,128]{1,0:T(8,128)}, f32[384,128]{1,0:T(8,128)}) custom-call(s32[3]{0:T(128)S(1)} %copy-done.2, bf16[64,1920]{1,0:T(8,128)(2,1)S(1)} %constant_dynamic-update-slice_fusion.8.low_ref, bf16[64,1920]{1,0:T(8,128)(2,1)S(1)} %collective-permute-done.53.high_ref), custom_call_target="tpu_custom_call" | custom-call | bytes 491532 | tf_op jit(solution)/shard_map/unpack_cross/pallas_call | solution.py:550
  (147 shorter events, 41.6 us)
Async XLA Ops:
  2.5 13.4 %collective-permute-start.1 = (bf16[128,1664]{1,0:T(8,128)(2,1)}, bf16[128,1664]{1,0:T(8,128)(2,1)S(1)}, u32[]{:S(2)}, u32[]{:S(2)}) collective-permute-start(bf16[128,1664]{1,0:T(8,128)(2,1)} %pack_first.1.w0), channel_id=1, source_target_pairs={{0,2},{1,3},{2,0},{3,1},{4,6},{5,7},{6,4},{7,5},{8,10},{9,11},{10,... | collective-permute-start | bytes 1277960 | tf_op jit(solution)/shard_map/ppermute | solution.py:564
  5.5 18.1 %collective-permute-start = (bf16[128,1664]{1,0:T(8,128)(2,1)}, bf16[128,1664]{1,0:T(8,128)(2,1)S(1)}, u32[]{:S(2)}, u32[]{:S(2)}) collective-permute-start(bf16[128,1664]{1,0:T(8,128)(2,1)} %pack_first.1.w0), channel_id=1, source_target_pairs={{0,1},{1,0},{2,3},{3,2},{4,5},{5,4},{6,7},{7,6},{8,9},{9,8},{10,11... | collective-permute-start | bytes 1277960 | tf_op jit(solution)/shard_map/ppermute | solution.py:564
  7.7 8.2 %collective-permute-start.2 = (bf16[16,512]{1,0:T(8,128)(2,1)S(1)}, bf16[16,512]{1,0:T(8,128)(2,1)S(1)}, u32[]{:S(2)}, u32[]{:S(2)}) collective-permute-start(bf16[16,512]{1,0:T(8,128)(2,1)S(1)} %dynamic_update_slice.7.a0), channel_id=1, source_target_pairs={{0,2},{1,3},{2,0},{3,1},{4,6},{5,7},{6,4},{7,5},{8,10},{9,11},{10,... | collective-permute-start | bytes 49160 | tf_op jit(solution)/shard_map/ppermute | solution.py:564
  15.9 9.6 %collective-permute-start.3 = (bf16[128,1664]{1,0:T(8,128)(2,1)S(1)}, bf16[128,1664]{1,0:T(8,128)(2,1)S(1)}, u32[]{:S(2)}, u32[]{:S(2)}) collective-permute-start(bf16[128,1664]{1,0:T(8,128)(2,1)S(1)} %collective-permute-done.1.w2), channel_id=1, source_target_pairs={{0,1},{1,0},{2,3},{3,2},{4,5},{5,4},{6,7},{7,6},{8,9},{9,8},{10,11... | collective-permute-start | bytes 1277960 | tf_op jit(solution)/shard_map/ppermute | solution.py:564
  15.9 7.2 %collective-permute-start.7 = (bf16[384,128]{1,0:T(8,128)(2,1)}, bf16[384,128]{1,0:T(8,128)(2,1)S(1)}, u32[]{:S(2)}, u32[]{:S(2)}) collective-permute-start(bf16[384,128]{1,0:T(8,128)(2,1)} %get-tuple-element.158), channel_id=1, source_target_pairs={{0,2},{1,3},{2,0},{3,1},{4,6},{5,7},{6,4},{7,5},{8,10},{9,11},{10,... | collective-permute-start | bytes 294920 | tf_op jit(solution)/shard_map/ppermute | solution.py:564
  18.8 13.1 %collective-permute-start.10 = (bf16[64,2048]{1,0:T(8,128)(2,1)}, bf16[64,2048]{1,0:T(8,128)(2,1)S(1)}, u32[]{:S(2)}, u32[]{:S(2)}) collective-permute-start(bf16[64,2048]{1,0:T(8,128)(2,1)} %get-tuple-element.161), channel_id=1, source_target_pairs={{0,2},{1,3},{2,0},{3,1},{4,6},{5,7},{6,4},{7,5},{8,10},{9,11},{10,... | collective-permute-start | bytes 786440 | tf_op jit(solution)/shard_map/ppermute | solution.py:564
  23.1 13.0 %collective-permute-start.6 = (bf16[128,1152]{1,0:T(8,128)(2,1)S(1)}, bf16[128,1152]{1,0:T(8,128)(2,1)S(1)}, u32[]{:S(2)}, u32[]{:S(2)}) collective-permute-start(bf16[128,1152]{1,0:T(8,128)(2,1)S(1)} %copy-done.4), channel_id=1, source_target_pairs={{0,1},{1,0},{2,3},{3,2},{4,5},{5,4},{6,7},{7,6},{8,9},{9,8},{10,11... | collective-permute-start | bytes 884744 | tf_op jit(solution)/shard_map/ppermute | solution.py:564
  23.6 8.3 %collective-permute-start.8 = (bf16[64,1152]{1,0:T(8,128)(2,1)}, bf16[64,1152]{1,0:T(8,128)(2,1)S(1)}, u32[]{:S(2)}, u32[]{:S(2)}) collective-permute-start(bf16[64,1152]{1,0:T(8,128)(2,1)} %get-tuple-element.159), channel_id=1, source_target_pairs={{0,2},{1,3},{2,0},{3,1},{4,6},{5,7},{6,4},{7,5},{8,10},{9,11},{10,... | collective-permute-start | bytes 442376 | tf_op jit(solution)/shard_map/ppermute | solution.py:564
  25.4 10.0 %collective-permute-start.14 = (bf16[768,128]{1,0:T(8,128)(2,1)}, bf16[768,128]{1,0:T(8,128)(2,1)S(1)}, u32[]{:S(2)}, u32[]{:S(2)}) collective-permute-start(bf16[768,128]{1,0:T(8,128)(2,1)} %get-tuple-element.163.o0), channel_id=1, source_target_pairs={{0,1},{1,0},{2,3},{3,2},{4,5},{5,4},{6,7},{7,6},{8,9},{9,8},{10,11... | collective-permute-start | bytes 589832 | tf_op jit(solution)/shard_map/ppermute | solution.py:564
  25.5 9.6 %collective-permute-start.23 = (bf16[128,512]{1,0:T(8,128)(2,1)S(1)}, bf16[128,512]{1,0:T(8,128)(2,1)S(1)}, u32[]{:S(2)}, u32[]{:S(2)}) collective-permute-start(bf16[128,512]{1,0:T(8,128)(2,1)S(1)} %bitcast.18), channel_id=1, source_target_pairs={{0,2},{1,3},{2,0},{3,1},{4,6},{5,7},{6,4},{7,5},{8,10},{9,11},{10,... | collective-permute-start | bytes 393224 | tf_op jit(solution)/shard_map/ppermute | solution.py:564
  35.1 15.5 %collective-permute-start.20 = (bf16[128,2048]{1,0:T(8,128)(2,1)S(1)}, bf16[128,2048]{1,0:T(8,128)(2,1)S(1)}, u32[]{:S(2)}, u32[]{:S(2)}) collective-permute-start(bf16[128,2048]{1,0:T(8,128)(2,1)S(1)} %copy-done.3), channel_id=1, source_target_pairs={{0,1},{1,0},{2,3},{3,2},{4,5},{5,4},{6,7},{7,6},{8,9},{9,8},{10,11... | collective-permute-start | bytes 1572872 | tf_op jit(solution)/shard_map/ppermute | solution.py:564
  40.3 8.7 %collective-permute-start.21 = (bf16[64,2048]{1,0:T(8,128)(2,1)S(1)}, bf16[64,2048]{1,0:T(8,128)(2,1)S(1)}, u32[]{:S(2)}, u32[]{:S(2)}) collective-permute-start(bf16[64,2048]{1,0:T(8,128)(2,1)S(1)} %collective-permute-done.10.g2), channel_id=1, source_target_pairs={{0,4},{4,0},{8,12},{12,8},{16,20},{20,16},{24,28},{28,24},{1,5},{5... | collective-permute-start | bytes 786440 | tf_op jit(solution)/shard_map/ppermute | solution.py:564
  41.3 8.7 %collective-permute-start.30 = (bf16[128,512]{1,0:T(8,128)(2,1)S(1)}, bf16[128,512]{1,0:T(8,128)(2,1)S(1)}, u32[]{:S(2)}, u32[]{:S(2)}) collective-permute-start(bf16[128,512]{1,0:T(8,128)(2,1)S(1)} %bitcast.19), channel_id=1, source_target_pairs={{0,1},{1,0},{2,3},{3,2},{4,5},{5,4},{6,7},{7,6},{8,9},{9,8},{10,11... | collective-permute-start | bytes 393224 | tf_op jit(solution)/shard_map/ppermute | solution.py:564
  41.6 8.9 %collective-permute-start.26 = (bf16[256,512]{1,0:T(8,128)(2,1)S(1)}, bf16[256,512]{1,0:T(8,128)(2,1)S(1)}, u32[]{:S(2)}, u32[]{:S(2)}) collective-permute-start(bf16[256,512]{1,0:T(8,128)(2,1)S(1)} %copy-done.1), channel_id=1, source_target_pairs={{0,1},{1,0},{2,3},{3,2},{4,5},{5,4},{6,7},{7,6},{8,9},{9,8},{10,11... | collective-permute-start | bytes 786440 | tf_op jit(solution)/shard_map/ppermute | solution.py:564
  65.3 11.4 %collective-permute-start.37 = (bf16[64,3072]{1,0:T(8,128)(2,1)S(1)}, bf16[64,3072]{1,0:T(8,128)(2,1)S(1)}, u32[]{:S(2)}, u32[]{:S(2)}) collective-permute-start(bf16[64,3072]{1,0:T(8,128)(2,1)S(1)} %get-tuple-element.209), channel_id=1, source_target_pairs={{0,4},{4,0},{8,12},{12,8},{16,20},{20,16},{24,28},{28,24},{1,5},{5... | collective-permute-start | bytes 1179656 | tf_op jit(solution)/shard_map/ppermute | solution.py:564
  74.6 8.8 %collective-permute-start.40 = (bf16[64,1920]{1,0:T(8,128)(2,1)S(1)}, bf16[64,1920]{1,0:T(8,128)(2,1)S(1)}, u32[]{:S(2)}, u32[]{:S(2)}) collective-permute-start(bf16[64,1920]{1,0:T(8,128)(2,1)S(1)} %get-tuple-element.218), channel_id=1, source_target_pairs={{0,4},{4,0},{8,12},{12,8},{16,20},{20,16},{24,28},{28,24},{1,5},{5... | collective-permute-start | bytes 737288 | tf_op jit(solution)/shard_map/ppermute | solution.py:564
  76.9 8.2 %collective-permute-start.39 = (bf16[32,3072]{1,0:T(8,128)(2,1)S(1)}, bf16[32,3072]{1,0:T(8,128)(2,1)S(1)}, u32[]{:S(2)}, u32[]{:S(2)}) collective-permute-start(bf16[32,3072]{1,0:T(8,128)(2,1)S(1)} %get-tuple-element.217), channel_id=1, source_target_pairs={{0,8},{4,12},{8,0},{12,4},{16,24},{20,28},{24,16},{28,20},{1,9},{5... | collective-permute-start | bytes 589832 | tf_op jit(solution)/shard_map/ppermute | solution.py:564
  78.6 9.2 %collective-permute-start.38 = (bf16[64,1280]{1,0:T(8,128)(2,1)S(1)}, bf16[64,1280]{1,0:T(8,128)(2,1)S(1)}, u32[]{:S(2)}, u32[]{:S(2)}) collective-permute-start(bf16[64,1280]{1,0:T(8,128)(2,1)S(1)} %get-tuple-element.216), channel_id=1, source_target_pairs={{0,4},{4,0},{8,12},{12,8},{16,20},{20,16},{24,28},{28,24},{1,5},{5... | collective-permute-start | bytes 491528 | tf_op jit(solution)/shard_map/ppermute | solution.py:564
  79.7 14.4 %collective-permute-start.35 = (f32[64,512]{1,0:T(8,128)S(1)}, f32[64,512]{1,0:T(8,128)S(1)}, u32[]{:S(2)}, u32[]{:S(2)}) collective-permute-start(f32[64,512]{1,0:T(8,128)S(1)} %get-tuple-element.206), channel_id=1, source_target_pairs={{0,1},{1,0},{2,3},{3,2},{4,5},{5,4},{6,7},{7,6},{8,9},{9,8},{10,11... | collective-permute-start | bytes 393224 | tf_op jit(solution)/shard_map/ppermute | solution.py:564
  83.5 6.0 %collective-permute-start.43 = (bf16[32,1920]{1,0:T(8,128)(2,1)S(1)}, bf16[32,1920]{1,0:T(8,128)(2,1)S(1)}, u32[]{:S(2)}, u32[]{:S(2)}) collective-permute-start(bf16[32,1920]{1,0:T(8,128)(2,1)S(1)} %get-tuple-element.230), channel_id=1, source_target_pairs={{0,8},{4,12},{8,0},{12,4},{16,24},{20,28},{24,16},{28,20},{1,9},{5... | collective-permute-start | bytes 368648 | tf_op jit(solution)/shard_map/ppermute | solution.py:564
  85.2 8.3 %collective-permute-start.42 = (bf16[16,3072]{1,0:T(8,128)(2,1)S(1)}, bf16[16,3072]{1,0:T(8,128)(2,1)S(1)}, u32[]{:S(2)}, u32[]{:S(2)}) collective-permute-start(bf16[16,3072]{1,0:T(8,128)(2,1)S(1)} %get-tuple-element.229), channel_id=1, source_target_pairs={{0,16},{4,20},{8,24},{12,28},{16,0},{20,4},{24,8},{28,12},{1,17},{... | collective-permute-start | bytes 294920 | tf_op jit(solution)/shard_map/ppermute | solution.py:564
  89.5 7.0 %collective-permute-start.46 = (bf16[16,1920]{1,0:T(8,128)(2,1)S(1)}, bf16[16,1920]{1,0:T(8,128)(2,1)S(1)}, u32[]{:S(2)}, u32[]{:S(2)}) collective-permute-start(bf16[16,1920]{1,0:T(8,128)(2,1)S(1)} %get-tuple-element.240), channel_id=1, source_target_pairs={{0,16},{4,20},{8,24},{12,28},{16,0},{20,4},{24,8},{28,12},{1,17},{... | collective-permute-start | bytes 184328 | tf_op jit(solution)/shard_map/ppermute | solution.py:564
  93.5 6.7 %collective-permute-start.45 = (bf16[16,3072]{1,0:T(8,128)(2,1)S(1)}, bf16[16,3072]{1,0:T(8,128)(2,1)S(1)}, u32[]{:S(2)}, u32[]{:S(2)}) collective-permute-start(bf16[16,3072]{1,0:T(8,128)(2,1)S(1)} %feed_fold.7), channel_id=1, source_target_pairs={{0,16},{4,20},{8,24},{12,28},{16,0},{20,4},{24,8},{28,12},{1,17},{... | collective-permute-start | bytes 294920 | tf_op jit(solution)/shard_map/ppermute | solution.py:564
  94.8 21.1 %collective-permute-start.34 = (f32[128,512]{1,0:T(8,128)S(1)}, f32[128,512]{1,0:T(8,128)S(1)}, u32[]{:S(2)}, u32[]{:S(2)}) collective-permute-start(f32[128,512]{1,0:T(8,128)S(1)} %get-tuple-element.204), channel_id=1, source_target_pairs={{0,1},{1,0},{2,3},{3,2},{4,5},{5,4},{6,7},{7,6},{8,9},{9,8},{10,11... | collective-permute-start | bytes 786440 | tf_op jit(solution)/shard_map/ppermute | solution.py:564
  96.5 6.8 %collective-permute-start.44 = (bf16[16,1280]{1,0:T(8,128)(2,1)S(1)}, bf16[16,1280]{1,0:T(8,128)(2,1)S(1)}, u32[]{:S(2)}, u32[]{:S(2)}) collective-permute-start(bf16[16,1280]{1,0:T(8,128)(2,1)S(1)} %get-tuple-element.239), channel_id=1, source_target_pairs={{0,16},{4,20},{8,24},{12,28},{16,0},{20,4},{24,8},{28,12},{1,17},{... | collective-permute-start | bytes 122888 | tf_op jit(solution)/shard_map/ppermute | solution.py:564
  97.8 7.0 %collective-permute-start.49 = (bf16[16,1920]{1,0:T(8,128)(2,1)S(1)}, bf16[16,1920]{1,0:T(8,128)(2,1)S(1)}, u32[]{:S(2)}, u32[]{:S(2)}) collective-permute-start(bf16[16,1920]{1,0:T(8,128)(2,1)S(1)} %cross_fold.7), channel_id=1, source_target_pairs={{0,16},{4,20},{8,24},{12,28},{16,0},{20,4},{24,8},{28,12},{1,17},{... | collective-permute-start | bytes 184328 | tf_op jit(solution)/shard_map/ppermute | solution.py:564
  100.3 8.9 %collective-permute-start.48 = (bf16[32,3072]{1,0:T(8,128)(2,1)S(1)}, bf16[32,3072]{1,0:T(8,128)(2,1)S(1)}, u32[]{:S(2)}, u32[]{:S(2)}) collective-permute-start(bf16[32,3072]{1,0:T(8,128)(2,1)S(1)} %constant_dynamic-update-slice_fusion), channel_id=1, source_target_pairs={{0,8},{4,12},{8,0},{12,4},{16,24},{20,28},{24,16},{28,20},{1,9},{5... | collective-permute-start | bytes 589832 | tf_op jit(solution)/shard_map/ppermute | solution.py:564
  103.3 7.0 %collective-permute-start.47 = (bf16[16,1280]{1,0:T(8,128)(2,1)S(1)}, bf16[16,1280]{1,0:T(8,128)(2,1)S(1)}, u32[]{:S(2)}, u32[]{:S(2)}) collective-permute-start(bf16[16,1280]{1,0:T(8,128)(2,1)S(1)} %self_fold.7), channel_id=1, source_target_pairs={{0,16},{4,20},{8,24},{12,28},{16,0},{20,4},{24,8},{28,12},{1,17},{... | collective-permute-start | bytes 122888 | tf_op jit(solution)/shard_map/ppermute | solution.py:564
  104.8 6.5 %collective-permute-start.51 = (bf16[32,1920]{1,0:T(8,128)(2,1)S(1)}, bf16[32,1920]{1,0:T(8,128)(2,1)S(1)}, u32[]{:S(2)}, u32[]{:S(2)}) collective-permute-start(bf16[32,1920]{1,0:T(8,128)(2,1)S(1)} %constant_dynamic-update-slice_fusion.2), channel_id=1, source_target_pairs={{0,8},{4,12},{8,0},{12,4},{16,24},{20,28},{24,16},{28,20},{1,9},{5... | collective-permute-start | bytes 368648 | tf_op jit(solution)/shard_map/ppermute | solution.py:564
  109.2 12.1 %collective-permute-start.54 = (bf16[64,3072]{1,0:T(8,128)(2,1)S(1)}, bf16[64,3072]{1,0:T(8,128)(2,1)S(1)}, u32[]{:S(2)}, u32[]{:S(2)}) collective-permute-start(bf16[64,3072]{1,0:T(8,128)(2,1)S(1)} %constant_dynamic-update-slice_fusion.4.low_ref), channel_id=1, source_target_pairs={{0,4},{4,0},{8,12},{12,8},{16,20},{20,16},{24,28},{28,24},{1,5},{5... | collective-permute-start | bytes 1179656 | tf_op jit(solution)/shard_map/ppermute | solution.py:564
  111.3 13.3 %collective-permute-start.53 = (bf16[64,1920]{1,0:T(8,128)(2,1)S(1)}, bf16[64,1920]{1,0:T(8,128)(2,1)S(1)}, u32[]{:S(2)}, u32[]{:S(2)}) collective-permute-start(bf16[64,1920]{1,0:T(8,128)(2,1)S(1)} %constant_dynamic-update-slice_fusion.8.low_ref), channel_id=1, source_target_pairs={{0,4},{4,0},{8,12},{12,8},{16,20},{20,16},{24,28},{28,24},{1,5},{5... | collective-permute-start | bytes 737288 | tf_op jit(solution)/shard_map/ppermute | solution.py:564
  114.8 11.6 %collective-permute-start.52 = (bf16[64,1280]{1,0:T(8,128)(2,1)S(1)}, bf16[64,1280]{1,0:T(8,128)(2,1)S(1)}, u32[]{:S(2)}, u32[]{:S(2)}) collective-permute-start(bf16[64,1280]{1,0:T(8,128)(2,1)S(1)} %constant_dynamic-update-slice_fusion.10.low_ref), channel_id=1, source_target_pairs={{0,4},{4,0},{8,12},{12,8},{16,20},{20,16},{24,28},{28,24},{1,5},{5... | collective-permute-start | bytes 491528 | tf_op jit(solution)/shard_map/ppermute | solution.py:564
  (36 other events, 201.4 us)

commit v3 on v2

--- a/solution.py
+++ b/solution.py
@@ -1,4 +1,5 @@
 import functools
+import itertools
 import math
 
 import jax
@@ -18,7 +19,11 @@
 BLOCK = 128
 HALF = 256
 GROUP = 4
-PIECES = 8
+PIECES = 4
+EARLY = "F"
+TURNS = "XFSTCFSCSFCSCS"
+SELF_HALVINGS = 2
+SELF_ORDER = PIECES - (PIECES >> SELF_HALVINGS)
 VMEM_BYTES = 32 * 1024 * 1024
 HIGHEST = lax.Precision.HIGHEST
 F32 = jnp.float32
@@ -57,21 +62,17 @@
 
 def split_pieces(pieces, f, half):
     for k, piece in enumerate(pieces[:2]):
-        rows = piece.shape[0] // 2
-        for h in range(2):
-            yield f ^ k, h, piece, h * rows, rows
-    for i, piece in enumerate(pieces[2:]):
-        yield f ^ (2 + i // 2), half ^ (i % 2), piece, 0, piece.shape[0]
-
-
-def place_split_rows(dst, pieces, f, half):
-    for owner, h, piece, first, rows in split_pieces(pieces, f, half):
-        dst[own(2 * owner + h, rows), :] = piece[first : first + rows, :]
-
-
-def place_split_columns(dst, pieces, f, half):
-    for owner, h, piece, first, rows in split_pieces(pieces, f, half):
-        dst[own(h, rows), own(owner, piece.shape[1])] = piece[first : first + rows, :]
+        yield f ^ k, 0, piece.shape[0], piece
+    parts = (len(pieces) - 2) // 2
+    for k in range(2):
+        far = pieces[2 + k * parts : 2 + (k + 1) * parts]
+        rows = far[0].shape[0]
+        for i, start in enumerate((half * rows, (1 - half) * rows, 2 * rows)[:parts]):
+            yield f ^ (2 + k), start, far[i].shape[0], far[i]
+
+
+def place_rows_of(dst, start, size, piece):
+    dst[pl.ds(pl.multiple_of(start, 16), size), :] = piece
 
 
 def bucket_of(distance):
@@ -129,30 +130,40 @@
     return jnp.where(head_lanes(rows), stacked[:rows, :], stacked[rows:, :])
 
 
-def emit(keep_ref, send_ref, chip_s, first, f, order):
+def emit(keep_ref, send_ref, chip_s, first, f, orders):
     core = f & 1
     rows = keep_ref.shape[0]
     piece = rows // PIECES
     columns = chip_s.shape[1]
     for q in range(PIECES):
-        to = pl.ds(pl.multiple_of((q ^ order) * piece, piece), piece)
-        for ref, which in ((keep_ref, core), (send_ref, 1 - core)):
+        for ref, which, order in ((keep_ref, core, orders[0]), (send_ref, 1 - core, orders[1])):
+            to = pl.ds(pl.multiple_of((q ^ order) * piece, piece), piece)
             at = pl.ds(pl.multiple_of(which * rows + q * piece, piece), piece)
             ref[to, first : first + columns] = chip_s[at, :]
 
 
-def pack_first(tokens_ref, q_ref, k_ref, v_ref, pack_ref, pack_s, sems):
-    width, inner = tokens_ref.shape[1], q_ref.shape[1]
-    copies, first = [], 0
-    for i, ref in enumerate((tokens_ref, q_ref, k_ref, v_ref)):
-        copies.append(pltpu.make_async_copy(ref, pack_s.at[:, first : first + ref.shape[1]], sems.at[i]))
-        copies[-1].start()
-        first += ref.shape[1]
-    for c in copies:
-        c.wait()
-    out = pltpu.make_async_copy(pack_s, pack_ref, sems.at[4])
-    out.start()
-    out.wait()
+def pack_first(
+    tokens_ref, q_ref, k_ref, v_ref, states_ref, g1_ref, g2_ref, g3_ref, table_ref,
+    pack_ref, pack_s, g1_s, g2_s, g3_s, table_s, wide_s, sems,
+):
+    rows = pack_s.shape[0]
+    pairs = side_by_side((tokens_ref, q_ref, k_ref, v_ref), rows, pack_s)
+    first = sum(ref.shape[1] for ref in (tokens_ref, q_ref, k_ref, v_ref))
+    enc, columns = states_ref.shape[0], states_ref.shape[1] * states_ref.shape[0] // rows
+    for i in range(rows // enc):
+        pairs.append((
+            states_ref.at[:, i * columns : (i + 1) * columns],
+            pack_s.at[i * enc : (i + 1) * enc, first : first + columns],
+        ))
+    first += columns
+    pairs += [(g1_ref, g1_s), (g2_ref, g2_s), (g3_ref, g3_s), (table_ref, table_s)]
+    wide_s[...] = jnp.zeros_like(wide_s)
+    run_copies(pairs, sems)
+    for i, gain in enumerate((g1_s, g2_s, g3_s)):
+        wide_s[i : i + 1, :] = gain[...].astype(F32)
+    wide_s[8:16, 0 : table_s.shape[1]] = table_s[...].astype(F32)
+    pack_s[0:16, first:] = wide_s[...].astype(BF16)
+    run_copies([(pack_s, pack_ref)], sems)
 
 
 def run_copies(pairs, sems):
@@ -163,55 +174,55 @@
         c.wait()
 
 
-def half_of(ref, half):
-    rows = ref.shape[0] // 2
-    return ref.at[pl.ds(pl.multiple_of(half * rows, rows), rows), :]
-
-
-def pack_second(
-    ids_ref, cq_ref, ck_ref, cv_ref, out_ref, co_ref, cross_ref, outs_ref, cross_half, out_half,
-    cross_s, outs_s, in_sems, out_sems,
-):
-    half, inner = ids_ref[2], cq_ref.shape[1]
-    run_copies(
-        [(ref, cross_s.at[:, i * inner : (i + 1) * inner]) for i, ref in enumerate((cq_ref, ck_ref, cv_ref))]
-        + [(ref, outs_s.at[i * inner : (i + 1) * inner, :]) for i, ref in enumerate((out_ref, co_ref))],
-        in_sems,
-    )
-    run_copies(
-        [(half_of(cross_s, half), cross_half), (half_of(outs_s, half), out_half), (cross_s, cross_ref), (outs_s, outs_ref)],
-        out_sems,
-    )
-
-
-def pack_third(ids_ref, gate_ref, up_ref, down_ref, gu_ref, gu_half, down_half, gu_s, down_s, in_sems, out_sems):
-    half, units = ids_ref[2], gate_ref.shape[1]
-    run_copies([(gate_ref, gu_s.at[:, :units]), (up_ref, gu_s.at[:, units:]), (down_ref, down_s)], in_sems)
-    run_copies([(half_of(gu_s, half), gu_half), (half_of(down_s, half), down_half), (gu_s, gu_ref)], out_sems)
+def side_by_side(refs, rows, target):
+    pairs, first = [], 0
+    for ref in refs:
+        for b in range(ref.shape[0] // rows):
+            pairs.append((ref.at[b * rows : (b + 1) * rows, :], target.at[:, first : first + ref.shape[1]]))
+            first += ref.shape[1]
+    return pairs
+
+
+def pack_weights(count, ids_ref, *refs):
+    weights, (whole_ref, *part_refs, whole_s, in_sems, out_sems) = refs[:count], refs[count:]
+    run_copies(side_by_side(weights, whole_s.shape[0], whole_s), in_sems)
+    rows = part_refs[0].shape[0]
+    starts = (pl.multiple_of(ids_ref[2] * rows, rows), 2 * rows)
+    parts = [(whole_s.at[pl.ds(a, ref.shape[0]), :], ref) for a, ref in zip(starts, part_refs)]
+    run_copies(parts + [(whole_s, whole_ref)], out_sems)
 
 
 def self_forward(
-    ids_ref, w0, w1, w2, w3, a0, a1, a2, a3,
-    x_ref, normed_ref, q_ref, kv_ref, pa_ref, pb_ref, mixed_ref, aux_ref,
-    w_s, bias_a, bias_b,
+    ids_ref, w0, w1, w2, w3,
+    x_ref, states_ref, normed_ref, q_ref, kv_ref, pa_ref, pb_ref, mixed_ref, aux_ref,
+    w_s, bias_a, bias_b, table_s,
 ):
     f = ids_ref[0]
     length, width = x_ref.shape
     inner = H * DH
+    enc = states_ref.shape[0] // GROUP
+    after_weights = width + w_s.shape[1]
+    columns = width * enc // w0.shape[0]
     for k, piece in enumerate((w0, w1, w2, w3)):
         x_ref[own(f ^ k, w0.shape[0]), :] = piece[:, :width]
-        w_s[own(f ^ k, w0.shape[0]), :] = piece[:, width:]
-    aux = sum(a[...].astype(F32) for a in (a0, a1, a2, a3))
-    aux_ref[...] = aux
+        w_s[own(f ^ k, w0.shape[0]), :] = piece[:, width:after_weights]
+        for i in range(width // columns):
+            states_ref[own(f ^ k, enc), i * columns : (i + 1) * columns] = (
+                piece[i * enc : (i + 1) * enc, after_weights : after_weights + columns]
+            )
+        small = piece[0:16, after_weights + columns :].astype(F32)
+        aux_ref[:, own(f ^ k, BLOCK)] = small[0:8, :]
+        table_s[own(f ^ k, 8), :] = small[8:16, :]
     for hb in range(length // HALF):
         at = slice(hb * HALF, (hb + 1) * HALF)
         x = x_ref[at, :].astype(F32)
-        normed = (x * rms(x) * aux[0:1, :]).astype(BF16)
+        normed = (x * rms(x) * aux_ref[0:1, :]).astype(BF16)
         normed_ref[at, :] = normed
         kv_ref[at, :] = dot(normed, w_s[:, inner:]).astype(BF16)
     q_ref[...] = dot(place_mine(normed_ref, f), w_s[:, :inner]).astype(BF16)
-    per_offset = jnp.dot(
-        aux[8:16, 0:BLOCK], offset_onehot(BLOCK, 1), precision=HIGHEST, preferred_element_type=F32
+    per_offset = lax.dot_general(
+        table_s[...], offset_onehot(BUCKETS, 1), (((0,), (0,)), ((), ())),
+        precision=HIGHEST, preferred_element_type=F32,
     )
     first, second = my_blocks(f)
     row = lax.broadcasted_iota(jnp.int32, (BLOCK, 2 * BLOCK), 0)
@@ -241,18 +252,26 @@
             mixed_ref[at, lanes] = unstack_heads(dot(probs, v2[:seen, :])).astype(BF16)
 
 
+def place_cross(w_s, outs_s, pieces, f, half):
+    first = w_s.shape[1]
+    own_rows = pieces[0].shape[0]
+    for owner, start, rows, piece in split_pieces(pieces, f, half):
+        place_rows_of(w_s, owner * own_rows + start, rows, piece[:, :first])
+        for b in range(outs_s.shape[0] // own_rows):
+            to = pl.ds(pl.multiple_of(b * own_rows + start, 16), rows)
+            outs_s[to, own(owner, BLOCK)] = piece[:, first + b * BLOCK : first + (b + 1) * BLOCK]
+
+
 def cross_forward(
     ids_ref, x_ref, mixed_ref, aux_ref,
-    w0, w1, w2, w3, w4, w5, o0, o1, o2, o3, o4, o5, s0, s1, s2, s3,
+    w0, w1, w2, w3, w4, w5, states_s,
     h1_ref, n2_ref, cq_ref, ckv_ref, probs_ref, cmixed_ref, h2_ref, n3_ref,
-    w_s, outs_s, states_s,
+    w_s, outs_s,
 ):
     f = ids_ref[0]
     inner = H * DH
     half = ids_ref[2]
-    place_split_rows(w_s, (w0, w1, w2, w3, w4, w5), f, half)
-    place_split_columns(outs_s, (o0, o1, o2, o3, o4, o5), f, half)
-    place_rows(states_s, (s0, s1, s2, s3), f, 0, s0.shape[0])
+    place_cross(w_s, outs_s, (w0, w1, w2, w3, w4, w5), f, half)
     hidden = place_mine(x_ref, f).astype(F32) + dot(mixed_ref[...], outs_s[:inner, :])
     h1_ref[...] = hidden
     normed = (hidden * rms(hidden) * aux_ref[1:2, :]).astype(BF16)
@@ -272,19 +291,23 @@
 
 def feed_forward(
     ids_ref, h2_ref, n3_ref, aux_ref,
-    g0, g1, g2, g3, g4, g5, d0, d1, d2, d3, d4, d5, c0, c1, c2, c3,
+    g0, g1, g2, g3, g4, g5, g6, g7, c0, c1, c2, c3,
     result_ref, grad_h2_ref, keep_ref, send_ref, gain_ref,
     gu_s, down_s, cot_s, cot_mine, units_s, gate_s, up_s, chip_s, down_chip_s,
 ):
-    f, order = ids_ref[0], ids_ref[1]
+    f, orders = ids_ref[0], (ids_ref[1], ids_ref[3])
     chip = f >> 1
     mine_rows, width = h2_ref.shape
     rows = cot_s.shape[0] // GROUP
     hidden_units = down_s.shape[0]
     own_units = hidden_units // GROUP
     half = ids_ref[2]
-    place_split_rows(gu_s, (g0, g1, g2, g3, g4, g5), f, half)
-    place_split_rows(down_s, (d0, d1, d2, d3, d4, d5), f, half)
+    own_rows = g0.shape[0]
+    for owner, start, size, piece in split_pieces((g0, g1, g2, g3, g4, g5, g6, g7), f, half):
+        place_rows_of(gu_s, owner * own_rows + start, size, piece[:, : 2 * hidden_units])
+        for b in range(own_units // own_rows):
+            first = 2 * hidden_units + b * width
+            place_rows_of(down_s, owner * own_units + b * own_rows + start, size, piece[:, first : first + width])
     place_rows(cot_s, (c0, c1, c2, c3), f, 0, rows)
     cot_mine[...] = place_mine(cot_s, f)
     grad_normed = jnp.zeros((mine_rows, width), F32)
@@ -315,14 +338,14 @@
     normed_chip = n3_ref[:, own(chip, chip_rows)]
     chip_s[:, :hidden_units] = t_dot(normed_chip, gate_s[...]).astype(BF16)
     chip_s[:, hidden_units:] = t_dot(normed_chip, up_s[...]).astype(BF16)
-    emit(keep_ref, send_ref, chip_s, 0, f, order)
+    emit(keep_ref, send_ref, chip_s, 0, f, orders)
     grad_down = t_dot(units_s[:, own(chip, 2 * own_units)], cot_mine[...]).astype(BF16)
     parts = own_units // g0.shape[0]
     for which in range(2):
         for part in range(parts):
             at = slice((which * parts + part) * g0.shape[0], (which * parts + part + 1) * g0.shape[0])
             down_chip_s[which * g0.shape[0] : (which + 1) * g0.shape[0], part * width : (part + 1) * width] = grad_down[at, :]
-    emit(keep_ref, send_ref, down_chip_s, 2 * hidden_units, f, order)
+    emit(keep_ref, send_ref, down_chip_s, 2 * hidden_units, f, orders)
 
 
 def put_columns(chip_s, first, grad, own_rows):
@@ -336,19 +359,17 @@
 
 def cross_backward(
     ids_ref, grad_h2_ref, h1_ref, n2_ref, cq_ref, ckv_ref, probs_ref, cmixed_ref, mixed_ref, aux_ref,
-    w0, w1, w2, w3, w4, w5, o0, o1, o2, o3, o4, o5, s0, s1, s2, s3,
+    w0, w1, w2, w3, w4, w5, states_s,
     grad_h1_ref, mix_ref, states_keep, states_send, keep_ref, send_ref, gain_ref,
-    w_s, outs_s, states_s, low_s, dq_s, dkv_s, chip_s, states_chip,
+    w_s, outs_s, low_s, dq_s, dkv_s, chip_s, states_chip,
 ):
-    f, order = ids_ref[0], ids_ref[1]
+    f, orders = ids_ref[0], (ids_ref[1], ids_ref[3])
     chip, core = f >> 1, f & 1
     inner = H * DH
     own_rows = w0.shape[0]
     chip_columns = own(chip, 2 * own_rows)
     half = ids_ref[2]
-    place_split_rows(w_s, (w0, w1, w2, w3, w4, w5), f, half)
-    place_split_columns(outs_s, (o0, o1, o2, o3, o4, o5), f, half)
-    place_rows(states_s, (s0, s1, s2, s3), f, 0, s0.shape[0])
+    place_cross(w_s, outs_s, (w0, w1, w2, w3, w4, w5), f, half)
     low = grad_h2_ref[...].astype(BF16)
     low_s[...] = low
     grad_mixed = dot_t(low, outs_s[inner:, :]).astype(BF16)
@@ -374,29 +395,16 @@
     put_columns(chip_s, 4 * inner, t_dot(mixed_ref[...], low_s[:, chip_columns]).astype(BF16), own_rows)
     chip_s[:, :inner] = t_dot(n2_ref[:, chip_columns], dq_s[...]).astype(BF16)
     chip_s[:, inner : 3 * inner] = t_dot(states_s[:, chip_columns], dkv_s[...]).astype(BF16)
-    emit(keep_ref, send_ref, chip_s, 0, f, order)
-    enc = s0.shape[0]
+    emit(keep_ref, send_ref, chip_s, 0, f, orders)
+    enc = states_s.shape[0] // GROUP
     states_chip[...] = dot_t(dkv_s[own(chip, 2 * enc), :], w_s[:, inner:])
     states_keep[...] = states_chip[own(core, enc), :]
     states_send[...] = states_chip[own(1 - core, enc), :]
 
 
-def self_backward(
-    ids_ref, grad_h1_ref, mix_ref, x_ref, normed_ref, q_ref, kv_ref, pa_ref, pb_ref, aux_ref, gain2_ref, gain3_ref,
-    w0, w1, w2, w3,
-    tokens_keep, tokens_send, keep_ref, send_ref,
-    w_s, dq_s, dkv_s, ds_a, ds_b, chip_s, small_s, gain_s, table_s,
-):
-    f, order = ids_ref[0], ids_ref[1]
-    chip, core = f >> 1, f & 1
-    length, width = x_ref.shape
-    rows = length // GROUP
+def self_backward(ids_ref, mix_ref, q_ref, kv_ref, pa_ref, pb_ref, dq_s, dkv_s, table_s, ds_a, ds_b):
     inner = H * DH
-    own_rows = w0.shape[0]
-    chip_columns = own(chip, 2 * own_rows)
-    for k, piece in enumerate((w0, w1, w2, w3)):
-        w_s[own(f ^ k, own_rows), :] = piece[:, width:]
-    first, second = my_blocks(f)
+    first, second = my_blocks(ids_ref[0])
     row = lax.broadcasted_iota(jnp.int32, (2 * BLOCK, 4 * BLOCK), 0)
     ds_a[:, 0:BLOCK] = jnp.zeros((2 * BLOCK, BLOCK), F32)
     offset_sums, far_sums = [], []
@@ -446,6 +454,22 @@
         precision=HIGHEST, preferred_element_type=F32,
     )
 
+
+def self_gradients(
+    ids_ref, grad_h1_ref, x_ref, normed_ref, aux_ref, gain2_ref, gain3_ref, dq_s, dkv_s, table_s, w0, w1, w2, w3,
+    tokens_keep, tokens_send, keep_ref, send_ref,
+    w_s, chip_s, small_s, gain_s,
+):
+    f, orders = ids_ref[0], (ids_ref[1] & SELF_ORDER, ids_ref[3] & SELF_ORDER)
+    chip = f >> 1
+    length, width = x_ref.shape
+    rows = length // GROUP
+    inner = H * DH
+    own_rows = w0.shape[0]
+    chip_columns = own(chip, 2 * own_rows)
+    first, second = my_blocks(f)
+    for k, piece in enumerate((w0, w1, w2, w3)):
+        w_s[own(f ^ k, own_rows), :] = piece[:, width : width + 3 * inner]
     gain = aux_ref[0:1, :]
     mine, block = own(chip, rows), own(f, rows)
     others = own(f ^ 1, rows)
@@ -467,7 +491,7 @@
     normed_mine = jnp.concatenate([normed_ref[own(b, BLOCK), chip_columns] for b in (first, second)], axis=0)
     chip_s[:, :inner] = t_dot(normed_mine, dq_s[...]).astype(BF16)
     chip_s[:, inner:] = t_dot(normed_ref[:, chip_columns], dkv_s[...]).astype(BF16)
-    emit(keep_ref, send_ref, chip_s, 0, f, order)
+    emit(keep_ref, send_ref, chip_s, 0, f, orders)
     gain_s[0:8, :] = gain2_ref[...]
     gain_s[8:16, :] = gain3_ref[...]
     buckets = BUCKETS // GROUP
@@ -484,7 +508,7 @@
             axis=0,
         )
         small_s[which * own_rows : (which + 1) * own_rows, :] = small.astype(BF16)
-    emit(keep_ref, send_ref, small_s, 3 * inner, f, order)
+    emit(keep_ref, send_ref, small_s, 3 * inner, f, orders)
 
 
 def fold(keep_ref, arrived_ref, *out_refs):
@@ -494,8 +518,8 @@
         ref[...] = total[i * rows : (i + 1) * rows, :]
 
 
-def pieces_of(ids_ref, halves):
-    order = ids_ref[1]
+def pieces_of(ids_ref, halves, mask=PIECES - 1):
+    order = ids_ref[1] & mask
     for i, half in enumerate(halves):
         piece = half.shape[0] * len(halves) // PIECES
         here = PIECES // len(halves)
@@ -530,7 +554,7 @@
 
 def unpack_self(ids_ref, low_ref, high_ref, q_ref, k_ref, v_ref, g1_ref, g2_ref, g3_ref, table_ref, small_s):
     inner = q_ref.shape[1]
-    for at, size, rows in pieces_of(ids_ref, (low_ref, high_ref)):
+    for at, size, rows in pieces_of(ids_ref, (low_ref, high_ref), SELF_ORDER):
         to = pl.ds(pl.multiple_of(at, size), size)
         for i, ref in enumerate((q_ref, k_ref, v_ref)):
             ref[to, :] = rows[:, i * inner : (i + 1) * inner]
@@ -545,8 +569,7 @@
 SMEM = pl.BlockSpec(memory_space=pltpu.SMEM)
 
 
-def call(kernel, name, out_shapes, scratch, args, flops, with_ids=True, place=VMEM):
-    moved = sum(a.size * a.dtype.itemsize for a in args)
+def call(kernel, name, out_shapes, scratch, args, with_ids=True, place=VMEM):
     return pl.pallas_call(
         kernel,
         name=name,
@@ -555,7 +578,7 @@
         out_specs=[place] * len(out_shapes),
         scratch_shapes=[pltpu.VMEM(*s) if isinstance(s, tuple) else s for s in scratch],
         compiler_params=pltpu.CompilerParams(vmem_limit_bytes=VMEM_BYTES if place is VMEM else 56 * 1024 * 1024),
-        cost_estimate=pl.CostEstimate(flops=flops, bytes_accessed=moved, transcendentals=0),
+        cost_estimate=pl.CostEstimate(flops=1, bytes_accessed=1, transcendentals=0),
     )(*args)
 
 
@@ -572,26 +595,37 @@
     return pack, hop(pack, "fsdp", 1), far, hop(far, "fsdp", 1)
 
 
-def beside_split(pack, far, far_other):
-    return pack, hop(pack, "fsdp", 1), far, far_other, hop(far, "fsdp", 1), hop(far_other, "fsdp", 1)
+def beside_split(pack, far, far_other, *rest):
+    parts = (far, far_other, *rest)
+    return pack, hop(pack, "fsdp", 1), *parts, *(hop(a, "fsdp", 1) for a in parts)
+
+
+def rep_hop(x, bits):
+    replicas, group = lax.axis_size("rep"), lax.axis_size("fsdp")
+    pairs = [(r * group + f, (r ^ bits[f & 1]) * group + f) for r in range(replicas) for f in range(group)]
+    return lax.ppermute(x, ("rep", "fsdp"), pairs)
 
 
 class Sum:
-    def __init__(self, name, keep, send, steps):
-        self.name, self.keep, self.steps, self.at = name, keep, steps, 0
+    def __init__(self, name, keep, send, halvings):
+        bits = (lax.axis_size("rep") - 1).bit_length()
+        self.name, self.keep, self.at = name, keep, 0
         self.arrived = hop(send, "fsdp", 1)
+        self.steps = [(1, 2), (2, 1)] + [(1 << i, 1 << i) for i in range(2, bits)]
+        self.back = self.steps[:halvings]
+        self.halvings = halvings
 
     def fold(self, earlier):
         keep, arrived = all_after((self.keep, self.arrived), earlier)
-        halving = self.at < len(self.steps) and (1 << self.at) < PIECES
-        shape = (keep.shape[0] // 2, keep.shape[1]) if halving else keep.shape
-        out = call(fold, f"{self.name}_fold", [(shape, BF16)] * (1 + halving), [], [keep, arrived], 0, False)
+        halving = self.at < self.halvings
+        total = (keep.astype(F32) + arrived.astype(F32)).astype(BF16)
+        middle = total.shape[0] // 2
+        out = (total[:middle], total[middle:]) if halving else (total,)
         self.keep = out[0]
         if self.at < len(self.steps):
-            self.arrived = hop(out[-1], "rep", self.steps[self.at])
+            self.arrived = rep_hop(out[-1], self.steps[self.at])
         else:
-            self.back = [i for i in range(len(self.steps)) if (1 << i) < PIECES]
-            self.arrived = hop(self.keep, "rep", self.steps[self.back[-1]])
+            self.arrived = rep_hop(self.keep, self.back[-1])
         self.at += 1
         return self.keep
 
@@ -599,11 +633,14 @@
         keep, arrived = all_after((self.keep, self.arrived), earlier)
         self.back.pop()
         self.keep = jnp.concatenate((keep, arrived))
-        self.arrived = hop(self.keep, "rep", self.steps[self.back[-1]])
+        self.arrived = rep_hop(self.keep, self.back[-1])
         return self.keep
 
     def halves(self, earlier):
         return all_after((self.keep, self.arrived), earlier)
+
+    def actions(self):
+        return [self.fold] * (len(self.steps) + 1 - self.at) + [self.widen] * (len(self.back) - 1)
 
 
 def per_device(
@@ -633,99 +670,92 @@
     length, enc_all, mine = rows * GROUP, enc * GROUP, 2 * BLOCK
     f = lax.axis_index("fsdp").astype(jnp.int32)
     replica = lax.axis_index("rep").astype(jnp.int32)
-    steps = [1 << i for i in range((lax.axis_size("rep") - 1).bit_length())]
-    order = ((replica & 1) << 2) | (replica & 2) | ((replica >> 2) & 1)
-    half = replica & 1
-    ids = jnp.stack([f, order, half])
+    order_0 = ((replica & 1) << 1) | ((replica >> 1) & 1)
+    order_1 = replica & 3
+    core = f & 1
+    ids = jnp.stack([f, jnp.where(core == 0, order_0, order_1), replica & 1, jnp.where(core == 0, order_1, order_0)])
 
     hbm = pl.BlockSpec(memory_space=pl.ANY)
+    first_columns = width + 3 * inner + enc * width // rows + BLOCK
     (first_pack,) = call(
         pack_first,
         "pack_first",
-        [((rows, width + 3 * inner), BF16)],
-        [((rows, width + 3 * inner), BF16), pltpu.SemaphoreType.DMA((5,))],
-        [tokens[0], query_w, key_w, value_w],
-        0,
+        [((rows, first_columns), BF16)],
+        [
+            ((rows, first_columns), BF16),
+            ((1, own_rows), BF16),
+            ((1, own_rows), BF16),
+            ((1, own_rows), BF16),
+            (bias_table.shape, BF16),
+            ((16, BLOCK), F32),
+            pltpu.SemaphoreType.DMA((8 + rows // enc,)),
+        ],
+        [tokens[0], query_w, key_w, value_w, states[0], self_gain[None], cross_gain[None], mlp_gain[None], bias_table],
         False,
         hbm,
     )
-    aux = jnp.zeros((16, width), BF16)
-    aux = lax.dynamic_update_slice(aux, jnp.stack([self_gain, cross_gain, mlp_gain]), (0, f * own_rows))
-    aux = lax.dynamic_update_slice(aux, bias_table.T, (8, f * bias_table.shape[0]))
-    (aux,) = all_after((aux,), (first_pack,))
-    (second_ids,) = all_after((ids,), (aux,))
-    cross_pack, out_pack, cross_half, out_half = call(
-        pack_second,
-        "pack_second",
-        [
-            ((own_rows, 3 * inner), BF16),
-            ((2 * inner, own_rows), BF16),
-            ((own_rows // 2, 3 * inner), BF16),
-            ((inner, own_rows), BF16),
-        ],
-        [
-            ((own_rows, 3 * inner), BF16),
-            ((2 * inner, own_rows), BF16),
-            pltpu.SemaphoreType.DMA((5,)),
-            pltpu.SemaphoreType.DMA((4,)),
-        ],
-        [second_ids, cross_query_w, cross_key_w, cross_value_w, out_w, cross_out_w],
-        0,
-        place=hbm,
-    )
-    third_ids, states_own = all_after((ids, states[0]), (cross_pack,))
-    gate_pack, gate_half, down_half = call(
-        pack_third,
-        "pack_third",
-        [
-            ((own_rows, 2 * hidden_units), BF16),
-            ((own_rows // 2, 2 * hidden_units), BF16),
-            ((down_w.shape[0] // 2, width), BF16),
-        ],
-        [
-            ((own_rows, 2 * hidden_units), BF16),
-            (down_w.shape, BF16),
-            pltpu.SemaphoreType.DMA((3,)),
-            pltpu.SemaphoreType.DMA((3,)),
-        ],
-        [third_ids, gate_w, up_w, down_w],
-        0,
-        place=hbm,
-    )
-    (cot_own,) = all_after((cotangent[0],), (gate_pack,))
-    first_far = hop(first_pack, "fsdp", 2)
-    aux_far = hop(aux, "fsdp", 2)
-    out_far, cross_far, states_far = (hop(a, "fsdp", 2) for a in (out_half, cross_half, states_own))
-    gate_far, down_far, cot_far = (hop(a, "fsdp", 2) for a in (gate_half, down_half, cot_own))
-    first_far, aux_far = all_after((first_far, aux_far), (gate_pack,))
-    first_packs, aux_ws = beside(first_pack, first_far), beside(aux, aux_far)
-
-    x, normed_one, q, kv, probs_a, probs_b, mixed, aux = call(
+    (second_ids,) = all_after((ids,), (first_pack,))
+
+    def packed(name, ids, weights, parts):
+        columns = sum(w.size for w in weights) // own_rows
+        return call(
+            functools.partial(pack_weights, len(weights)),
+            name,
+            [((rows, columns), BF16) for rows in (own_rows, *parts)],
+            [
+                ((own_rows, columns), BF16),
+                pltpu.SemaphoreType.DMA((sum(w.shape[0] for w in weights) // own_rows,)),
+                pltpu.SemaphoreType.DMA((1 + len(parts),)),
+            ],
+            [ids, *weights],
+            place=hbm,
+        )
+
+    second_pack, second_half = packed(
+        "pack_second", second_ids, [cross_query_w, cross_key_w, cross_value_w, out_w, cross_out_w], [own_rows // 2]
+    )
+    (third_ids,) = all_after((ids,), (second_pack,))
+    part = 3 * own_rows // 8
+    third_pack, third_part, third_rest = packed(
+        "pack_third", third_ids, [gate_w, up_w, down_w], [part, own_rows - 2 * part]
+    )
+    first_far, second_far = hop(first_pack, "fsdp", 2), hop(second_half, "fsdp", 2)
+    (first_far,) = all_after((first_far,), (third_pack,))
+    first_packs = beside(first_pack, first_far)
+
+    x, states_all, normed_one, q, kv, probs_a, probs_b, mixed, aux = call(
         self_forward,
         "self_forward",
         [
             ((length, width), BF16),
+            ((enc_all, width), BF16),
             ((length, width), BF16),
             ((mine, inner), BF16),
             ((length, 2 * inner), BF16),
             ((PAIRS, 2 * BLOCK, 2 * BLOCK), BF16),
             ((PAIRS, 2 * BLOCK, length), BF16),
             ((mine, inner), BF16),
-            ((16, width), F32),
+            ((8, width), F32),
         ],
         [
             ((width, 3 * inner), BF16),
             ((PAIRS, 2 * BLOCK, 3 * BLOCK), F32),
             ((PAIRS, 2 * BLOCK, length), F32),
-        ],
-        [ids, *first_packs, *aux_ws],
-        2 * 10**9,
-    )
-    out_far, cross_far, states_far, gate_far = all_after((out_far, cross_far, states_far, gate_far), (aux,))
-    out_other, cross_other, gate_other = (hop(a, "rep", 1) for a in (out_far, cross_far, gate_far))
-    outs_ws = beside_split(out_pack, out_far, out_other)
-    cross_ws = beside_split(cross_pack, cross_far, cross_other)
-    states_all = beside(states[0], states_far)
+            ((BUCKETS, BLOCK), F32),
+        ],
+        [ids, *first_packs],
+    )
+    (cot_own,) = all_after((cotangent[0],), (first_far,))
+    second_far, second_pack, third_pack, third_part, third_rest = all_after(
+        (second_far, second_pack, third_pack, third_part, third_rest), (aux,)
+    )
+    third_far = hop(third_part, "fsdp", 2)
+    second_other = hop(second_far, "rep", 1)
+    rest_far = hop(third_rest, "fsdp", 2)
+    cot_far = hop(cot_own, "fsdp", 2)
+    seconds = beside_split(second_pack, second_far, second_other)
+    cots = beside(cot_own, cot_far)
+    (cross_ids,) = all_after((ids,), (third_far, cots[3]))
     hidden_one, normed_two, cross_q, cross_kv, cross_probs, cross_mixed, hidden_two, normed_three = call(
         cross_forward,
         "cross_forward",
@@ -742,16 +772,12 @@
         [
             ((width, 3 * inner), BF16),
             ((2 * inner, width), BF16),
-            ((enc_all, width), BF16),
-        ],
-        [ids, x, mixed, aux, *cross_ws, *outs_ws, *states_all],
-        2 * 10**9,
-    )
-    gate_far, gate_other, down_far, cot_far = all_after((gate_far, gate_other, down_far, cot_far), (normed_three,))
-    down_other = hop(down_far, "rep", 1)
-    gates = beside_split(gate_pack, gate_far, gate_other)
-    downs = beside_split(down_w, down_far, down_other)
-    cots = beside(cotangent[0], cot_far)
+        ],
+        [cross_ids, x, mixed, aux, *seconds, states_all],
+    )
+    third_other = hop(third_far, "rep", 1)
+    third_far, third_other, rest_far = all_after((third_far, third_other, rest_far), (normed_three,))
+    thirds = beside_split(third_pack, third_far, third_other, rest_far)
     down_columns = down_w.size // own_rows
     result, grad_hidden_two, ff_keep, ff_send, mlp_gain_sum = call(
         feed_forward,
@@ -774,10 +800,9 @@
             ((2 * own_rows, 2 * hidden_units), BF16),
             ((2 * own_rows, down_columns), BF16),
         ],
-        [ids, hidden_two, normed_three, aux, *gates, *downs, *cots],
-        4 * 10**9,
-    )
-    ff_sum = Sum("feed", ff_keep, ff_send, steps)
+        [ids, hidden_two, normed_three, aux, *thirds, *cots],
+    )
+    ff_sum = Sum("feed", ff_keep, ff_send, 2)
     grad_hidden_one, grad_mixed, states_keep, states_send, cross_keep, cross_send, cross_gain_sum = call(
         cross_backward,
         "cross_backward",
@@ -793,7 +818,6 @@
         [
             ((width, 3 * inner), BF16),
             ((2 * inner, width), BF16),
-            ((enc_all, width), BF16),
             ((mine, width), BF16),
             ((mine, inner), BF16),
             ((enc_all, 2 * inner), BF16),
@@ -802,17 +826,28 @@
         ],
         [
             ids, grad_hidden_two, hidden_one, normed_two, cross_q, cross_kv, cross_probs, cross_mixed, mixed,
-            aux, *cross_ws, *outs_ws, *states_all,
-        ],
-        2 * 10**9,
-    )
-    cross_sum = Sum("cross", cross_keep, cross_send, steps)
+            aux, *seconds, states_all,
+        ],
+    )
+    cross_sum = Sum("cross", cross_keep, cross_send, 2)
+    sums = {"F": ff_sum, "C": cross_sum}
     done = ff_sum.fold((grad_hidden_one,))
     done = cross_sum.fold((done,))
-    (grad_hidden_one,) = all_after((grad_hidden_one,), (done,))
-    tokens_keep, tokens_send, self_keep, self_send = call(
+    (grad_mixed,) = all_after((grad_mixed,), (done,))
+    grad_q, grad_kv, table_sums = call(
         self_backward,
         "self_backward",
+        [((mine, inner), BF16), ((length, 2 * inner), BF16), ((BLOCK, BLOCK), F32)],
+        [((2 * BLOCK, 3 * BLOCK), F32), ((2 * BLOCK, length), F32)],
+        [ids, grad_mixed, q, kv, probs_a, probs_b],
+    )
+    done = grad_q
+    for turn in EARLY:
+        done = sums[turn].fold((done,))
+    (late_ids,) = all_after((ids,), (done,))
+    tokens_keep, tokens_send, self_keep, self_send = call(
+        self_gradients,
+        "self_gradients",
         [
             ((rows, width), F32),
             ((rows, width), F32),
@@ -821,47 +856,35 @@
         ],
         [
             ((width, 3 * inner), BF16),
-            ((mine, inner), BF16),
-            ((length, 2 * inner), BF16),
-            ((2 * BLOCK, 3 * BLOCK), F32),
-            ((2 * BLOCK, length), F32),
             ((2 * own_rows, 3 * inner), BF16),
             ((2 * own_rows, BLOCK), BF16),
             ((16, width), F32),
-            ((BLOCK, BLOCK), F32),
-        ],
-        [
-            ids, grad_hidden_one, grad_mixed, x, normed_one, q, kv, probs_a, probs_b, aux,
-            cross_gain_sum, mlp_gain_sum, *first_packs,
-        ],
-        3 * 10**9,
-    )
-    self_sum = Sum("self", self_keep, self_send, steps)
-    grad_states = states_keep + hop(states_send, "fsdp", 1)
-    grad_tokens = tokens_keep + hop(tokens_send, "fsdp", 1)
-
-    done = ff_sum.fold((tokens_keep,))
-    order_of_sums = (self_sum, cross_sum, ff_sum)
-    for _ in range(len(steps) - 1):
-        for part in order_of_sums:
-            done = part.fold((done,))
-    for part in (self_sum, cross_sum):
-        done = part.fold((done,))
-    widenings = len(ff_sum.back) - 1
-    done = ff_sum.widen((done,)) if widenings else done
-    done = self_sum.fold((done,))
-    for i in range(widenings):
-        done = cross_sum.widen((done,))
-        if i + 1 < widenings:
-            done = ff_sum.widen((done,))
-        done = self_sum.widen((done,))
+        ],
+        [
+            late_ids, grad_hidden_one, x, normed_one, aux, cross_gain_sum, mlp_gain_sum,
+            grad_q, grad_kv, table_sums, *first_packs,
+        ],
+    )
+    done = tokens_keep
+    for turn in TURNS:
+        if turn == "X":
+            self_keep, self_send = all_after((self_keep, self_send), (done,))
+            self_sum = sums["S"] = Sum("self", self_keep, self_send, SELF_HALVINGS)
+        elif turn == "T":
+            states_send, tokens_send = all_after((states_send, tokens_send), (done,))
+            grad_states = states_keep + hop(states_send, "fsdp", 1)
+            grad_tokens = tokens_keep + hop(tokens_send, "fsdp", 1)
+        elif sums[turn].actions():
+            done = sums[turn].actions()[0]((done,))
+    while any(part.actions() for part in sums.values()):
+        for part in sums.values():
+            done = part.actions()[0]((done,)) if part.actions() else done
     grad_gate, grad_up, grad_down = call(
         unpack_feed,
         "unpack_feed",
         [(gate_w.shape, F32), (up_w.shape, F32), (down_w.shape, F32)],
         [],
         [ids, *ff_sum.halves((done,))],
-        0,
     )
     grad_cross_query, grad_cross_key, grad_cross_value, grad_cross_out, grad_out = call(
         unpack_cross,
@@ -869,7 +892,6 @@
         [(query_w.shape, F32)] * 3 + [(out_w.shape, F32)] * 2,
         [],
         [ids, *cross_sum.halves((grad_gate,))],
-        0,
     )
     grad_query, grad_key, grad_value, grad_g1, grad_g2, grad_g3, grad_table = call(
         unpack_self,
@@ -877,7 +899,6 @@
         [(query_w.shape, F32)] * 3 + [((1, own_rows), F32)] * 3 + [(bias_table.shape, F32)],
         [((own_rows, BLOCK), F32)],
         [ids, *self_sum.halves((grad_cross_query,))],
-        0,
     )
     return (
         result[None],

time: 128 us -> 112 us (0.88)
  waiting for transfers between devices: 45.5 us -> 37.9 us
  starting transfers between devices: 41.3 us -> 34 us
  local copies, waits for them, and re-layouts: 2.26 us -> 0.28 us
    ppermute x55 -> x23, waiting for transfers between devices: 45.5 us -> 18.8 us  [hop(): return lax.ppermute(x, axis, [(i, i ^ bits) for i in range(size)])]
    ppermute x55 -> x23, starting transfers between devices: 41.3 us -> 14.6 us  [hop(): return lax.ppermute(x, axis, [(i, i ^ bits) for i in range(size)])]
    ppermute x0 -> x15, starting transfers between devices: none -> 19.4 us  [rep_hop(): return lax.ppermute(x, ('rep', 'fsdp'), pairs)]
    ppermute x0 -> x15, waiting for transfers between devices: none -> 19.2 us  [rep_hop(): return lax.ppermute(x, ('rep', 'fsdp'), pairs)]
    unnamed x33 -> x19, local copies, waits for them, and re-layouts: 1.55 us -> 0.07 us
    pallas_call x23 -> x12, Pallas kernels: 35.8 us -> 35.7 us  [call(): pl.pallas_call(kernel, name=name, out_shape=[jax.ShapeDtypeStruct(s, d) f...]
  transfers between devices with their start and end apart: 55 -> 38, of which waited for: 27 -> 17; matrix products, arithmetic and copies ran while one was open for 2% -> 3% of each run, Pallas kernels for 22% -> 25%
where the time goes in v3:
time: 112 us
  waiting for transfers between devices  37.9 us (34%)
  Pallas kernels  35.7 us (32%)
  starting transfers between devices  34 us (30%)
  other arithmetic  2.78 us (2%)
    pallas_call x12, Pallas kernels, call(): pl.pallas_call(kernel, name=name, out_shape=[jax.ShapeDtypeStruct(s, d) f...  35.7 us
    ppermute x15, starting transfers between devices, rep_hop(): return lax.ppermute(x, ('rep', 'fsdp'), pairs)  19.4 us
    ppermute x15, waiting for transfers between devices, rep_hop(): return lax.ppermute(x, ('rep', 'fsdp'), pairs)  19.2 us
    ppermute x23, waiting for transfers between devices, hop(): return lax.ppermute(x, axis, [(i, i ^ bits) for i in range(size)])  18.8 us
    ppermute x23, starting transfers between devices, hop(): return lax.ppermute(x, axis, [(i, i ^ bits) for i in range(size)])  14.6 us
  transfers between devices with their start and end apart: 38, of which 17 were waited for; matrix products, arithmetic and copies ran while one was open for 3% of the time, Pallas kernels for 25%

profile of v3, /device:TPU:0, one launch (start us, length us, event | category | flops | bytes accessed | tf_op | source)
XLA Modules:
  0.0 111.7 jit_solution(10660223943343845266)
XLA Ops:
  0.7 1.9 %pack_first.1.w0 = bf16[128,2048]{1,0:T(8,128)(2,1)} custom-call(bf16[128,512]{1,0:T(8,128)(2,1)} %bitcast.21, bf16[128,384]{1,0:T(8,128)(2,1)} %q_ref.1, bf16[128,384]{1,0:T(8,128)(2,1)} %k_ref.1, bf16[128,384]{1,0:T(8,128)(2,1)} %v_ref.1, bf16[64,512]{1,0:T(8,128)(2,1)} %bitcast.22, bf16[1,128]{1,0:T(2,128)(2,1)} %bitcast.23, bf16[1,128]{1,0:T(2,128)(2,1)} %bitcast.24, ...), custom_call_target="tpu_custom_call" | custom-call | flops 1 | bytes 1 | tf_op jit(solution)/shard_map/pack_first/pallas_call | solution.py:573
  2.6 3.0 %collective-permute-start.2 = (bf16[128,2048]{1,0:T(8,128)(2,1)}, bf16[128,2048]{1,0:T(8,128)(2,1)S(1)}, u32[]{:S(2)}, u32[]{:S(2)}) collective-permute-start(bf16[128,2048]{1,0:T(8,128)(2,1)} %pack_first.1.w0), channel_id=1, source_target_pairs={{0,2},{1,3},{2,0},{3,1},{4,6},{5,7},{6,4},{7,5},{8,10},{9,11},{10,... | collective-permute-start | bytes 1572872 | tf_op jit(solution)/shard_map/ppermute | solution.py:587
  6.2 2.7 %pack_second.1 = (bf16[128,1920]{1,0:T(8,128)(2,1)}, bf16[64,1920]{1,0:T(8,128)(2,1)}) custom-call(s32[4]{0:T(128)} %pad_add_fusion.ids_ref, bf16[128,384]{1,0:T(8,128)(2,1)} %refs_0_.2, bf16[128,384]{1,0:T(8,128)(2,1)} %refs_1_.2, bf16[128,384]{1,0:T(8,128)(2,1)} %refs_2_.2, bf16[384,128]{1,0:T(8,128)(2,1)} %refs_3_.1, bf16[384,128]{1,0:T(8,128)(2,1)} %refs_4_.1), custom_call_target="tpu_custom_call" | custom-call | flops 1 | bytes 1 | tf_op jit(solution)/shard_map/pack_second/pallas_call | solution.py:573
  9.0 3.0 %pack_third.1 = (bf16[128,3072]{1,0:T(8,128)(2,1)}, bf16[48,3072]{1,0:T(8,128)(2,1)}, bf16[32,3072]{1,0:T(8,128)(2,1)}) custom-call(s32[4]{0:T(128)} %pad_add_fusion.ids_ref, bf16[128,1024]{1,0:T(8,128)(2,1)} %refs_0_.3, bf16[128,1024]{1,0:T(8,128)(2,1)} %refs_1_.3, bf16[256,512]{1,0:T(8,128)(2,1)} %refs_2_.3), custom_call_target="tpu_custom_call" | custom-call | flops 1 | bytes 1 | tf_op jit(solution)/shard_map/pack_third/pallas_call | solution.py:573
  12.1 5.7 %collective-permute-done.2.w2 = bf16[128,2048]{1,0:T(8,128)(2,1)S(1)} collective-permute-done((bf16[128,2048]{1,0:T(8,128)(2,1)}, bf16[128,2048]{1,0:T(8,128)(2,1)S(1)}, u32[]{:S(2)}, u32[]{:S(2)}) %collective-permute-start.2) | collective-permute-done | bytes 524320 | tf_op jit(solution)/shard_map/ppermute | solution.py:587
  17.8 1.7 %collective-permute-start = (bf16[64,1920]{1,0:T(8,128)(2,1)S(1)}, bf16[64,1920]{1,0:T(8,128)(2,1)S(1)}, u32[]{:S(2)}, u32[]{:S(2)}) collective-permute-start(bf16[64,1920]{1,0:T(8,128)(2,1)S(1)} %copy-done.6), channel_id=1, source_target_pairs={{0,2},{1,3},{2,0},{3,1},{4,6},{5,7},{6,4},{7,5},{8,10},{9,11},{10,... | collective-permute-start | bytes 737288 | tf_op jit(solution)/shard_map/ppermute | solution.py:587
  19.9 4.4 %self_forward.1 = (bf16[512,512]{1,0:T(8,128)(2,1)S(1)}, bf16[256,512]{1,0:T(8,128)(2,1)S(1)}, bf16[512,512]{1,0:T(8,128)(2,1)S(1)}, bf16[256,384]{1,0:T(8,128)(...) custom-call(s32[4]{0:T(128)S(1)} %copy-done.4, ...), custom_call_target="tpu_custom_call" | custom-call | flops 1 | bytes 1 | tf_op jit(solution)/shard_map/self_forward/pallas_call | solution.py:573
  24.3 2.3 %collective-permute-done.w2 = bf16[64,1920]{1,0:T(8,128)(2,1)S(1)} collective-permute-done((bf16[64,1920]{1,0:T(8,128)(2,1)S(1)}, bf16[64,1920]{1,0:T(8,128)(2,1)S(1)}, u32[]{:S(2)}, u32[]{:S(2)}) %collective-permute-start) | collective-permute-done | bytes 245792 | tf_op jit(solution)/shard_map/ppermute | solution.py:587
  26.5 1.7 %collective-permute-start.4 = (bf16[48,3072]{1,0:T(8,128)(2,1)S(1)}, bf16[48,3072]{1,0:T(8,128)(2,1)S(1)}, u32[]{:S(2)}, u32[]{:S(2)}) collective-permute-start(bf16[48,3072]{1,0:T(8,128)(2,1)S(1)} %copy-done.5), channel_id=1, source_target_pairs={{0,2},{1,3},{2,0},{3,1},{4,6},{5,7},{6,4},{7,5},{8,10},{9,11},{10,... | collective-permute-start | bytes 884744 | tf_op jit(solution)/shard_map/ppermute | solution.py:587
  29.3 1.8 %collective-permute-start.8 = (bf16[64,1920]{1,0:T(8,128)(2,1)S(1)}, bf16[64,1920]{1,0:T(8,128)(2,1)S(1)}, u32[]{:S(2)}, u32[]{:S(2)}) collective-permute-start(bf16[64,1920]{1,0:T(8,128)(2,1)S(1)} %collective-permute-done.w2), channel_id=1, source_target_pairs={{0,4},{4,0},{8,12},{12,8},{16,20},{20,16},{24,28},{28,24},{1,5},{5... | collective-permute-start | bytes 737288 | tf_op jit(solution)/shard_map/ppermute | solution.py:587
  31.9 3.4 %collective-permute-done.4.g2 = bf16[48,3072]{1,0:T(8,128)(2,1)S(1)} collective-permute-done((bf16[48,3072]{1,0:T(8,128)(2,1)S(1)}, bf16[48,3072]{1,0:T(8,128)(2,1)S(1)}, u32[]{:S(2)}, u32[]{:S(2)}) %collective-permute-start.4) | collective-permute-done | bytes 294944 | tf_op jit(solution)/shard_map/ppermute | solution.py:587
  35.3 1.8 %collective-permute-start.12 = (bf16[48,3072]{1,0:T(8,128)(2,1)S(1)}, bf16[48,3072]{1,0:T(8,128)(2,1)S(1)}, u32[]{:S(2)}, u32[]{:S(2)}) collective-permute-start(bf16[48,3072]{1,0:T(8,128)(2,1)S(1)} %collective-permute-done.4.g2), channel_id=1, source_target_pairs={{0,4},{4,0},{8,12},{12,8},{16,20},{20,16},{24,28},{28,24},{1,5},{5... | collective-permute-start | bytes 884744 | tf_op jit(solution)/shard_map/ppermute | solution.py:587
  38.1 1.8 %collective-permute-start.13 = (bf16[32,3072]{1,0:T(8,128)(2,1)S(1)}, bf16[32,3072]{1,0:T(8,128)(2,1)S(1)}, u32[]{:S(2)}, u32[]{:S(2)}) collective-permute-start(bf16[32,3072]{1,0:T(8,128)(2,1)S(1)} %copy-done.7), channel_id=1, source_target_pairs={{0,2},{1,3},{2,0},{3,1},{4,6},{5,7},{6,4},{7,5},{8,10},{9,11},{10,... | collective-permute-start | bytes 589832 | tf_op jit(solution)/shard_map/ppermute | solution.py:587
  39.9 2.9 %cross_forward.1 = (f32[256,512]{1,0:T(8,128)S(1)}, bf16[256,512]{1,0:T(8,128)(2,1)S(1)}, bf16[256,384]{1,0:T(8,128)(2,1)S(1)}, bf16[256,768]{1,0:T(8,128)(2,1)S...) custom-call(s32[4]{0:T(128)S(1)} %copy-done.4, ...), custom_call_target="tpu_custom_call" | custom-call | flops 1 | bytes 1 | tf_op jit(solution)/shard_map/cross_forward/pallas_call | solution.py:573
  42.9 2.5 %collective-permute-done.13.g4 = bf16[32,3072]{1,0:T(8,128)(2,1)S(1)} collective-permute-done((bf16[32,3072]{1,0:T(8,128)(2,1)S(1)}, bf16[32,3072]{1,0:T(8,128)(2,1)S(1)}, u32[]{:S(2)}, u32[]{:S(2)}) %collective-permute-start.13) | collective-permute-done | bytes 196640 | tf_op jit(solution)/shard_map/ppermute | solution.py:587
  47.9 4.0 %feed_forward.1 = (bf16[128,512]{1,0:T(8,128)(2,1)}, f32[256,512]{1,0:T(8,128)S(1)}, bf16[128,3072]{1,0:T(8,128)(2,1)S(1)}, bf16[128,3072]{1,0:T(8,128)(2,1)S(1)}, f32[8,512]{1,0:T(8,128)S(1)}) custom-call(s32[4]{0:T(128)S(1)} %copy-done.4, f32[256,512]{1,0:T(8,128)S(1)} %get-tuple-element.146.h2_ref, bf16[256,512]{1,0:T(8,128)(2,1)S(1)} %get-tuple-element.147.n3_ref, ...), custom_call_target="tpu_custom_call" | custom-call | flops 1 | bytes 1 | tf_op jit(solution)/shard_map/feed_forward/pallas_call | solution.py:573
  52.0 3.8 %cross_backward.1 = (f32[256,512]{1,0:T(8,128)S(1)}, bf16[256,384]{1,0:T(8,128)(2,1)S(1)}, f32[64,512]{1,0:T(8,128)S(1)}, f32[64,512]{1,0:T(8,128)S(1)}, bf16[12...) custom-call(s32[4]{0:T(128)S(1)} %copy-done.4, ...), custom_call_target="tpu_custom_call" | custom-call | flops 1 | bytes 1 | tf_op jit(solution)/shard_map/cross_backward/pallas_call | solution.py:573
  57.8 1.8 %collective-permute-start.19 = (bf16[64,3072]{1,0:T(8,128)(2,1)S(1)}, bf16[64,3072]{1,0:T(8,128)(2,1)S(1)}, u32[]{:S(2)}, u32[]{:S(2)}) collective-permute-start(bf16[64,3072]{1,0:T(8,128)(2,1)S(1)} %get-tuple-element.240), channel_id=1, source_target_pairs={{0,4},{1,9},{2,6},{3,11},{4,0},{5,13},{6,2},{7,15},{8,12},{9,1},{1... | collective-permute-start | bytes 1179656 | tf_op jit(solution)/shard_map/ppermute | solution.py:606
  59.7 6.0 %self_backward.1 = (bf16[256,384]{1,0:T(8,128)(2,1)S(1)}, bf16[512,768]{1,0:T(8,128)(2,1)S(1)}, f32[128,128]{1,0:T(8,128)S(1)}) custom-call(s32[4]{0:T(128)S(1)} %copy-done.4, bf16[256,384]{1,0:T(8,128)(2,1)S(1)} %get-tuple-element.171.mix_ref, bf16[256,384]{1,0:T(8,128)(2,1)S(1)} %get-tuple-element.172.q_ref, ...), custom_call_target="tpu_custom_call" | custom-call | flops 1 | bytes 1 | tf_op jit(solution)/shard_map/self_backward/pallas_call | solution.py:573
  65.9 1.7 %collective-permute-start.22 = (bf16[32,3072]{1,0:T(8,128)(2,1)S(1)}, bf16[32,3072]{1,0:T(8,128)(2,1)S(1)}, u32[]{:S(2)}, u32[]{:S(2)}) collective-permute-start(bf16[32,3072]{1,0:T(8,128)(2,1)S(1)} %get-tuple-element.244), channel_id=1, source_target_pairs={{0,8},{1,5},{2,10},{3,7},{4,12},{5,1},{6,14},{7,3},{8,0},{9,13},{1... | collective-permute-start | bytes 589832 | tf_op jit(solution)/shard_map/ppermute | solution.py:606
  69.1 2.1 %self_gradients.1 = (f32[128,512]{1,0:T(8,128)S(1)}, f32[128,512]{1,0:T(8,128)S(1)}, bf16[128,1280]{1,0:T(8,128)(2,1)S(1)}, bf16[128,1280]{1,0:T(8,128)(2,1)S(1)}) custom-call(s32[4]{0:T(128)S(1)} %copy-done.4, f32[256,512]{1,0:T(8,128)S(1)} %get-tuple-element.163.grad_h1_ref, bf16[512,512]{1,0:T(8,128)(2,1)S(1)} %get-tuple-element.141.x_ref, ...), custom_call_target="tpu_custom_call" | custom-call | flops 1 | bytes 1 | tf_op jit(solution)/shard_map/self_gradients/pallas_call | solution.py:573
  71.3 2.1 %collective-permute-done.22 = bf16[32,3072]{1,0:T(8,128)(2,1)S(1)} collective-permute-done((bf16[32,3072]{1,0:T(8,128)(2,1)S(1)}, bf16[32,3072]{1,0:T(8,128)(2,1)S(1)}, u32[]{:S(2)}, u32[]{:S(2)}) %collective-permute-start.22) | collective-permute-done | bytes 196640 | tf_op jit(solution)/shard_map/ppermute | solution.py:606
  73.4 2.7 %collective-permute-start.26 = (bf16[32,3072]{1,0:T(8,128)(2,1)S(1)}, bf16[32,3072]{1,0:T(8,128)(2,1)S(1)}, u32[]{:S(2)}, u32[]{:S(2)}) collective-permute-start(bf16[32,3072]{1,0:T(8,128)(2,1)S(1)} %add_convert_fusion.6), channel_id=1, source_target_pairs={{0,16},{1,17},{2,18},{3,19},{4,20},{5,21},{6,22},{7,23},{8,24},{9,... | collective-permute-start | bytes 589832 | tf_op jit(solution)/shard_map/ppermute | solution.py:606
  76.4 1.9 %collective-permute-start.29 = (bf16[32,1920]{1,0:T(8,128)(2,1)S(1)}, bf16[32,1920]{1,0:T(8,128)(2,1)S(1)}, u32[]{:S(2)}, u32[]{:S(2)}) collective-permute-start(bf16[32,1920]{1,0:T(8,128)(2,1)S(1)} %get-tuple-element.248), channel_id=1, source_target_pairs={{0,8},{1,5},{2,10},{3,7},{4,12},{5,1},{6,14},{7,3},{8,0},{9,13},{1... | collective-permute-start | bytes 368648 | tf_op jit(solution)/shard_map/ppermute | solution.py:606
  79.2 4.8 %collective-permute-done.26 = bf16[32,3072]{1,0:T(8,128)(2,1)S(1)} collective-permute-done((bf16[32,3072]{1,0:T(8,128)(2,1)S(1)}, bf16[32,3072]{1,0:T(8,128)(2,1)S(1)}, u32[]{:S(2)}, u32[]{:S(2)}) %collective-permute-start.26) | collective-permute-done | bytes 196640 | tf_op jit(solution)/shard_map/ppermute | solution.py:606
  84.9 2.1 %collective-permute-start.28 = (bf16[32,1280]{1,0:T(8,128)(2,1)S(1)}, bf16[32,1280]{1,0:T(8,128)(2,1)S(1)}, u32[]{:S(2)}, u32[]{:S(2)}) collective-permute-start(bf16[32,1280]{1,0:T(8,128)(2,1)S(1)} %get-tuple-element.250), channel_id=1, source_target_pairs={{0,8},{1,5},{2,10},{3,7},{4,12},{5,1},{6,14},{7,3},{8,0},{9,13},{1... | collective-permute-start | bytes 245768 | tf_op jit(solution)/shard_map/ppermute | solution.py:606
  88.0 2.9 %collective-permute-done.28 = bf16[32,1280]{1,0:T(8,128)(2,1)S(1)} collective-permute-done((bf16[32,1280]{1,0:T(8,128)(2,1)S(1)}, bf16[32,1280]{1,0:T(8,128)(2,1)S(1)}, u32[]{:S(2)}, u32[]{:S(2)}) %collective-permute-start.28) | collective-permute-done | bytes 81952 | tf_op jit(solution)/shard_map/ppermute | solution.py:606
  91.0 2.4 %collective-permute-start.30 = (bf16[32,1280]{1,0:T(8,128)(2,1)S(1)}, bf16[32,1280]{1,0:T(8,128)(2,1)S(1)}, u32[]{:S(2)}, u32[]{:S(2)}) collective-permute-start(bf16[32,1280]{1,0:T(8,128)(2,1)S(1)} %add_convert_fusion.11), channel_id=1, source_target_pairs={{0,16},{1,17},{2,18},{3,19},{4,20},{5,21},{6,22},{7,23},{8,24},{9,... | collective-permute-start | bytes 245768 | tf_op jit(solution)/shard_map/ppermute | solution.py:606
  94.7 2.6 %collective-permute-done.31 = bf16[32,1920]{1,0:T(8,128)(2,1)S(1)} collective-permute-done((bf16[32,1920]{1,0:T(8,128)(2,1)S(1)}, bf16[32,1920]{1,0:T(8,128)(2,1)S(1)}, u32[]{:S(2)}, u32[]{:S(2)}) %collective-permute-start.31) | collective-permute-done | bytes 122912 | tf_op jit(solution)/shard_map/ppermute | solution.py:606
  99.5 2.8 %collective-permute-done.34 = bf16[32,1920]{1,0:T(8,128)(2,1)S(1)} collective-permute-done((bf16[32,1920]{1,0:T(8,128)(2,1)S(1)}, bf16[32,1920]{1,0:T(8,128)(2,1)S(1)}, u32[]{:S(2)}, u32[]{:S(2)}) %collective-permute-start.34) | collective-permute-done | bytes 122912 | tf_op jit(solution)/shard_map/ppermute | solution.py:606
  105.2 1.8 %unpack_feed.1 = (f32[128,1024]{1,0:T(8,128)}, f32[128,1024]{1,0:T(8,128)}, f32[256,512]{1,0:T(8,128)}) custom-call(s32[4]{0:T(128)S(1)} %copy-done.4, bf16[64,3072]{1,0:T(8,128)(2,1)S(1)} %constant_dynamic-update-slice_fusion.low_ref, bf16[64,3072]{1,0:T(8,128)(2,1)S(1)} %collective-permute-done.37.high_ref), custom_call_target="tpu_custom_call" | custom-call | flops 1 | bytes 1 | tf_op jit(solution)/shard_map/unpack_feed/pallas_call | solution.py:573
  107.0 1.6 %collective-permute-done.36.high_ref = bf16[64,1920]{1,0:T(8,128)(2,1)S(1)} collective-permute-done((bf16[64,1920]{1,0:T(8,128)(2,1)S(1)}, bf16[64,1920]{1,0:T(8,128)(2,1)S(1)}, u32[]{:S(2)}, u32[]{:S(2)}) %collective-permute-start.36) | collective-permute-done | bytes 245792 | tf_op jit(solution)/shard_map/ppermute | solution.py:606
  (99 shorter events, 22.9 us)
Async XLA Ops:
  2.6 15.1 %collective-permute-start.2 = (bf16[128,2048]{1,0:T(8,128)(2,1)}, bf16[128,2048]{1,0:T(8,128)(2,1)S(1)}, u32[]{:S(2)}, u32[]{:S(2)}) collective-permute-start(bf16[128,2048]{1,0:T(8,128)(2,1)} %pack_first.1.w0), channel_id=1, source_target_pairs={{0,2},{1,3},{2,0},{3,1},{4,6},{5,7},{6,4},{7,5},{8,10},{9,11},{10,... | collective-permute-start | bytes 1572872 | tf_op jit(solution)/shard_map/ppermute | solution.py:587
  5.6 14.3 %collective-permute-start.1 = (bf16[128,2048]{1,0:T(8,128)(2,1)}, bf16[128,2048]{1,0:T(8,128)(2,1)S(1)}, u32[]{:S(2)}, u32[]{:S(2)}) collective-permute-start(bf16[128,2048]{1,0:T(8,128)(2,1)} %pack_first.1.w0), channel_id=1, source_target_pairs={{0,1},{1,0},{2,3},{3,2},{4,5},{5,4},{6,7},{7,6},{8,9},{9,8},{10,11... | collective-permute-start | bytes 1572872 | tf_op jit(solution)/shard_map/ppermute | solution.py:587
  17.8 8.8 %collective-permute-start = (bf16[64,1920]{1,0:T(8,128)(2,1)S(1)}, bf16[64,1920]{1,0:T(8,128)(2,1)S(1)}, u32[]{:S(2)}, u32[]{:S(2)}) collective-permute-start(bf16[64,1920]{1,0:T(8,128)(2,1)S(1)} %copy-done.6), channel_id=1, source_target_pairs={{0,2},{1,3},{2,0},{3,1},{4,6},{5,7},{6,4},{7,5},{8,10},{9,11},{10,... | collective-permute-start | bytes 737288 | tf_op jit(solution)/shard_map/ppermute | solution.py:587
  19.6 9.8 %collective-permute-start.5 = (bf16[128,512]{1,0:T(8,128)(2,1)S(1)}, bf16[128,512]{1,0:T(8,128)(2,1)S(1)}, u32[]{:S(2)}, u32[]{:S(2)}) collective-permute-start(bf16[128,512]{1,0:T(8,128)(2,1)S(1)} %bitcast.18), channel_id=1, source_target_pairs={{0,2},{1,3},{2,0},{3,1},{4,6},{5,7},{6,4},{7,5},{8,10},{9,11},{10,... | collective-permute-start | bytes 393224 | tf_op jit(solution)/shard_map/ppermute | solution.py:587
  26.5 8.7 %collective-permute-start.4 = (bf16[48,3072]{1,0:T(8,128)(2,1)S(1)}, bf16[48,3072]{1,0:T(8,128)(2,1)S(1)}, u32[]{:S(2)}, u32[]{:S(2)}) collective-permute-start(bf16[48,3072]{1,0:T(8,128)(2,1)S(1)} %copy-done.5), channel_id=1, source_target_pairs={{0,2},{1,3},{2,0},{3,1},{4,6},{5,7},{6,4},{7,5},{8,10},{9,11},{10,... | collective-permute-start | bytes 884744 | tf_op jit(solution)/shard_map/ppermute | solution.py:587
  29.3 8.7 %collective-permute-start.8 = (bf16[64,1920]{1,0:T(8,128)(2,1)S(1)}, bf16[64,1920]{1,0:T(8,128)(2,1)S(1)}, u32[]{:S(2)}, u32[]{:S(2)}) collective-permute-start(bf16[64,1920]{1,0:T(8,128)(2,1)S(1)} %collective-permute-done.w2), channel_id=1, source_target_pairs={{0,4},{4,0},{8,12},{12,8},{16,20},{20,16},{24,28},{28,24},{1,5},{5... | collective-permute-start | bytes 737288 | tf_op jit(solution)/shard_map/ppermute | solution.py:587
  31.1 8.8 %collective-permute-start.7 = (bf16[128,1920]{1,0:T(8,128)(2,1)S(1)}, bf16[128,1920]{1,0:T(8,128)(2,1)S(1)}, u32[]{:S(2)}, u32[]{:S(2)}) collective-permute-start(bf16[128,1920]{1,0:T(8,128)(2,1)S(1)} %copy-done.1), channel_id=1, source_target_pairs={{0,1},{1,0},{2,3},{3,2},{4,5},{5,4},{6,7},{7,6},{8,9},{9,8},{10,11... | collective-permute-start | bytes 1474568 | tf_op jit(solution)/shard_map/ppermute | solution.py:587
  31.4 16.6 %collective-permute-start.11 = (bf16[128,3072]{1,0:T(8,128)(2,1)S(1)}, bf16[128,3072]{1,0:T(8,128)(2,1)S(1)}, u32[]{:S(2)}, u32[]{:S(2)}) collective-permute-start(bf16[128,3072]{1,0:T(8,128)(2,1)S(1)} %copy-done.2), channel_id=1, source_target_pairs={{0,1},{1,0},{2,3},{3,2},{4,5},{5,4},{6,7},{7,6},{8,9},{9,8},{10,11... | collective-permute-start | bytes 2359304 | tf_op jit(solution)/shard_map/ppermute | solution.py:587
  31.6 6.5 %collective-permute-start.9 = (bf16[64,1920]{1,0:T(8,128)(2,1)S(1)}, bf16[64,1920]{1,0:T(8,128)(2,1)S(1)}, u32[]{:S(2)}, u32[]{:S(2)}) collective-permute-start(bf16[64,1920]{1,0:T(8,128)(2,1)S(1)} %collective-permute-done.w2), channel_id=1, source_target_pairs={{0,1},{1,0},{2,3},{3,2},{4,5},{5,4},{6,7},{7,6},{8,9},{9,8},{10,11... | collective-permute-start | bytes 737288 | tf_op jit(solution)/shard_map/ppermute | solution.py:587
  35.3 10.1 %collective-permute-start.12 = (bf16[48,3072]{1,0:T(8,128)(2,1)S(1)}, bf16[48,3072]{1,0:T(8,128)(2,1)S(1)}, u32[]{:S(2)}, u32[]{:S(2)}) collective-permute-start(bf16[48,3072]{1,0:T(8,128)(2,1)S(1)} %collective-permute-done.4.g2), channel_id=1, source_target_pairs={{0,4},{4,0},{8,12},{12,8},{16,20},{20,16},{24,28},{28,24},{1,5},{5... | collective-permute-start | bytes 884744 | tf_op jit(solution)/shard_map/ppermute | solution.py:587
  38.1 7.3 %collective-permute-start.13 = (bf16[32,3072]{1,0:T(8,128)(2,1)S(1)}, bf16[32,3072]{1,0:T(8,128)(2,1)S(1)}, u32[]{:S(2)}, u32[]{:S(2)}) collective-permute-start(bf16[32,3072]{1,0:T(8,128)(2,1)S(1)} %copy-done.7), channel_id=1, source_target_pairs={{0,2},{1,3},{2,0},{3,1},{4,6},{5,7},{6,4},{7,5},{8,10},{9,11},{10,... | collective-permute-start | bytes 589832 | tf_op jit(solution)/shard_map/ppermute | solution.py:587
  45.4 2.5 %collective-permute-start.14 = (bf16[48,3072]{1,0:T(8,128)(2,1)S(1)}, bf16[48,3072]{1,0:T(8,128)(2,1)S(1)}, u32[]{:S(2)}, u32[]{:S(2)}) collective-permute-start(bf16[48,3072]{1,0:T(8,128)(2,1)S(1)} %collective-permute-done.4.g2), channel_id=1, source_target_pairs={{0,1},{1,0},{2,3},{3,2},{4,5},{5,4},{6,7},{7,6},{8,9},{9,8},{10,11... | collective-permute-start | bytes 884744 | tf_op jit(solution)/shard_map/ppermute | solution.py:587
  45.4 2.5 %collective-permute-start.15 = (bf16[48,3072]{1,0:T(8,128)(2,1)S(1)}, bf16[48,3072]{1,0:T(8,128)(2,1)S(1)}, u32[]{:S(2)}, u32[]{:S(2)}) collective-permute-start(bf16[48,3072]{1,0:T(8,128)(2,1)S(1)} %collective-permute-done.12.g3), channel_id=1, source_target_pairs={{0,1},{1,0},{2,3},{3,2},{4,5},{5,4},{6,7},{7,6},{8,9},{9,8},{10,11... | collective-permute-start | bytes 884744 | tf_op jit(solution)/shard_map/ppermute | solution.py:587
  51.9 4.4 %collective-permute-start.18 = (bf16[128,3072]{1,0:T(8,128)(2,1)S(1)}, bf16[128,3072]{1,0:T(8,128)(2,1)S(1)}, u32[]{:S(2)}, u32[]{:S(2)}) collective-permute-start(bf16[128,3072]{1,0:T(8,128)(2,1)S(1)} %get-tuple-element.155), channel_id=1, source_target_pairs={{0,1},{1,0},{2,3},{3,2},{4,5},{5,4},{6,7},{7,6},{8,9},{9,8},{10,11... | collective-permute-start | bytes 2359304 | tf_op jit(solution)/shard_map/ppermute | solution.py:587
  57.8 8.0 %collective-permute-start.19 = (bf16[64,3072]{1,0:T(8,128)(2,1)S(1)}, bf16[64,3072]{1,0:T(8,128)(2,1)S(1)}, u32[]{:S(2)}, u32[]{:S(2)}) collective-permute-start(bf16[64,3072]{1,0:T(8,128)(2,1)S(1)} %get-tuple-element.240), channel_id=1, source_target_pairs={{0,4},{1,9},{2,6},{3,11},{4,0},{5,13},{6,2},{7,15},{8,12},{9,1},{1... | collective-permute-start | bytes 1179656 | tf_op jit(solution)/shard_map/ppermute | solution.py:606
  65.9 7.5 %collective-permute-start.22 = (bf16[32,3072]{1,0:T(8,128)(2,1)S(1)}, bf16[32,3072]{1,0:T(8,128)(2,1)S(1)}, u32[]{:S(2)}, u32[]{:S(2)}) collective-permute-start(bf16[32,3072]{1,0:T(8,128)(2,1)S(1)} %get-tuple-element.244), channel_id=1, source_target_pairs={{0,8},{1,5},{2,10},{3,7},{4,12},{5,1},{6,14},{7,3},{8,0},{9,13},{1... | collective-permute-start | bytes 589832 | tf_op jit(solution)/shard_map/ppermute | solution.py:606
  67.6 8.7 %collective-permute-start.27 = (bf16[64,1920]{1,0:T(8,128)(2,1)S(1)}, bf16[64,1920]{1,0:T(8,128)(2,1)S(1)}, u32[]{:S(2)}, u32[]{:S(2)}) collective-permute-start(bf16[64,1920]{1,0:T(8,128)(2,1)S(1)} %get-tuple-element.242), channel_id=1, source_target_pairs={{0,4},{1,9},{2,6},{3,11},{4,0},{5,13},{6,2},{7,15},{8,12},{9,1},{1... | collective-permute-start | bytes 737288 | tf_op jit(solution)/shard_map/ppermute | solution.py:606
  71.2 4.9 %collective-permute-start.21 = (bf16[128,1280]{1,0:T(8,128)(2,1)S(1)}, bf16[128,1280]{1,0:T(8,128)(2,1)S(1)}, u32[]{:S(2)}, u32[]{:S(2)}) collective-permute-start(bf16[128,1280]{1,0:T(8,128)(2,1)S(1)} %get-tuple-element.191), channel_id=1, source_target_pairs={{0,1},{1,0},{2,3},{3,2},{4,5},{5,4},{6,7},{7,6},{8,9},{9,8},{10,11... | collective-permute-start | bytes 983048 | tf_op jit(solution)/shard_map/ppermute | solution.py:587
  73.4 10.5 %collective-permute-start.26 = (bf16[32,3072]{1,0:T(8,128)(2,1)S(1)}, bf16[32,3072]{1,0:T(8,128)(2,1)S(1)}, u32[]{:S(2)}, u32[]{:S(2)}) collective-permute-start(bf16[32,3072]{1,0:T(8,128)(2,1)S(1)} %add_convert_fusion.6), channel_id=1, source_target_pairs={{0,16},{1,17},{2,18},{3,19},{4,20},{5,21},{6,22},{7,23},{8,24},{9,... | collective-permute-start | bytes 589832 | tf_op jit(solution)/shard_map/ppermute | solution.py:606
  76.4 8.5 %collective-permute-start.29 = (bf16[32,1920]{1,0:T(8,128)(2,1)S(1)}, bf16[32,1920]{1,0:T(8,128)(2,1)S(1)}, u32[]{:S(2)}, u32[]{:S(2)}) collective-permute-start(bf16[32,1920]{1,0:T(8,128)(2,1)S(1)} %get-tuple-element.248), channel_id=1, source_target_pairs={{0,8},{1,5},{2,10},{3,7},{4,12},{5,1},{6,14},{7,3},{8,0},{9,13},{1... | collective-permute-start | bytes 368648 | tf_op jit(solution)/shard_map/ppermute | solution.py:606
  78.3 5.8 %collective-permute-start.24 = (f32[64,512]{1,0:T(8,128)S(1)}, f32[64,512]{1,0:T(8,128)S(1)}, u32[]{:S(2)}, u32[]{:S(2)}) collective-permute-start(f32[64,512]{1,0:T(8,128)S(1)} %get-tuple-element.198), channel_id=1, source_target_pairs={{0,1},{1,0},{2,3},{3,2},{4,5},{5,4},{6,7},{7,6},{8,9},{9,8},{10,11... | collective-permute-start | bytes 393224 | tf_op jit(solution)/shard_map/ppermute | solution.py:587
  78.3 6.4 %collective-permute-start.25 = (bf16[64,1280]{1,0:T(8,128)(2,1)S(1)}, bf16[64,1280]{1,0:T(8,128)(2,1)S(1)}, u32[]{:S(2)}, u32[]{:S(2)}) collective-permute-start(bf16[64,1280]{1,0:T(8,128)(2,1)S(1)} %get-tuple-element.246), channel_id=1, source_target_pairs={{0,4},{1,9},{2,6},{3,11},{4,0},{5,13},{6,2},{7,15},{8,12},{9,1},{1... | collective-permute-start | bytes 491528 | tf_op jit(solution)/shard_map/ppermute | solution.py:606
  79.2 25.3 %collective-permute-start.23 = (f32[128,512]{1,0:T(8,128)S(1)}, f32[128,512]{1,0:T(8,128)S(1)}, u32[]{:S(2)}, u32[]{:S(2)}) collective-permute-start(f32[128,512]{1,0:T(8,128)S(1)} %get-tuple-element.196), channel_id=1, source_target_pairs={{0,1},{1,0},{2,3},{3,2},{4,5},{5,4},{6,7},{7,6},{8,9},{9,8},{10,11... | collective-permute-start | bytes 786440 | tf_op jit(solution)/shard_map/ppermute | solution.py:587
  84.0 9.4 %collective-permute-start.32 = (bf16[32,3072]{1,0:T(8,128)(2,1)S(1)}, bf16[32,3072]{1,0:T(8,128)(2,1)S(1)}, u32[]{:S(2)}, u32[]{:S(2)}) collective-permute-start(bf16[32,3072]{1,0:T(8,128)(2,1)S(1)} %add_convert_fusion.5), channel_id=1, source_target_pairs={{0,8},{1,5},{2,10},{3,7},{4,12},{5,1},{6,14},{7,3},{8,0},{9,13},{1... | collective-permute-start | bytes 589832 | tf_op jit(solution)/shard_map/ppermute | solution.py:606
  84.9 6.1 %collective-permute-start.28 = (bf16[32,1280]{1,0:T(8,128)(2,1)S(1)}, bf16[32,1280]{1,0:T(8,128)(2,1)S(1)}, u32[]{:S(2)}, u32[]{:S(2)}) collective-permute-start(bf16[32,1280]{1,0:T(8,128)(2,1)S(1)} %get-tuple-element.250), channel_id=1, source_target_pairs={{0,8},{1,5},{2,10},{3,7},{4,12},{5,1},{6,14},{7,3},{8,0},{9,13},{1... | collective-permute-start | bytes 245768 | tf_op jit(solution)/shard_map/ppermute | solution.py:606
  87.0 10.3 %collective-permute-start.31 = (bf16[32,1920]{1,0:T(8,128)(2,1)S(1)}, bf16[32,1920]{1,0:T(8,128)(2,1)S(1)}, u32[]{:S(2)}, u32[]{:S(2)}) collective-permute-start(bf16[32,1920]{1,0:T(8,128)(2,1)S(1)} %add_convert_fusion.9), channel_id=1, source_target_pairs={{0,16},{1,17},{2,18},{3,19},{4,20},{5,21},{6,22},{7,23},{8,24},{9,... | collective-permute-start | bytes 368648 | tf_op jit(solution)/shard_map/ppermute | solution.py:606
  91.0 7.8 %collective-permute-start.30 = (bf16[32,1280]{1,0:T(8,128)(2,1)S(1)}, bf16[32,1280]{1,0:T(8,128)(2,1)S(1)}, u32[]{:S(2)}, u32[]{:S(2)}) collective-permute-start(bf16[32,1280]{1,0:T(8,128)(2,1)S(1)} %add_convert_fusion.11), channel_id=1, source_target_pairs={{0,16},{1,17},{2,18},{3,19},{4,20},{5,21},{6,22},{7,23},{8,24},{9,... | collective-permute-start | bytes 245768 | tf_op jit(solution)/shard_map/ppermute | solution.py:606
  93.4 11.7 %collective-permute-start.37 = (bf16[64,3072]{1,0:T(8,128)(2,1)S(1)}, bf16[64,3072]{1,0:T(8,128)(2,1)S(1)}, u32[]{:S(2)}, u32[]{:S(2)}) collective-permute-start(bf16[64,3072]{1,0:T(8,128)(2,1)S(1)} %constant_dynamic-update-slice_fusion.low_ref), channel_id=1, source_target_pairs={{0,4},{1,9},{2,6},{3,11},{4,0},{5,13},{6,2},{7,15},{8,12},{9,1},{1... | collective-permute-start | bytes 1179656 | tf_op jit(solution)/shard_map/ppermute | solution.py:606
  97.3 4.9 %collective-permute-start.34 = (bf16[32,1920]{1,0:T(8,128)(2,1)S(1)}, bf16[32,1920]{1,0:T(8,128)(2,1)S(1)}, u32[]{:S(2)}, u32[]{:S(2)}) collective-permute-start(bf16[32,1920]{1,0:T(8,128)(2,1)S(1)} %add_convert_fusion.8), channel_id=1, source_target_pairs={{0,8},{1,5},{2,10},{3,7},{4,12},{5,1},{6,14},{7,3},{8,0},{9,13},{1... | collective-permute-start | bytes 368648 | tf_op jit(solution)/shard_map/ppermute | solution.py:606
  98.8 4.5 %collective-permute-start.33 = (bf16[32,1280]{1,0:T(8,128)(2,1)S(1)}, bf16[32,1280]{1,0:T(8,128)(2,1)S(1)}, u32[]{:S(2)}, u32[]{:S(2)}) collective-permute-start(bf16[32,1280]{1,0:T(8,128)(2,1)S(1)} %add_convert_fusion.10), channel_id=1, source_target_pairs={{0,8},{1,5},{2,10},{3,7},{4,12},{5,1},{6,14},{7,3},{8,0},{9,13},{1... | collective-permute-start | bytes 245768 | tf_op jit(solution)/shard_map/ppermute | solution.py:606
  102.3 6.3 %collective-permute-start.36 = (bf16[64,1920]{1,0:T(8,128)(2,1)S(1)}, bf16[64,1920]{1,0:T(8,128)(2,1)S(1)}, u32[]{:S(2)}, u32[]{:S(2)}) collective-permute-start(bf16[64,1920]{1,0:T(8,128)(2,1)S(1)} %constant_dynamic-update-slice_fusion.2.low_ref), channel_id=1, source_target_pairs={{0,4},{1,9},{2,6},{3,11},{4,0},{5,13},{6,2},{7,15},{8,12},{9,1},{1... | collective-permute-start | bytes 737288 | tf_op jit(solution)/shard_map/ppermute | solution.py:606
  103.3 7.0 %collective-permute-start.35 = (bf16[64,1280]{1,0:T(8,128)(2,1)S(1)}, bf16[64,1280]{1,0:T(8,128)(2,1)S(1)}, u32[]{:S(2)}, u32[]{:S(2)}) collective-permute-start(bf16[64,1280]{1,0:T(8,128)(2,1)S(1)} %constant_dynamic-update-slice_fusion.4.low_ref), channel_id=1, source_target_pairs={{0,4},{1,9},{2,6},{3,11},{4,0},{5,13},{6,2},{7,15},{8,12},{9,1},{1... | collective-permute-start | bytes 491528 | tf_op jit(solution)/shard_map/ppermute | solution.py:606
  (14 other events, 117.8 us)

commit v4 on v3

--- a/solution.py
+++ b/solution.py
@@ -21,7 +21,7 @@
 GROUP = 4
 PIECES = 4
 EARLY = "F"
-TURNS = "XFSTCFSCSFCSCS"
+TURNS = "XFSTCFCSSFCSCS"
 SELF_HALVINGS = 2
 SELF_ORDER = PIECES - (PIECES >> SELF_HALVINGS)
 VMEM_BYTES = 32 * 1024 * 1024
@@ -183,11 +183,11 @@
     return pairs
 
 
-def pack_weights(count, ids_ref, *refs):
+def pack_weights(count, bit, ids_ref, *refs):
     weights, (whole_ref, *part_refs, whole_s, in_sems, out_sems) = refs[:count], refs[count:]
     run_copies(side_by_side(weights, whole_s.shape[0], whole_s), in_sems)
     rows = part_refs[0].shape[0]
-    starts = (pl.multiple_of(ids_ref[2] * rows, rows), 2 * rows)
+    starts = (pl.multiple_of(ids_ref[bit] * rows, rows), 2 * rows)
     parts = [(whole_s.at[pl.ds(a, ref.shape[0]), :], ref) for a, ref in zip(starts, part_refs)]
     run_copies(parts + [(whole_s, whole_ref)], out_sems)
 
@@ -270,7 +270,7 @@
 ):
     f = ids_ref[0]
     inner = H * DH
-    half = ids_ref[2]
+    half = ids_ref[4]
     place_cross(w_s, outs_s, (w0, w1, w2, w3, w4, w5), f, half)
     hidden = place_mine(x_ref, f).astype(F32) + dot(mixed_ref[...], outs_s[:inner, :])
     h1_ref[...] = hidden
@@ -368,7 +368,7 @@
     inner = H * DH
     own_rows = w0.shape[0]
     chip_columns = own(chip, 2 * own_rows)
-    half = ids_ref[2]
+    half = ids_ref[4]
     place_cross(w_s, outs_s, (w0, w1, w2, w3, w4, w5), f, half)
     low = grad_h2_ref[...].astype(BF16)
     low_s[...] = low
@@ -673,7 +673,9 @@
     order_0 = ((replica & 1) << 1) | ((replica >> 1) & 1)
     order_1 = replica & 3
     core = f & 1
-    ids = jnp.stack([f, jnp.where(core == 0, order_0, order_1), replica & 1, jnp.where(core == 0, order_1, order_0)])
+    ids = jnp.stack(
+        [f, jnp.where(core == 0, order_0, order_1), replica & 1, jnp.where(core == 0, order_1, order_0), (replica >> 1) & 1]
+    )
 
     hbm = pl.BlockSpec(memory_space=pl.ANY)
     first_columns = width + 3 * inner + enc * width // rows + BLOCK
@@ -696,10 +698,10 @@
     )
     (second_ids,) = all_after((ids,), (first_pack,))
 
-    def packed(name, ids, weights, parts):
+    def packed(name, ids, weights, parts, bit):
         columns = sum(w.size for w in weights) // own_rows
         return call(
-            functools.partial(pack_weights, len(weights)),
+            functools.partial(pack_weights, len(weights), bit),
             name,
             [((rows, columns), BF16) for rows in (own_rows, *parts)],
             [
@@ -712,12 +714,12 @@
         )
 
     second_pack, second_half = packed(
-        "pack_second", second_ids, [cross_query_w, cross_key_w, cross_value_w, out_w, cross_out_w], [own_rows // 2]
+        "pack_second", second_ids, [cross_query_w, cross_key_w, cross_value_w, out_w, cross_out_w], [own_rows // 2], 4
     )
     (third_ids,) = all_after((ids,), (second_pack,))
     part = 3 * own_rows // 8
     third_pack, third_part, third_rest = packed(
-        "pack_third", third_ids, [gate_w, up_w, down_w], [part, own_rows - 2 * part]
+        "pack_third", third_ids, [gate_w, up_w, down_w], [part, own_rows - 2 * part], 2
     )
     first_far, second_far = hop(first_pack, "fsdp", 2), hop(second_half, "fsdp", 2)
     (first_far,) = all_after((first_far,), (third_pack,))
@@ -750,7 +752,7 @@
         (second_far, second_pack, third_pack, third_part, third_rest), (aux,)
     )
     third_far = hop(third_part, "fsdp", 2)
-    second_other = hop(second_far, "rep", 1)
+    second_other = hop(second_far, "rep", 2)
     rest_far = hop(third_rest, "fsdp", 2)
     cot_far = hop(cot_own, "fsdp", 2)
     seconds = beside_split(second_pack, second_far, second_other)
@@ -832,7 +834,6 @@
     cross_sum = Sum("cross", cross_keep, cross_send, 2)
     sums = {"F": ff_sum, "C": cross_sum}
     done = ff_sum.fold((grad_hidden_one,))
-    done = cross_sum.fold((done,))
     (grad_mixed,) = all_after((grad_mixed,), (done,))
     grad_q, grad_kv, table_sums = call(
         self_backward,
@@ -844,6 +845,7 @@
     done = grad_q
     for turn in EARLY:
         done = sums[turn].fold((done,))
+    done = cross_sum.fold((done,))
     (late_ids,) = all_after((ids,), (done,))
     tokens_keep, tokens_send, self_keep, self_send = call(
         self_gradients,

time: 112 us -> 110 us (0.982)
  waiting for transfers between devices: 37.9 us -> 31.9 us
  starting transfers between devices: 34 us -> 38.2 us
    ppermute x15, waiting for transfers between devices: 19.2 us -> 14.6 us  [rep_hop(): return lax.ppermute(x, ('rep', 'fsdp'), pairs)]
    ppermute x15, starting transfers between devices: 19.4 us -> 23.7 us  [rep_hop(): return lax.ppermute(x, ('rep', 'fsdp'), pairs)]
    ppermute x23, waiting for transfers between devices: 18.8 us -> 17.3 us  [hop(): return lax.ppermute(x, axis, [(i, i ^ bits) for i in range(size)])]
  transfers between devices with their start and end apart: 38 -> 38, of which waited for: 17 -> 15; matrix products, arithmetic and copies ran while one was open for 3% -> 3% of each run, Pallas kernels for 25% -> 26%
where the time goes in v4:
time: 110 us
  starting transfers between devices  38.2 us (35%)
  Pallas kernels  35.7 us (32%)
  waiting for transfers between devices  31.9 us (29%)
  other arithmetic  2.19 us (2%)
    pallas_call x12, Pallas kernels, call(): pl.pallas_call(kernel, name=name, out_shape=[jax.ShapeDtypeStruct(s, d) f...  35.7 us
    ppermute x15, starting transfers between devices, rep_hop(): return lax.ppermute(x, ('rep', 'fsdp'), pairs)  23.7 us
    ppermute x23, waiting for transfers between devices, hop(): return lax.ppermute(x, axis, [(i, i ^ bits) for i in range(size)])  17.3 us
    ppermute x15, waiting for transfers between devices, rep_hop(): return lax.ppermute(x, ('rep', 'fsdp'), pairs)  14.6 us
    ppermute x23, starting transfers between devices, hop(): return lax.ppermute(x, axis, [(i, i ^ bits) for i in range(size)])  14.5 us
  transfers between devices with their start and end apart: 38, of which 15 were waited for; matrix products, arithmetic and copies ran while one was open for 3% of the time, Pallas kernels for 26%

profile of v4, /device:TPU:0, one launch (start us, length us, event | category | flops | bytes accessed | tf_op | source)
XLA Modules:
  0.0 109.8 jit_solution(9347824643333269521)
XLA Ops:
  0.7 1.9 %pack_first.1.w0 = bf16[128,2048]{1,0:T(8,128)(2,1)} custom-call(bf16[128,512]{1,0:T(8,128)(2,1)} %bitcast.22, bf16[128,384]{1,0:T(8,128)(2,1)} %q_ref.1, bf16[128,384]{1,0:T(8,128)(2,1)} %k_ref.1, bf16[128,384]{1,0:T(8,128)(2,1)} %v_ref.1, bf16[64,512]{1,0:T(8,128)(2,1)} %bitcast.23, bf16[1,128]{1,0:T(2,128)(2,1)} %bitcast.24, bf16[1,128]{1,0:T(2,128)(2,1)} %bitcast.25, ...), custom_call_target="tpu_custom_call" | custom-call | flops 1 | bytes 1 | tf_op jit(solution)/shard_map/pack_first/pallas_call | solution.py:573
  2.6 3.0 %collective-permute-start.2 = (bf16[128,2048]{1,0:T(8,128)(2,1)}, bf16[128,2048]{1,0:T(8,128)(2,1)S(1)}, u32[]{:S(2)}, u32[]{:S(2)}) collective-permute-start(bf16[128,2048]{1,0:T(8,128)(2,1)} %pack_first.1.w0), channel_id=1, source_target_pairs={{0,2},{1,3},{2,0},{3,1},{4,6},{5,7},{6,4},{7,5},{8,10},{9,11},{10,... | collective-permute-start | bytes 1572872 | tf_op jit(solution)/shard_map/ppermute | solution.py:587
  6.2 2.7 %pack_second.1 = (bf16[128,1920]{1,0:T(8,128)(2,1)}, bf16[64,1920]{1,0:T(8,128)(2,1)}) custom-call(s32[5]{0:T(128)} %stack.23.ids_ref, bf16[128,384]{1,0:T(8,128)(2,1)} %refs_0_.2, bf16[128,384]{1,0:T(8,128)(2,1)} %refs_1_.2, bf16[128,384]{1,0:T(8,128)(2,1)} %refs_2_.2, bf16[384,128]{1,0:T(8,128)(2,1)} %refs_3_.1, bf16[384,128]{1,0:T(8,128)(2,1)} %refs_4_.1), custom_call_target="tpu_custom_call" | custom-call | flops 1 | bytes 1 | tf_op jit(solution)/shard_map/pack_second/pallas_call | solution.py:573
  9.0 3.0 %pack_third.1 = (bf16[128,3072]{1,0:T(8,128)(2,1)}, bf16[48,3072]{1,0:T(8,128)(2,1)}, bf16[32,3072]{1,0:T(8,128)(2,1)}) custom-call(s32[5]{0:T(128)} %stack.23.ids_ref, bf16[128,1024]{1,0:T(8,128)(2,1)} %refs_0_.3, bf16[128,1024]{1,0:T(8,128)(2,1)} %refs_1_.3, bf16[256,512]{1,0:T(8,128)(2,1)} %refs_2_.3), custom_call_target="tpu_custom_call" | custom-call | flops 1 | bytes 1 | tf_op jit(solution)/shard_map/pack_third/pallas_call | solution.py:573
  12.1 5.7 %collective-permute-done.2.w2 = bf16[128,2048]{1,0:T(8,128)(2,1)S(1)} collective-permute-done((bf16[128,2048]{1,0:T(8,128)(2,1)}, bf16[128,2048]{1,0:T(8,128)(2,1)S(1)}, u32[]{:S(2)}, u32[]{:S(2)}) %collective-permute-start.2) | collective-permute-done | bytes 524320 | tf_op jit(solution)/shard_map/ppermute | solution.py:587
  17.8 1.7 %collective-permute-start = (bf16[64,1920]{1,0:T(8,128)(2,1)S(1)}, bf16[64,1920]{1,0:T(8,128)(2,1)S(1)}, u32[]{:S(2)}, u32[]{:S(2)}) collective-permute-start(bf16[64,1920]{1,0:T(8,128)(2,1)S(1)} %copy-done.6), channel_id=1, source_target_pairs={{0,2},{1,3},{2,0},{3,1},{4,6},{5,7},{6,4},{7,5},{8,10},{9,11},{10,... | collective-permute-start | bytes 737288 | tf_op jit(solution)/shard_map/ppermute | solution.py:587
  19.9 4.4 %self_forward.1 = (bf16[512,512]{1,0:T(8,128)(2,1)S(1)}, bf16[256,512]{1,0:T(8,128)(2,1)S(1)}, bf16[512,512]{1,0:T(8,128)(2,1)S(1)}, bf16[256,384]{1,0:T(8,128)(...) custom-call(s32[5]{0:T(128)S(1)} %copy-done.4, ...), custom_call_target="tpu_custom_call" | custom-call | flops 1 | bytes 1 | tf_op jit(solution)/shard_map/self_forward/pallas_call | solution.py:573
  24.3 2.3 %collective-permute-done.w2 = bf16[64,1920]{1,0:T(8,128)(2,1)S(1)} collective-permute-done((bf16[64,1920]{1,0:T(8,128)(2,1)S(1)}, bf16[64,1920]{1,0:T(8,128)(2,1)S(1)}, u32[]{:S(2)}, u32[]{:S(2)}) %collective-permute-start) | collective-permute-done | bytes 245792 | tf_op jit(solution)/shard_map/ppermute | solution.py:587
  26.5 1.7 %collective-permute-start.4 = (bf16[48,3072]{1,0:T(8,128)(2,1)S(1)}, bf16[48,3072]{1,0:T(8,128)(2,1)S(1)}, u32[]{:S(2)}, u32[]{:S(2)}) collective-permute-start(bf16[48,3072]{1,0:T(8,128)(2,1)S(1)} %copy-done.5), channel_id=1, source_target_pairs={{0,2},{1,3},{2,0},{3,1},{4,6},{5,7},{6,4},{7,5},{8,10},{9,11},{10,... | collective-permute-start | bytes 884744 | tf_op jit(solution)/shard_map/ppermute | solution.py:587
  29.3 1.8 %collective-permute-start.8 = (bf16[64,1920]{1,0:T(8,128)(2,1)S(1)}, bf16[64,1920]{1,0:T(8,128)(2,1)S(1)}, u32[]{:S(2)}, u32[]{:S(2)}) collective-permute-start(bf16[64,1920]{1,0:T(8,128)(2,1)S(1)} %collective-permute-done.w2), channel_id=1, source_target_pairs={{0,8},{4,12},{8,0},{12,4},{16,24},{20,28},{24,16},{28,20},{1,9},{5... | collective-permute-start | bytes 737288 | tf_op jit(solution)/shard_map/ppermute | solution.py:587
  31.9 3.4 %collective-permute-done.4.g2 = bf16[48,3072]{1,0:T(8,128)(2,1)S(1)} collective-permute-done((bf16[48,3072]{1,0:T(8,128)(2,1)S(1)}, bf16[48,3072]{1,0:T(8,128)(2,1)S(1)}, u32[]{:S(2)}, u32[]{:S(2)}) %collective-permute-start.4) | collective-permute-done | bytes 294944 | tf_op jit(solution)/shard_map/ppermute | solution.py:587
  35.3 1.8 %collective-permute-start.12 = (bf16[48,3072]{1,0:T(8,128)(2,1)S(1)}, bf16[48,3072]{1,0:T(8,128)(2,1)S(1)}, u32[]{:S(2)}, u32[]{:S(2)}) collective-permute-start(bf16[48,3072]{1,0:T(8,128)(2,1)S(1)} %collective-permute-done.4.g2), channel_id=1, source_target_pairs={{0,4},{4,0},{8,12},{12,8},{16,20},{20,16},{24,28},{28,24},{1,5},{5... | collective-permute-start | bytes 884744 | tf_op jit(solution)/shard_map/ppermute | solution.py:587
  37.8 1.7 %collective-permute-start.13 = (bf16[32,3072]{1,0:T(8,128)(2,1)S(1)}, bf16[32,3072]{1,0:T(8,128)(2,1)S(1)}, u32[]{:S(2)}, u32[]{:S(2)}) collective-permute-start(bf16[32,3072]{1,0:T(8,128)(2,1)S(1)} %copy-done.7), channel_id=1, source_target_pairs={{0,2},{1,3},{2,0},{3,1},{4,6},{5,7},{6,4},{7,5},{8,10},{9,11},{10,... | collective-permute-start | bytes 589832 | tf_op jit(solution)/shard_map/ppermute | solution.py:587
  39.5 2.9 %cross_forward.1 = (f32[256,512]{1,0:T(8,128)S(1)}, bf16[256,512]{1,0:T(8,128)(2,1)S(1)}, bf16[256,384]{1,0:T(8,128)(2,1)S(1)}, bf16[256,768]{1,0:T(8,128)(2,1)S...) custom-call(s32[5]{0:T(128)S(1)} %copy-done.4, ...), custom_call_target="tpu_custom_call" | custom-call | flops 1 | bytes 1 | tf_op jit(solution)/shard_map/cross_forward/pallas_call | solution.py:573
  42.5 2.6 %collective-permute-done.13.g4 = bf16[32,3072]{1,0:T(8,128)(2,1)S(1)} collective-permute-done((bf16[32,3072]{1,0:T(8,128)(2,1)S(1)}, bf16[32,3072]{1,0:T(8,128)(2,1)S(1)}, u32[]{:S(2)}, u32[]{:S(2)}) %collective-permute-start.13) | collective-permute-done | bytes 196640 | tf_op jit(solution)/shard_map/ppermute | solution.py:587
  47.6 4.0 %feed_forward.1 = (bf16[128,512]{1,0:T(8,128)(2,1)}, f32[256,512]{1,0:T(8,128)S(1)}, bf16[128,3072]{1,0:T(8,128)(2,1)S(1)}, bf16[128,3072]{1,0:T(8,128)(2,1)S(1)}, f32[8,512]{1,0:T(8,128)S(1)}) custom-call(s32[5]{0:T(128)S(1)} %copy-done.4, f32[256,512]{1,0:T(8,128)S(1)} %get-tuple-element.146.h2_ref, bf16[256,512]{1,0:T(8,128)(2,1)S(1)} %get-tuple-element.147.n3_ref, ...), custom_call_target="tpu_custom_call" | custom-call | flops 1 | bytes 1 | tf_op jit(solution)/shard_map/feed_forward/pallas_call | solution.py:573
  51.7 3.8 %cross_backward.1 = (f32[256,512]{1,0:T(8,128)S(1)}, bf16[256,384]{1,0:T(8,128)(2,1)S(1)}, f32[64,512]{1,0:T(8,128)S(1)}, f32[64,512]{1,0:T(8,128)S(1)}, bf16[12...) custom-call(s32[5]{0:T(128)S(1)} %copy-done.4, ...), custom_call_target="tpu_custom_call" | custom-call | flops 1 | bytes 1 | tf_op jit(solution)/shard_map/cross_backward/pallas_call | solution.py:573
  55.8 1.8 %collective-permute-start.20 = (bf16[64,3072]{1,0:T(8,128)(2,1)S(1)}, bf16[64,3072]{1,0:T(8,128)(2,1)S(1)}, u32[]{:S(2)}, u32[]{:S(2)}) collective-permute-start(bf16[64,3072]{1,0:T(8,128)(2,1)S(1)} %get-tuple-element.240), channel_id=1, source_target_pairs={{0,4},{1,9},{2,6},{3,11},{4,0},{5,13},{6,2},{7,15},{8,12},{9,1},{1... | collective-permute-start | bytes 1179656 | tf_op jit(solution)/shard_map/ppermute | solution.py:606
  57.7 6.0 %self_backward.1 = (bf16[256,384]{1,0:T(8,128)(2,1)S(1)}, bf16[512,768]{1,0:T(8,128)(2,1)S(1)}, f32[128,128]{1,0:T(8,128)S(1)}) custom-call(s32[5]{0:T(128)S(1)} %copy-done.4, bf16[256,384]{1,0:T(8,128)(2,1)S(1)} %get-tuple-element.169.mix_ref, bf16[256,384]{1,0:T(8,128)(2,1)S(1)} %get-tuple-element.170.q_ref, ...), custom_call_target="tpu_custom_call" | custom-call | flops 1 | bytes 1 | tf_op jit(solution)/shard_map/self_backward/pallas_call | solution.py:573
  63.9 1.7 %collective-permute-start.22 = (bf16[32,3072]{1,0:T(8,128)(2,1)S(1)}, bf16[32,3072]{1,0:T(8,128)(2,1)S(1)}, u32[]{:S(2)}, u32[]{:S(2)}) collective-permute-start(bf16[32,3072]{1,0:T(8,128)(2,1)S(1)} %get-tuple-element.244), channel_id=1, source_target_pairs={{0,8},{1,5},{2,10},{3,7},{4,12},{5,1},{6,14},{7,3},{8,0},{9,13},{1... | collective-permute-start | bytes 589832 | tf_op jit(solution)/shard_map/ppermute | solution.py:606
  65.8 2.2 %self_gradients.1 = (f32[128,512]{1,0:T(8,128)S(1)}, f32[128,512]{1,0:T(8,128)S(1)}, bf16[128,1280]{1,0:T(8,128)(2,1)S(1)}, bf16[128,1280]{1,0:T(8,128)(2,1)S(1)}) custom-call(s32[5]{0:T(128)S(1)} %copy-done.4, f32[256,512]{1,0:T(8,128)S(1)} %get-tuple-element.165.grad_h1_ref, bf16[512,512]{1,0:T(8,128)(2,1)S(1)} %get-tuple-element.141.x_ref, ...), custom_call_target="tpu_custom_call" | custom-call | flops 1 | bytes 1 | tf_op jit(solution)/shard_map/self_gradients/pallas_call | solution.py:573
  67.9 1.6 %collective-permute-start.26 = (bf16[64,1920]{1,0:T(8,128)(2,1)S(1)}, bf16[64,1920]{1,0:T(8,128)(2,1)S(1)}, u32[]{:S(2)}, u32[]{:S(2)}) collective-permute-start(bf16[64,1920]{1,0:T(8,128)(2,1)S(1)} %get-tuple-element.242), channel_id=1, source_target_pairs={{0,4},{1,9},{2,6},{3,11},{4,0},{5,13},{6,2},{7,15},{8,12},{9,1},{1... | collective-permute-start | bytes 737288 | tf_op jit(solution)/shard_map/ppermute | solution.py:606
  69.7 2.7 %collective-permute-start.28 = (bf16[32,3072]{1,0:T(8,128)(2,1)S(1)}, bf16[32,3072]{1,0:T(8,128)(2,1)S(1)}, u32[]{:S(2)}, u32[]{:S(2)}) collective-permute-start(bf16[32,3072]{1,0:T(8,128)(2,1)S(1)} %add_convert_fusion.6), channel_id=1, source_target_pairs={{0,16},{1,17},{2,18},{3,19},{4,20},{5,21},{6,22},{7,23},{8,24},{9,... | collective-permute-start | bytes 589832 | tf_op jit(solution)/shard_map/ppermute | solution.py:606
  72.5 1.7 %collective-permute-done.26 = bf16[64,1920]{1,0:T(8,128)(2,1)S(1)} collective-permute-done((bf16[64,1920]{1,0:T(8,128)(2,1)S(1)}, bf16[64,1920]{1,0:T(8,128)(2,1)S(1)}, u32[]{:S(2)}, u32[]{:S(2)}) %collective-permute-start.26) | collective-permute-done | bytes 245792 | tf_op jit(solution)/shard_map/ppermute | solution.py:606
  76.6 5.6 %collective-permute-done.28 = bf16[32,3072]{1,0:T(8,128)(2,1)S(1)} collective-permute-done((bf16[32,3072]{1,0:T(8,128)(2,1)S(1)}, bf16[32,3072]{1,0:T(8,128)(2,1)S(1)}, u32[]{:S(2)}, u32[]{:S(2)}) %collective-permute-start.28) | collective-permute-done | bytes 196640 | tf_op jit(solution)/shard_map/ppermute | solution.py:606
  83.4 2.2 %collective-permute-start.31 = (bf16[32,1920]{1,0:T(8,128)(2,1)S(1)}, bf16[32,1920]{1,0:T(8,128)(2,1)S(1)}, u32[]{:S(2)}, u32[]{:S(2)}) collective-permute-start(bf16[32,1920]{1,0:T(8,128)(2,1)S(1)} %add_convert_fusion.9), channel_id=1, source_target_pairs={{0,16},{1,17},{2,18},{3,19},{4,20},{5,21},{6,22},{7,23},{8,24},{9,... | collective-permute-start | bytes 368648 | tf_op jit(solution)/shard_map/ppermute | solution.py:606
  86.7 4.3 %collective-permute-done.29 = bf16[32,1280]{1,0:T(8,128)(2,1)S(1)} collective-permute-done((bf16[32,1280]{1,0:T(8,128)(2,1)S(1)}, bf16[32,1280]{1,0:T(8,128)(2,1)S(1)}, u32[]{:S(2)}, u32[]{:S(2)}) %collective-permute-start.29) | collective-permute-done | bytes 81952 | tf_op jit(solution)/shard_map/ppermute | solution.py:606
  93.3 2.9 %collective-permute-start.34 = (bf16[32,1920]{1,0:T(8,128)(2,1)S(1)}, bf16[32,1920]{1,0:T(8,128)(2,1)S(1)}, u32[]{:S(2)}, u32[]{:S(2)}) collective-permute-start(bf16[32,1920]{1,0:T(8,128)(2,1)S(1)} %add_convert_fusion.8), channel_id=1, source_target_pairs={{0,8},{1,5},{2,10},{3,7},{4,12},{5,1},{6,14},{7,3},{8,0},{9,13},{1... | collective-permute-start | bytes 368648 | tf_op jit(solution)/shard_map/ppermute | solution.py:606
  96.6 2.4 %collective-permute-start.33 = (bf16[32,1280]{1,0:T(8,128)(2,1)S(1)}, bf16[32,1280]{1,0:T(8,128)(2,1)S(1)}, u32[]{:S(2)}, u32[]{:S(2)}) collective-permute-start(bf16[32,1280]{1,0:T(8,128)(2,1)S(1)} %add_convert_fusion.10), channel_id=1, source_target_pairs={{0,8},{1,5},{2,10},{3,7},{4,12},{5,1},{6,14},{7,3},{8,0},{9,13},{1... | collective-permute-start | bytes 245768 | tf_op jit(solution)/shard_map/ppermute | solution.py:606
  100.4 2.1 %collective-permute-start.36 = (bf16[64,1920]{1,0:T(8,128)(2,1)S(1)}, bf16[64,1920]{1,0:T(8,128)(2,1)S(1)}, u32[]{:S(2)}, u32[]{:S(2)}) collective-permute-start(bf16[64,1920]{1,0:T(8,128)(2,1)S(1)} %constant_dynamic-update-slice_fusion.2.low_ref), channel_id=1, source_target_pairs={{0,4},{1,9},{2,6},{3,11},{4,0},{5,13},{6,2},{7,15},{8,12},{9,1},{1... | collective-permute-start | bytes 737288 | tf_op jit(solution)/shard_map/ppermute | solution.py:606
  102.5 1.7 %collective-permute-start.35 = (bf16[64,1280]{1,0:T(8,128)(2,1)S(1)}, bf16[64,1280]{1,0:T(8,128)(2,1)S(1)}, u32[]{:S(2)}, u32[]{:S(2)}) collective-permute-start(bf16[64,1280]{1,0:T(8,128)(2,1)S(1)} %constant_dynamic-update-slice_fusion.4.low_ref), channel_id=1, source_target_pairs={{0,4},{1,9},{2,6},{3,11},{4,0},{5,13},{6,2},{7,15},{8,12},{9,1},{1... | collective-permute-start | bytes 491528 | tf_op jit(solution)/shard_map/ppermute | solution.py:606
  105.0 1.8 %unpack_feed.1 = (f32[128,1024]{1,0:T(8,128)}, f32[128,1024]{1,0:T(8,128)}, f32[256,512]{1,0:T(8,128)}) custom-call(s32[5]{0:T(128)S(1)} %copy-done.4, bf16[64,3072]{1,0:T(8,128)(2,1)S(1)} %constant_dynamic-update-slice_fusion.low_ref, bf16[64,3072]{1,0:T(8,128)(2,1)S(1)} %collective-permute-done.37.high_ref), custom_call_target="tpu_custom_call" | custom-call | flops 1 | bytes 1 | tf_op jit(solution)/shard_map/unpack_feed/pallas_call | solution.py:573
  (99 shorter events, 19.6 us)
Async XLA Ops:
  2.6 15.1 %collective-permute-start.2 = (bf16[128,2048]{1,0:T(8,128)(2,1)}, bf16[128,2048]{1,0:T(8,128)(2,1)S(1)}, u32[]{:S(2)}, u32[]{:S(2)}) collective-permute-start(bf16[128,2048]{1,0:T(8,128)(2,1)} %pack_first.1.w0), channel_id=1, source_target_pairs={{0,2},{1,3},{2,0},{3,1},{4,6},{5,7},{6,4},{7,5},{8,10},{9,11},{10,... | collective-permute-start | bytes 1572872 | tf_op jit(solution)/shard_map/ppermute | solution.py:587
  5.6 14.3 %collective-permute-start.1 = (bf16[128,2048]{1,0:T(8,128)(2,1)}, bf16[128,2048]{1,0:T(8,128)(2,1)S(1)}, u32[]{:S(2)}, u32[]{:S(2)}) collective-permute-start(bf16[128,2048]{1,0:T(8,128)(2,1)} %pack_first.1.w0), channel_id=1, source_target_pairs={{0,1},{1,0},{2,3},{3,2},{4,5},{5,4},{6,7},{7,6},{8,9},{9,8},{10,11... | collective-permute-start | bytes 1572872 | tf_op jit(solution)/shard_map/ppermute | solution.py:587
  17.8 8.8 %collective-permute-start = (bf16[64,1920]{1,0:T(8,128)(2,1)S(1)}, bf16[64,1920]{1,0:T(8,128)(2,1)S(1)}, u32[]{:S(2)}, u32[]{:S(2)}) collective-permute-start(bf16[64,1920]{1,0:T(8,128)(2,1)S(1)} %copy-done.6), channel_id=1, source_target_pairs={{0,2},{1,3},{2,0},{3,1},{4,6},{5,7},{6,4},{7,5},{8,10},{9,11},{10,... | collective-permute-start | bytes 737288 | tf_op jit(solution)/shard_map/ppermute | solution.py:587
  19.6 9.8 %collective-permute-start.5 = (bf16[128,512]{1,0:T(8,128)(2,1)S(1)}, bf16[128,512]{1,0:T(8,128)(2,1)S(1)}, u32[]{:S(2)}, u32[]{:S(2)}) collective-permute-start(bf16[128,512]{1,0:T(8,128)(2,1)S(1)} %bitcast.19), channel_id=1, source_target_pairs={{0,2},{1,3},{2,0},{3,1},{4,6},{5,7},{6,4},{7,5},{8,10},{9,11},{10,... | collective-permute-start | bytes 393224 | tf_op jit(solution)/shard_map/ppermute | solution.py:587
  26.5 8.7 %collective-permute-start.4 = (bf16[48,3072]{1,0:T(8,128)(2,1)S(1)}, bf16[48,3072]{1,0:T(8,128)(2,1)S(1)}, u32[]{:S(2)}, u32[]{:S(2)}) collective-permute-start(bf16[48,3072]{1,0:T(8,128)(2,1)S(1)} %copy-done.5), channel_id=1, source_target_pairs={{0,2},{1,3},{2,0},{3,1},{4,6},{5,7},{6,4},{7,5},{8,10},{9,11},{10,... | collective-permute-start | bytes 884744 | tf_op jit(solution)/shard_map/ppermute | solution.py:587
  29.3 8.4 %collective-permute-start.8 = (bf16[64,1920]{1,0:T(8,128)(2,1)S(1)}, bf16[64,1920]{1,0:T(8,128)(2,1)S(1)}, u32[]{:S(2)}, u32[]{:S(2)}) collective-permute-start(bf16[64,1920]{1,0:T(8,128)(2,1)S(1)} %collective-permute-done.w2), channel_id=1, source_target_pairs={{0,8},{4,12},{8,0},{12,4},{16,24},{20,28},{24,16},{28,20},{1,9},{5... | collective-permute-start | bytes 737288 | tf_op jit(solution)/shard_map/ppermute | solution.py:587
  31.2 8.4 %collective-permute-start.7 = (bf16[128,1920]{1,0:T(8,128)(2,1)S(1)}, bf16[128,1920]{1,0:T(8,128)(2,1)S(1)}, u32[]{:S(2)}, u32[]{:S(2)}) collective-permute-start(bf16[128,1920]{1,0:T(8,128)(2,1)S(1)} %copy-done.1), channel_id=1, source_target_pairs={{0,1},{1,0},{2,3},{3,2},{4,5},{5,4},{6,7},{7,6},{8,9},{9,8},{10,11... | collective-permute-start | bytes 1474568 | tf_op jit(solution)/shard_map/ppermute | solution.py:587
  31.4 16.2 %collective-permute-start.11 = (bf16[128,3072]{1,0:T(8,128)(2,1)S(1)}, bf16[128,3072]{1,0:T(8,128)(2,1)S(1)}, u32[]{:S(2)}, u32[]{:S(2)}) collective-permute-start(bf16[128,3072]{1,0:T(8,128)(2,1)S(1)} %copy-done.2), channel_id=1, source_target_pairs={{0,1},{1,0},{2,3},{3,2},{4,5},{5,4},{6,7},{7,6},{8,9},{9,8},{10,11... | collective-permute-start | bytes 2359304 | tf_op jit(solution)/shard_map/ppermute | solution.py:587
  31.7 6.1 %collective-permute-start.9 = (bf16[64,1920]{1,0:T(8,128)(2,1)S(1)}, bf16[64,1920]{1,0:T(8,128)(2,1)S(1)}, u32[]{:S(2)}, u32[]{:S(2)}) collective-permute-start(bf16[64,1920]{1,0:T(8,128)(2,1)S(1)} %collective-permute-done.w2), channel_id=1, source_target_pairs={{0,1},{1,0},{2,3},{3,2},{4,5},{5,4},{6,7},{7,6},{8,9},{9,8},{10,11... | collective-permute-start | bytes 737288 | tf_op jit(solution)/shard_map/ppermute | solution.py:587
  35.3 9.8 %collective-permute-start.12 = (bf16[48,3072]{1,0:T(8,128)(2,1)S(1)}, bf16[48,3072]{1,0:T(8,128)(2,1)S(1)}, u32[]{:S(2)}, u32[]{:S(2)}) collective-permute-start(bf16[48,3072]{1,0:T(8,128)(2,1)S(1)} %collective-permute-done.4.g2), channel_id=1, source_target_pairs={{0,4},{4,0},{8,12},{12,8},{16,20},{20,16},{24,28},{28,24},{1,5},{5... | collective-permute-start | bytes 884744 | tf_op jit(solution)/shard_map/ppermute | solution.py:587
  37.8 7.3 %collective-permute-start.13 = (bf16[32,3072]{1,0:T(8,128)(2,1)S(1)}, bf16[32,3072]{1,0:T(8,128)(2,1)S(1)}, u32[]{:S(2)}, u32[]{:S(2)}) collective-permute-start(bf16[32,3072]{1,0:T(8,128)(2,1)S(1)} %copy-done.7), channel_id=1, source_target_pairs={{0,2},{1,3},{2,0},{3,1},{4,6},{5,7},{6,4},{7,5},{8,10},{9,11},{10,... | collective-permute-start | bytes 589832 | tf_op jit(solution)/shard_map/ppermute | solution.py:587
  45.1 2.5 %collective-permute-start.15 = (bf16[48,3072]{1,0:T(8,128)(2,1)S(1)}, bf16[48,3072]{1,0:T(8,128)(2,1)S(1)}, u32[]{:S(2)}, u32[]{:S(2)}) collective-permute-start(bf16[48,3072]{1,0:T(8,128)(2,1)S(1)} %collective-permute-done.12.g3), channel_id=1, source_target_pairs={{0,1},{1,0},{2,3},{3,2},{4,5},{5,4},{6,7},{7,6},{8,9},{9,8},{10,11... | collective-permute-start | bytes 884744 | tf_op jit(solution)/shard_map/ppermute | solution.py:587
  51.6 4.0 %collective-permute-start.19 = (bf16[128,3072]{1,0:T(8,128)(2,1)S(1)}, bf16[128,3072]{1,0:T(8,128)(2,1)S(1)}, u32[]{:S(2)}, u32[]{:S(2)}) collective-permute-start(bf16[128,3072]{1,0:T(8,128)(2,1)S(1)} %get-tuple-element.164), channel_id=1, source_target_pairs={{0,1},{1,0},{2,3},{3,2},{4,5},{5,4},{6,7},{7,6},{8,9},{9,8},{10,11... | collective-permute-start | bytes 2359304 | tf_op jit(solution)/shard_map/ppermute | solution.py:587
  55.8 8.0 %collective-permute-start.20 = (bf16[64,3072]{1,0:T(8,128)(2,1)S(1)}, bf16[64,3072]{1,0:T(8,128)(2,1)S(1)}, u32[]{:S(2)}, u32[]{:S(2)}) collective-permute-start(bf16[64,3072]{1,0:T(8,128)(2,1)S(1)} %get-tuple-element.240), channel_id=1, source_target_pairs={{0,4},{1,9},{2,6},{3,11},{4,0},{5,13},{6,2},{7,15},{8,12},{9,1},{1... | collective-permute-start | bytes 1179656 | tf_op jit(solution)/shard_map/ppermute | solution.py:606
  57.6 6.3 %collective-permute-start.18 = (bf16[128,1920]{1,0:T(8,128)(2,1)S(1)}, bf16[128,1920]{1,0:T(8,128)(2,1)S(1)}, u32[]{:S(2)}, u32[]{:S(2)}) collective-permute-start(bf16[128,1920]{1,0:T(8,128)(2,1)S(1)} %get-tuple-element.162), channel_id=1, source_target_pairs={{0,1},{1,0},{2,3},{3,2},{4,5},{5,4},{6,7},{7,6},{8,9},{9,8},{10,11... | collective-permute-start | bytes 1474568 | tf_op jit(solution)/shard_map/ppermute | solution.py:587
  63.9 5.7 %collective-permute-start.22 = (bf16[32,3072]{1,0:T(8,128)(2,1)S(1)}, bf16[32,3072]{1,0:T(8,128)(2,1)S(1)}, u32[]{:S(2)}, u32[]{:S(2)}) collective-permute-start(bf16[32,3072]{1,0:T(8,128)(2,1)S(1)} %get-tuple-element.244), channel_id=1, source_target_pairs={{0,8},{1,5},{2,10},{3,7},{4,12},{5,1},{6,14},{7,3},{8,0},{9,13},{1... | collective-permute-start | bytes 589832 | tf_op jit(solution)/shard_map/ppermute | solution.py:606
  67.9 6.3 %collective-permute-start.26 = (bf16[64,1920]{1,0:T(8,128)(2,1)S(1)}, bf16[64,1920]{1,0:T(8,128)(2,1)S(1)}, u32[]{:S(2)}, u32[]{:S(2)}) collective-permute-start(bf16[64,1920]{1,0:T(8,128)(2,1)S(1)} %get-tuple-element.242), channel_id=1, source_target_pairs={{0,4},{1,9},{2,6},{3,11},{4,0},{5,13},{6,2},{7,15},{8,12},{9,1},{1... | collective-permute-start | bytes 737288 | tf_op jit(solution)/shard_map/ppermute | solution.py:606
  69.5 2.9 %collective-permute-start.21 = (bf16[128,1280]{1,0:T(8,128)(2,1)S(1)}, bf16[128,1280]{1,0:T(8,128)(2,1)S(1)}, u32[]{:S(2)}, u32[]{:S(2)}) collective-permute-start(bf16[128,1280]{1,0:T(8,128)(2,1)S(1)} %get-tuple-element.191), channel_id=1, source_target_pairs={{0,1},{1,0},{2,3},{3,2},{4,5},{5,4},{6,7},{7,6},{8,9},{9,8},{10,11... | collective-permute-start | bytes 983048 | tf_op jit(solution)/shard_map/ppermute | solution.py:587
  69.7 12.5 %collective-permute-start.28 = (bf16[32,3072]{1,0:T(8,128)(2,1)S(1)}, bf16[32,3072]{1,0:T(8,128)(2,1)S(1)}, u32[]{:S(2)}, u32[]{:S(2)}) collective-permute-start(bf16[32,3072]{1,0:T(8,128)(2,1)S(1)} %add_convert_fusion.6), channel_id=1, source_target_pairs={{0,16},{1,17},{2,18},{3,19},{4,20},{5,21},{6,22},{7,23},{8,24},{9,... | collective-permute-start | bytes 589832 | tf_op jit(solution)/shard_map/ppermute | solution.py:606
  74.3 9.1 %collective-permute-start.27 = (bf16[32,1920]{1,0:T(8,128)(2,1)S(1)}, bf16[32,1920]{1,0:T(8,128)(2,1)S(1)}, u32[]{:S(2)}, u32[]{:S(2)}) collective-permute-start(bf16[32,1920]{1,0:T(8,128)(2,1)S(1)} %get-tuple-element.248), channel_id=1, source_target_pairs={{0,8},{1,5},{2,10},{3,7},{4,12},{5,1},{6,14},{7,3},{8,0},{9,13},{1... | collective-permute-start | bytes 368648 | tf_op jit(solution)/shard_map/ppermute | solution.py:606
  74.7 11.3 %collective-permute-start.24 = (f32[64,512]{1,0:T(8,128)S(1)}, f32[64,512]{1,0:T(8,128)S(1)}, u32[]{:S(2)}, u32[]{:S(2)}) collective-permute-start(f32[64,512]{1,0:T(8,128)S(1)} %get-tuple-element.198), channel_id=1, source_target_pairs={{0,1},{1,0},{2,3},{3,2},{4,5},{5,4},{6,7},{7,6},{8,9},{9,8},{10,11... | collective-permute-start | bytes 393224 | tf_op jit(solution)/shard_map/ppermute | solution.py:587
  74.7 10.9 %collective-permute-start.25 = (bf16[64,1280]{1,0:T(8,128)(2,1)S(1)}, bf16[64,1280]{1,0:T(8,128)(2,1)S(1)}, u32[]{:S(2)}, u32[]{:S(2)}) collective-permute-start(bf16[64,1280]{1,0:T(8,128)(2,1)S(1)} %get-tuple-element.246), channel_id=1, source_target_pairs={{0,4},{1,9},{2,6},{3,11},{4,0},{5,13},{6,2},{7,15},{8,12},{9,1},{1... | collective-permute-start | bytes 491528 | tf_op jit(solution)/shard_map/ppermute | solution.py:606
  76.3 27.9 %collective-permute-start.23 = (f32[128,512]{1,0:T(8,128)S(1)}, f32[128,512]{1,0:T(8,128)S(1)}, u32[]{:S(2)}, u32[]{:S(2)}) collective-permute-start(f32[128,512]{1,0:T(8,128)S(1)} %get-tuple-element.196), channel_id=1, source_target_pairs={{0,1},{1,0},{2,3},{3,2},{4,5},{5,4},{6,7},{7,6},{8,9},{9,8},{10,11... | collective-permute-start | bytes 786440 | tf_op jit(solution)/shard_map/ppermute | solution.py:587
  82.2 10.3 %collective-permute-start.32 = (bf16[32,3072]{1,0:T(8,128)(2,1)S(1)}, bf16[32,3072]{1,0:T(8,128)(2,1)S(1)}, u32[]{:S(2)}, u32[]{:S(2)}) collective-permute-start(bf16[32,3072]{1,0:T(8,128)(2,1)S(1)} %add_convert_fusion.5), channel_id=1, source_target_pairs={{0,8},{1,5},{2,10},{3,7},{4,12},{5,1},{6,14},{7,3},{8,0},{9,13},{1... | collective-permute-start | bytes 589832 | tf_op jit(solution)/shard_map/ppermute | solution.py:606
  83.4 9.8 %collective-permute-start.31 = (bf16[32,1920]{1,0:T(8,128)(2,1)S(1)}, bf16[32,1920]{1,0:T(8,128)(2,1)S(1)}, u32[]{:S(2)}, u32[]{:S(2)}) collective-permute-start(bf16[32,1920]{1,0:T(8,128)(2,1)S(1)} %add_convert_fusion.9), channel_id=1, source_target_pairs={{0,16},{1,17},{2,18},{3,19},{4,20},{5,21},{6,22},{7,23},{8,24},{9,... | collective-permute-start | bytes 368648 | tf_op jit(solution)/shard_map/ppermute | solution.py:606
  85.8 5.3 %collective-permute-start.29 = (bf16[32,1280]{1,0:T(8,128)(2,1)S(1)}, bf16[32,1280]{1,0:T(8,128)(2,1)S(1)}, u32[]{:S(2)}, u32[]{:S(2)}) collective-permute-start(bf16[32,1280]{1,0:T(8,128)(2,1)S(1)} %get-tuple-element.250), channel_id=1, source_target_pairs={{0,8},{1,5},{2,10},{3,7},{4,12},{5,1},{6,14},{7,3},{8,0},{9,13},{1... | collective-permute-start | bytes 245768 | tf_op jit(solution)/shard_map/ppermute | solution.py:606
  91.1 5.5 %collective-permute-start.30 = (bf16[32,1280]{1,0:T(8,128)(2,1)S(1)}, bf16[32,1280]{1,0:T(8,128)(2,1)S(1)}, u32[]{:S(2)}, u32[]{:S(2)}) collective-permute-start(bf16[32,1280]{1,0:T(8,128)(2,1)S(1)} %add_convert_fusion.11), channel_id=1, source_target_pairs={{0,16},{1,17},{2,18},{3,19},{4,20},{5,21},{6,22},{7,23},{8,24},{9,... | collective-permute-start | bytes 245768 | tf_op jit(solution)/shard_map/ppermute | solution.py:606
  92.6 12.4 %collective-permute-start.37 = (bf16[64,3072]{1,0:T(8,128)(2,1)S(1)}, bf16[64,3072]{1,0:T(8,128)(2,1)S(1)}, u32[]{:S(2)}, u32[]{:S(2)}) collective-permute-start(bf16[64,3072]{1,0:T(8,128)(2,1)S(1)} %constant_dynamic-update-slice_fusion.low_ref), channel_id=1, source_target_pairs={{0,4},{1,9},{2,6},{3,11},{4,0},{5,13},{6,2},{7,15},{8,12},{9,1},{1... | collective-permute-start | bytes 1179656 | tf_op jit(solution)/shard_map/ppermute | solution.py:606
  93.3 7.1 %collective-permute-start.34 = (bf16[32,1920]{1,0:T(8,128)(2,1)S(1)}, bf16[32,1920]{1,0:T(8,128)(2,1)S(1)}, u32[]{:S(2)}, u32[]{:S(2)}) collective-permute-start(bf16[32,1920]{1,0:T(8,128)(2,1)S(1)} %add_convert_fusion.8), channel_id=1, source_target_pairs={{0,8},{1,5},{2,10},{3,7},{4,12},{5,1},{6,14},{7,3},{8,0},{9,13},{1... | collective-permute-start | bytes 368648 | tf_op jit(solution)/shard_map/ppermute | solution.py:606
  96.6 5.9 %collective-permute-start.33 = (bf16[32,1280]{1,0:T(8,128)(2,1)S(1)}, bf16[32,1280]{1,0:T(8,128)(2,1)S(1)}, u32[]{:S(2)}, u32[]{:S(2)}) collective-permute-start(bf16[32,1280]{1,0:T(8,128)(2,1)S(1)} %add_convert_fusion.10), channel_id=1, source_target_pairs={{0,8},{1,5},{2,10},{3,7},{4,12},{5,1},{6,14},{7,3},{8,0},{9,13},{1... | collective-permute-start | bytes 245768 | tf_op jit(solution)/shard_map/ppermute | solution.py:606
  100.4 6.3 %collective-permute-start.36 = (bf16[64,1920]{1,0:T(8,128)(2,1)S(1)}, bf16[64,1920]{1,0:T(8,128)(2,1)S(1)}, u32[]{:S(2)}, u32[]{:S(2)}) collective-permute-start(bf16[64,1920]{1,0:T(8,128)(2,1)S(1)} %constant_dynamic-update-slice_fusion.2.low_ref), channel_id=1, source_target_pairs={{0,4},{1,9},{2,6},{3,11},{4,0},{5,13},{6,2},{7,15},{8,12},{9,1},{1... | collective-permute-start | bytes 737288 | tf_op jit(solution)/shard_map/ppermute | solution.py:606
  102.5 5.9 %collective-permute-start.35 = (bf16[64,1280]{1,0:T(8,128)(2,1)S(1)}, bf16[64,1280]{1,0:T(8,128)(2,1)S(1)}, u32[]{:S(2)}, u32[]{:S(2)}) collective-permute-start(bf16[64,1280]{1,0:T(8,128)(2,1)S(1)} %constant_dynamic-update-slice_fusion.4.low_ref), channel_id=1, source_target_pairs={{0,4},{1,9},{2,6},{3,11},{4,0},{5,13},{6,2},{7,15},{8,12},{9,1},{1... | collective-permute-start | bytes 491528 | tf_op jit(solution)/shard_map/ppermute | solution.py:606
  (14 other events, 118.1 us)

commit v5 on v4

--- a/solution.py
+++ b/solution.py
@@ -21,7 +21,7 @@
 GROUP = 4
 PIECES = 4
 EARLY = "F"
-TURNS = "XFSTCFCSSFCSCS"
+TURNS = "XFSCFCSSFTCSCS"
 SELF_HALVINGS = 2
 SELF_ORDER = PIECES - (PIECES >> SELF_HALVINGS)
 VMEM_BYTES = 32 * 1024 * 1024

time: 110 us -> 109 us (level)
  waiting for transfers between devices: 31.9 us -> 30.5 us
    ppermute x15, waiting for transfers between devices: 14.6 us -> 13.2 us  [rep_hop(): return lax.ppermute(x, ('rep', 'fsdp'), pairs)]
  transfers between devices with their start and end apart: 38 -> 38, of which waited for: 15 -> 16; matrix products, arithmetic and copies ran while one was open for 3% -> 3% of each run, Pallas kernels for 26% -> 26%
where the time goes in v5:
time: 109 us
  starting transfers between devices  38.7 us (36%)
  Pallas kernels  35.7 us (33%)
  waiting for transfers between devices  30.5 us (28%)
  other arithmetic  2.2 us (2%)
    pallas_call x12, Pallas kernels, call(): pl.pallas_call(kernel, name=name, out_shape=[jax.ShapeDtypeStruct(s, d) f...  35.7 us
    ppermute x15, starting transfers between devices, rep_hop(): return lax.ppermute(x, ('rep', 'fsdp'), pairs)  23.9 us
    ppermute x23, waiting for transfers between devices, hop(): return lax.ppermute(x, axis, [(i, i ^ bits) for i in range(size)])  17.3 us
    ppermute x23, starting transfers between devices, hop(): return lax.ppermute(x, axis, [(i, i ^ bits) for i in range(size)])  14.7 us
    ppermute x15, waiting for transfers between devices, rep_hop(): return lax.ppermute(x, ('rep', 'fsdp'), pairs)  13.2 us
  transfers between devices with their start and end apart: 38, of which 16 were waited for; matrix products, arithmetic and copies ran while one was open for 3% of the time, Pallas kernels for 26%

profile of v5, /device:TPU:0, one launch (start us, length us, event | category | flops | bytes accessed | tf_op | source)
XLA Modules:
  0.0 108.9 jit_solution(17537216765540088508)
XLA Ops:
  0.7 1.9 %pack_first.1.w0 = bf16[128,2048]{1,0:T(8,128)(2,1)} custom-call(bf16[128,512]{1,0:T(8,128)(2,1)} %bitcast.22, bf16[128,384]{1,0:T(8,128)(2,1)} %q_ref.1, bf16[128,384]{1,0:T(8,128)(2,1)} %k_ref.1, bf16[128,384]{1,0:T(8,128)(2,1)} %v_ref.1, bf16[64,512]{1,0:T(8,128)(2,1)} %bitcast.23, bf16[1,128]{1,0:T(2,128)(2,1)} %bitcast.24, bf16[1,128]{1,0:T(2,128)(2,1)} %bitcast.25, ...), custom_call_target="tpu_custom_call" | custom-call | flops 1 | bytes 1 | tf_op jit(solution)/shard_map/pack_first/pallas_call | solution.py:573
  2.6 3.0 %collective-permute-start.2 = (bf16[128,2048]{1,0:T(8,128)(2,1)}, bf16[128,2048]{1,0:T(8,128)(2,1)S(1)}, u32[]{:S(2)}, u32[]{:S(2)}) collective-permute-start(bf16[128,2048]{1,0:T(8,128)(2,1)} %pack_first.1.w0), channel_id=1, source_target_pairs={{0,2},{1,3},{2,0},{3,1},{4,6},{5,7},{6,4},{7,5},{8,10},{9,11},{10,... | collective-permute-start | bytes 1572872 | tf_op jit(solution)/shard_map/ppermute | solution.py:587
  6.2 2.7 %pack_second.1 = (bf16[128,1920]{1,0:T(8,128)(2,1)}, bf16[64,1920]{1,0:T(8,128)(2,1)}) custom-call(s32[5]{0:T(128)} %stack.23.ids_ref, bf16[128,384]{1,0:T(8,128)(2,1)} %refs_0_.2, bf16[128,384]{1,0:T(8,128)(2,1)} %refs_1_.2, bf16[128,384]{1,0:T(8,128)(2,1)} %refs_2_.2, bf16[384,128]{1,0:T(8,128)(2,1)} %refs_3_.1, bf16[384,128]{1,0:T(8,128)(2,1)} %refs_4_.1), custom_call_target="tpu_custom_call" | custom-call | flops 1 | bytes 1 | tf_op jit(solution)/shard_map/pack_second/pallas_call | solution.py:573
  9.0 3.0 %pack_third.1 = (bf16[128,3072]{1,0:T(8,128)(2,1)}, bf16[48,3072]{1,0:T(8,128)(2,1)}, bf16[32,3072]{1,0:T(8,128)(2,1)}) custom-call(s32[5]{0:T(128)} %stack.23.ids_ref, bf16[128,1024]{1,0:T(8,128)(2,1)} %refs_0_.3, bf16[128,1024]{1,0:T(8,128)(2,1)} %refs_1_.3, bf16[256,512]{1,0:T(8,128)(2,1)} %refs_2_.3), custom_call_target="tpu_custom_call" | custom-call | flops 1 | bytes 1 | tf_op jit(solution)/shard_map/pack_third/pallas_call | solution.py:573
  12.1 5.7 %collective-permute-done.2.w2 = bf16[128,2048]{1,0:T(8,128)(2,1)S(1)} collective-permute-done((bf16[128,2048]{1,0:T(8,128)(2,1)}, bf16[128,2048]{1,0:T(8,128)(2,1)S(1)}, u32[]{:S(2)}, u32[]{:S(2)}) %collective-permute-start.2) | collective-permute-done | bytes 524320 | tf_op jit(solution)/shard_map/ppermute | solution.py:587
  17.8 1.7 %collective-permute-start = (bf16[64,1920]{1,0:T(8,128)(2,1)S(1)}, bf16[64,1920]{1,0:T(8,128)(2,1)S(1)}, u32[]{:S(2)}, u32[]{:S(2)}) collective-permute-start(bf16[64,1920]{1,0:T(8,128)(2,1)S(1)} %copy-done.6), channel_id=1, source_target_pairs={{0,2},{1,3},{2,0},{3,1},{4,6},{5,7},{6,4},{7,5},{8,10},{9,11},{10,... | collective-permute-start | bytes 737288 | tf_op jit(solution)/shard_map/ppermute | solution.py:587
  19.9 4.4 %self_forward.1 = (bf16[512,512]{1,0:T(8,128)(2,1)S(1)}, bf16[256,512]{1,0:T(8,128)(2,1)S(1)}, bf16[512,512]{1,0:T(8,128)(2,1)S(1)}, bf16[256,384]{1,0:T(8,128)(...) custom-call(s32[5]{0:T(128)S(1)} %copy-done.4, ...), custom_call_target="tpu_custom_call" | custom-call | flops 1 | bytes 1 | tf_op jit(solution)/shard_map/self_forward/pallas_call | solution.py:573
  24.3 2.3 %collective-permute-done.w2 = bf16[64,1920]{1,0:T(8,128)(2,1)S(1)} collective-permute-done((bf16[64,1920]{1,0:T(8,128)(2,1)S(1)}, bf16[64,1920]{1,0:T(8,128)(2,1)S(1)}, u32[]{:S(2)}, u32[]{:S(2)}) %collective-permute-start) | collective-permute-done | bytes 245792 | tf_op jit(solution)/shard_map/ppermute | solution.py:587
  26.5 1.7 %collective-permute-start.4 = (bf16[48,3072]{1,0:T(8,128)(2,1)S(1)}, bf16[48,3072]{1,0:T(8,128)(2,1)S(1)}, u32[]{:S(2)}, u32[]{:S(2)}) collective-permute-start(bf16[48,3072]{1,0:T(8,128)(2,1)S(1)} %copy-done.5), channel_id=1, source_target_pairs={{0,2},{1,3},{2,0},{3,1},{4,6},{5,7},{6,4},{7,5},{8,10},{9,11},{10,... | collective-permute-start | bytes 884744 | tf_op jit(solution)/shard_map/ppermute | solution.py:587
  29.3 1.8 %collective-permute-start.8 = (bf16[64,1920]{1,0:T(8,128)(2,1)S(1)}, bf16[64,1920]{1,0:T(8,128)(2,1)S(1)}, u32[]{:S(2)}, u32[]{:S(2)}) collective-permute-start(bf16[64,1920]{1,0:T(8,128)(2,1)S(1)} %collective-permute-done.w2), channel_id=1, source_target_pairs={{0,8},{4,12},{8,0},{12,4},{16,24},{20,28},{24,16},{28,20},{1,9},{5... | collective-permute-start | bytes 737288 | tf_op jit(solution)/shard_map/ppermute | solution.py:587
  31.9 3.4 %collective-permute-done.4.g2 = bf16[48,3072]{1,0:T(8,128)(2,1)S(1)} collective-permute-done((bf16[48,3072]{1,0:T(8,128)(2,1)S(1)}, bf16[48,3072]{1,0:T(8,128)(2,1)S(1)}, u32[]{:S(2)}, u32[]{:S(2)}) %collective-permute-start.4) | collective-permute-done | bytes 294944 | tf_op jit(solution)/shard_map/ppermute | solution.py:587
  35.3 1.8 %collective-permute-start.12 = (bf16[48,3072]{1,0:T(8,128)(2,1)S(1)}, bf16[48,3072]{1,0:T(8,128)(2,1)S(1)}, u32[]{:S(2)}, u32[]{:S(2)}) collective-permute-start(bf16[48,3072]{1,0:T(8,128)(2,1)S(1)} %collective-permute-done.4.g2), channel_id=1, source_target_pairs={{0,4},{4,0},{8,12},{12,8},{16,20},{20,16},{24,28},{28,24},{1,5},{5... | collective-permute-start | bytes 884744 | tf_op jit(solution)/shard_map/ppermute | solution.py:587
  37.8 1.7 %collective-permute-start.13 = (bf16[32,3072]{1,0:T(8,128)(2,1)S(1)}, bf16[32,3072]{1,0:T(8,128)(2,1)S(1)}, u32[]{:S(2)}, u32[]{:S(2)}) collective-permute-start(bf16[32,3072]{1,0:T(8,128)(2,1)S(1)} %copy-done.7), channel_id=1, source_target_pairs={{0,2},{1,3},{2,0},{3,1},{4,6},{5,7},{6,4},{7,5},{8,10},{9,11},{10,... | collective-permute-start | bytes 589832 | tf_op jit(solution)/shard_map/ppermute | solution.py:587
  39.5 2.9 %cross_forward.1 = (f32[256,512]{1,0:T(8,128)S(1)}, bf16[256,512]{1,0:T(8,128)(2,1)S(1)}, bf16[256,384]{1,0:T(8,128)(2,1)S(1)}, bf16[256,768]{1,0:T(8,128)(2,1)S...) custom-call(s32[5]{0:T(128)S(1)} %copy-done.4, ...), custom_call_target="tpu_custom_call" | custom-call | flops 1 | bytes 1 | tf_op jit(solution)/shard_map/cross_forward/pallas_call | solution.py:573
  42.5 2.6 %collective-permute-done.13.g4 = bf16[32,3072]{1,0:T(8,128)(2,1)S(1)} collective-permute-done((bf16[32,3072]{1,0:T(8,128)(2,1)S(1)}, bf16[32,3072]{1,0:T(8,128)(2,1)S(1)}, u32[]{:S(2)}, u32[]{:S(2)}) %collective-permute-start.13) | collective-permute-done | bytes 196640 | tf_op jit(solution)/shard_map/ppermute | solution.py:587
  47.6 4.0 %feed_forward.1 = (bf16[128,512]{1,0:T(8,128)(2,1)}, f32[256,512]{1,0:T(8,128)S(1)}, bf16[128,3072]{1,0:T(8,128)(2,1)S(1)}, bf16[128,3072]{1,0:T(8,128)(2,1)S(1)}, f32[8,512]{1,0:T(8,128)S(1)}) custom-call(s32[5]{0:T(128)S(1)} %copy-done.4, f32[256,512]{1,0:T(8,128)S(1)} %get-tuple-element.146.h2_ref, bf16[256,512]{1,0:T(8,128)(2,1)S(1)} %get-tuple-element.147.n3_ref, ...), custom_call_target="tpu_custom_call" | custom-call | flops 1 | bytes 1 | tf_op jit(solution)/shard_map/feed_forward/pallas_call | solution.py:573
  51.7 3.8 %cross_backward.1 = (f32[256,512]{1,0:T(8,128)S(1)}, bf16[256,384]{1,0:T(8,128)(2,1)S(1)}, f32[64,512]{1,0:T(8,128)S(1)}, f32[64,512]{1,0:T(8,128)S(1)}, bf16[12...) custom-call(s32[5]{0:T(128)S(1)} %copy-done.4, ...), custom_call_target="tpu_custom_call" | custom-call | flops 1 | bytes 1 | tf_op jit(solution)/shard_map/cross_backward/pallas_call | solution.py:573
  55.8 1.8 %collective-permute-start.20 = (bf16[64,3072]{1,0:T(8,128)(2,1)S(1)}, bf16[64,3072]{1,0:T(8,128)(2,1)S(1)}, u32[]{:S(2)}, u32[]{:S(2)}) collective-permute-start(bf16[64,3072]{1,0:T(8,128)(2,1)S(1)} %get-tuple-element.240), channel_id=1, source_target_pairs={{0,4},{1,9},{2,6},{3,11},{4,0},{5,13},{6,2},{7,15},{8,12},{9,1},{1... | collective-permute-start | bytes 1179656 | tf_op jit(solution)/shard_map/ppermute | solution.py:606
  57.7 6.0 %self_backward.1 = (bf16[256,384]{1,0:T(8,128)(2,1)S(1)}, bf16[512,768]{1,0:T(8,128)(2,1)S(1)}, f32[128,128]{1,0:T(8,128)S(1)}) custom-call(s32[5]{0:T(128)S(1)} %copy-done.4, bf16[256,384]{1,0:T(8,128)(2,1)S(1)} %get-tuple-element.169.mix_ref, bf16[256,384]{1,0:T(8,128)(2,1)S(1)} %get-tuple-element.170.q_ref, ...), custom_call_target="tpu_custom_call" | custom-call | flops 1 | bytes 1 | tf_op jit(solution)/shard_map/self_backward/pallas_call | solution.py:573
  63.9 1.7 %collective-permute-start.21 = (bf16[32,3072]{1,0:T(8,128)(2,1)S(1)}, bf16[32,3072]{1,0:T(8,128)(2,1)S(1)}, u32[]{:S(2)}, u32[]{:S(2)}) collective-permute-start(bf16[32,3072]{1,0:T(8,128)(2,1)S(1)} %get-tuple-element.244), channel_id=1, source_target_pairs={{0,8},{1,5},{2,10},{3,7},{4,12},{5,1},{6,14},{7,3},{8,0},{9,13},{1... | collective-permute-start | bytes 589832 | tf_op jit(solution)/shard_map/ppermute | solution.py:606
  65.8 2.2 %self_gradients.1 = (f32[128,512]{1,0:T(8,128)S(1)}, f32[128,512]{1,0:T(8,128)S(1)}, bf16[128,1280]{1,0:T(8,128)(2,1)S(1)}, bf16[128,1280]{1,0:T(8,128)(2,1)S(1)}) custom-call(s32[5]{0:T(128)S(1)} %copy-done.4, f32[256,512]{1,0:T(8,128)S(1)} %get-tuple-element.165.grad_h1_ref, bf16[512,512]{1,0:T(8,128)(2,1)S(1)} %get-tuple-element.141.x_ref, ...), custom_call_target="tpu_custom_call" | custom-call | flops 1 | bytes 1 | tf_op jit(solution)/shard_map/self_gradients/pallas_call | solution.py:573
  69.7 2.7 %collective-permute-start.22 = (bf16[32,3072]{1,0:T(8,128)(2,1)S(1)}, bf16[32,3072]{1,0:T(8,128)(2,1)S(1)}, u32[]{:S(2)}, u32[]{:S(2)}) collective-permute-start(bf16[32,3072]{1,0:T(8,128)(2,1)S(1)} %add_convert_fusion.6), channel_id=1, source_target_pairs={{0,16},{1,17},{2,18},{3,19},{4,20},{5,21},{6,22},{7,23},{8,24},{9,... | collective-permute-start | bytes 589832 | tf_op jit(solution)/shard_map/ppermute | solution.py:606
  72.5 1.7 %collective-permute-done.23 = bf16[64,1920]{1,0:T(8,128)(2,1)S(1)} collective-permute-done((bf16[64,1920]{1,0:T(8,128)(2,1)S(1)}, bf16[64,1920]{1,0:T(8,128)(2,1)S(1)}, u32[]{:S(2)}, u32[]{:S(2)}) %collective-permute-start.23) | collective-permute-done | bytes 245792 | tf_op jit(solution)/shard_map/ppermute | solution.py:606
  76.3 5.9 %collective-permute-done.22 = bf16[32,3072]{1,0:T(8,128)(2,1)S(1)} collective-permute-done((bf16[32,3072]{1,0:T(8,128)(2,1)S(1)}, bf16[32,3072]{1,0:T(8,128)(2,1)S(1)}, u32[]{:S(2)}, u32[]{:S(2)}) %collective-permute-start.22) | collective-permute-done | bytes 196640 | tf_op jit(solution)/shard_map/ppermute | solution.py:606
  82.8 1.8 %collective-permute-start.25 = (bf16[32,3072]{1,0:T(8,128)(2,1)S(1)}, bf16[32,3072]{1,0:T(8,128)(2,1)S(1)}, u32[]{:S(2)}, u32[]{:S(2)}) collective-permute-start(bf16[32,3072]{1,0:T(8,128)(2,1)S(1)} %add_convert_fusion.5), channel_id=1, source_target_pairs={{0,8},{1,5},{2,10},{3,7},{4,12},{5,1},{6,14},{7,3},{8,0},{9,13},{1... | collective-permute-start | bytes 589832 | tf_op jit(solution)/shard_map/ppermute | solution.py:606
  84.6 2.3 %collective-permute-start.32 = (bf16[32,1920]{1,0:T(8,128)(2,1)S(1)}, bf16[32,1920]{1,0:T(8,128)(2,1)S(1)}, u32[]{:S(2)}, u32[]{:S(2)}) collective-permute-start(bf16[32,1920]{1,0:T(8,128)(2,1)S(1)} %add_convert_fusion.9), channel_id=1, source_target_pairs={{0,16},{1,17},{2,18},{3,19},{4,20},{5,21},{6,22},{7,23},{8,24},{9,... | collective-permute-start | bytes 368648 | tf_op jit(solution)/shard_map/ppermute | solution.py:606
  87.0 2.3 %collective-permute-start.31 = (bf16[32,1280]{1,0:T(8,128)(2,1)S(1)}, bf16[32,1280]{1,0:T(8,128)(2,1)S(1)}, u32[]{:S(2)}, u32[]{:S(2)}) collective-permute-start(bf16[32,1280]{1,0:T(8,128)(2,1)S(1)} %add_convert_fusion.11), channel_id=1, source_target_pairs={{0,16},{1,17},{2,18},{3,19},{4,20},{5,21},{6,22},{7,23},{8,24},{9,... | collective-permute-start | bytes 245768 | tf_op jit(solution)/shard_map/ppermute | solution.py:606
  89.3 1.7 %collective-permute-done.25 = bf16[32,3072]{1,0:T(8,128)(2,1)S(1)} collective-permute-done((bf16[32,3072]{1,0:T(8,128)(2,1)S(1)}, bf16[32,3072]{1,0:T(8,128)(2,1)S(1)}, u32[]{:S(2)}, u32[]{:S(2)}) %collective-permute-start.25) | collective-permute-done | bytes 196640 | tf_op jit(solution)/shard_map/ppermute | solution.py:606
  91.6 1.8 %collective-permute-done.32 = bf16[32,1920]{1,0:T(8,128)(2,1)S(1)} collective-permute-done((bf16[32,1920]{1,0:T(8,128)(2,1)S(1)}, bf16[32,1920]{1,0:T(8,128)(2,1)S(1)}, u32[]{:S(2)}, u32[]{:S(2)}) %collective-permute-start.32) | collective-permute-done | bytes 122912 | tf_op jit(solution)/shard_map/ppermute | solution.py:606
  93.5 3.1 %collective-permute-start.34 = (bf16[32,1920]{1,0:T(8,128)(2,1)S(1)}, bf16[32,1920]{1,0:T(8,128)(2,1)S(1)}, u32[]{:S(2)}, u32[]{:S(2)}) collective-permute-start(bf16[32,1920]{1,0:T(8,128)(2,1)S(1)} %add_convert_fusion.8), channel_id=1, source_target_pairs={{0,8},{1,5},{2,10},{3,7},{4,12},{5,1},{6,14},{7,3},{8,0},{9,13},{1... | collective-permute-start | bytes 368648 | tf_op jit(solution)/shard_map/ppermute | solution.py:606
  101.8 1.6 %collective-permute-start.35 = (bf16[64,1280]{1,0:T(8,128)(2,1)S(1)}, bf16[64,1280]{1,0:T(8,128)(2,1)S(1)}, u32[]{:S(2)}, u32[]{:S(2)}) collective-permute-start(bf16[64,1280]{1,0:T(8,128)(2,1)S(1)} %constant_dynamic-update-slice_fusion.4.low_ref), channel_id=1, source_target_pairs={{0,4},{1,9},{2,6},{3,11},{4,0},{5,13},{6,2},{7,15},{8,12},{9,1},{1... | collective-permute-start | bytes 491528 | tf_op jit(solution)/shard_map/ppermute | solution.py:606
  104.2 1.8 %unpack_feed.1 = (f32[128,1024]{1,0:T(8,128)}, f32[128,1024]{1,0:T(8,128)}, f32[256,512]{1,0:T(8,128)}) custom-call(s32[5]{0:T(128)S(1)} %copy-done.4, bf16[64,3072]{1,0:T(8,128)(2,1)S(1)} %constant_dynamic-update-slice_fusion.low_ref, bf16[64,3072]{1,0:T(8,128)(2,1)S(1)} %collective-permute-done.37.high_ref), custom_call_target="tpu_custom_call" | custom-call | flops 1 | bytes 1 | tf_op jit(solution)/shard_map/unpack_feed/pallas_call | solution.py:573
  (99 shorter events, 21.1 us)
Async XLA Ops:
  2.6 15.1 %collective-permute-start.2 = (bf16[128,2048]{1,0:T(8,128)(2,1)}, bf16[128,2048]{1,0:T(8,128)(2,1)S(1)}, u32[]{:S(2)}, u32[]{:S(2)}) collective-permute-start(bf16[128,2048]{1,0:T(8,128)(2,1)} %pack_first.1.w0), channel_id=1, source_target_pairs={{0,2},{1,3},{2,0},{3,1},{4,6},{5,7},{6,4},{7,5},{8,10},{9,11},{10,... | collective-permute-start | bytes 1572872 | tf_op jit(solution)/shard_map/ppermute | solution.py:587
  5.6 14.3 %collective-permute-start.1 = (bf16[128,2048]{1,0:T(8,128)(2,1)}, bf16[128,2048]{1,0:T(8,128)(2,1)S(1)}, u32[]{:S(2)}, u32[]{:S(2)}) collective-permute-start(bf16[128,2048]{1,0:T(8,128)(2,1)} %pack_first.1.w0), channel_id=1, source_target_pairs={{0,1},{1,0},{2,3},{3,2},{4,5},{5,4},{6,7},{7,6},{8,9},{9,8},{10,11... | collective-permute-start | bytes 1572872 | tf_op jit(solution)/shard_map/ppermute | solution.py:587
  17.8 8.8 %collective-permute-start = (bf16[64,1920]{1,0:T(8,128)(2,1)S(1)}, bf16[64,1920]{1,0:T(8,128)(2,1)S(1)}, u32[]{:S(2)}, u32[]{:S(2)}) collective-permute-start(bf16[64,1920]{1,0:T(8,128)(2,1)S(1)} %copy-done.6), channel_id=1, source_target_pairs={{0,2},{1,3},{2,0},{3,1},{4,6},{5,7},{6,4},{7,5},{8,10},{9,11},{10,... | collective-permute-start | bytes 737288 | tf_op jit(solution)/shard_map/ppermute | solution.py:587
  19.6 9.8 %collective-permute-start.5 = (bf16[128,512]{1,0:T(8,128)(2,1)S(1)}, bf16[128,512]{1,0:T(8,128)(2,1)S(1)}, u32[]{:S(2)}, u32[]{:S(2)}) collective-permute-start(bf16[128,512]{1,0:T(8,128)(2,1)S(1)} %bitcast.19), channel_id=1, source_target_pairs={{0,2},{1,3},{2,0},{3,1},{4,6},{5,7},{6,4},{7,5},{8,10},{9,11},{10,... | collective-permute-start | bytes 393224 | tf_op jit(solution)/shard_map/ppermute | solution.py:587
  26.5 8.7 %collective-permute-start.4 = (bf16[48,3072]{1,0:T(8,128)(2,1)S(1)}, bf16[48,3072]{1,0:T(8,128)(2,1)S(1)}, u32[]{:S(2)}, u32[]{:S(2)}) collective-permute-start(bf16[48,3072]{1,0:T(8,128)(2,1)S(1)} %copy-done.5), channel_id=1, source_target_pairs={{0,2},{1,3},{2,0},{3,1},{4,6},{5,7},{6,4},{7,5},{8,10},{9,11},{10,... | collective-permute-start | bytes 884744 | tf_op jit(solution)/shard_map/ppermute | solution.py:587
  29.3 8.4 %collective-permute-start.8 = (bf16[64,1920]{1,0:T(8,128)(2,1)S(1)}, bf16[64,1920]{1,0:T(8,128)(2,1)S(1)}, u32[]{:S(2)}, u32[]{:S(2)}) collective-permute-start(bf16[64,1920]{1,0:T(8,128)(2,1)S(1)} %collective-permute-done.w2), channel_id=1, source_target_pairs={{0,8},{4,12},{8,0},{12,4},{16,24},{20,28},{24,16},{28,20},{1,9},{5... | collective-permute-start | bytes 737288 | tf_op jit(solution)/shard_map/ppermute | solution.py:587
  31.2 8.4 %collective-permute-start.7 = (bf16[128,1920]{1,0:T(8,128)(2,1)S(1)}, bf16[128,1920]{1,0:T(8,128)(2,1)S(1)}, u32[]{:S(2)}, u32[]{:S(2)}) collective-permute-start(bf16[128,1920]{1,0:T(8,128)(2,1)S(1)} %copy-done.1), channel_id=1, source_target_pairs={{0,1},{1,0},{2,3},{3,2},{4,5},{5,4},{6,7},{7,6},{8,9},{9,8},{10,11... | collective-permute-start | bytes 1474568 | tf_op jit(solution)/shard_map/ppermute | solution.py:587
  31.4 16.2 %collective-permute-start.11 = (bf16[128,3072]{1,0:T(8,128)(2,1)S(1)}, bf16[128,3072]{1,0:T(8,128)(2,1)S(1)}, u32[]{:S(2)}, u32[]{:S(2)}) collective-permute-start(bf16[128,3072]{1,0:T(8,128)(2,1)S(1)} %copy-done.2), channel_id=1, source_target_pairs={{0,1},{1,0},{2,3},{3,2},{4,5},{5,4},{6,7},{7,6},{8,9},{9,8},{10,11... | collective-permute-start | bytes 2359304 | tf_op jit(solution)/shard_map/ppermute | solution.py:587
  31.7 6.1 %collective-permute-start.9 = (bf16[64,1920]{1,0:T(8,128)(2,1)S(1)}, bf16[64,1920]{1,0:T(8,128)(2,1)S(1)}, u32[]{:S(2)}, u32[]{:S(2)}) collective-permute-start(bf16[64,1920]{1,0:T(8,128)(2,1)S(1)} %collective-permute-done.w2), channel_id=1, source_target_pairs={{0,1},{1,0},{2,3},{3,2},{4,5},{5,4},{6,7},{7,6},{8,9},{9,8},{10,11... | collective-permute-start | bytes 737288 | tf_op jit(solution)/shard_map/ppermute | solution.py:587
  35.3 9.8 %collective-permute-start.12 = (bf16[48,3072]{1,0:T(8,128)(2,1)S(1)}, bf16[48,3072]{1,0:T(8,128)(2,1)S(1)}, u32[]{:S(2)}, u32[]{:S(2)}) collective-permute-start(bf16[48,3072]{1,0:T(8,128)(2,1)S(1)} %collective-permute-done.4.g2), channel_id=1, source_target_pairs={{0,4},{4,0},{8,12},{12,8},{16,20},{20,16},{24,28},{28,24},{1,5},{5... | collective-permute-start | bytes 884744 | tf_op jit(solution)/shard_map/ppermute | solution.py:587
  37.8 7.3 %collective-permute-start.13 = (bf16[32,3072]{1,0:T(8,128)(2,1)S(1)}, bf16[32,3072]{1,0:T(8,128)(2,1)S(1)}, u32[]{:S(2)}, u32[]{:S(2)}) collective-permute-start(bf16[32,3072]{1,0:T(8,128)(2,1)S(1)} %copy-done.7), channel_id=1, source_target_pairs={{0,2},{1,3},{2,0},{3,1},{4,6},{5,7},{6,4},{7,5},{8,10},{9,11},{10,... | collective-permute-start | bytes 589832 | tf_op jit(solution)/shard_map/ppermute | solution.py:587
  45.1 2.5 %collective-permute-start.15 = (bf16[48,3072]{1,0:T(8,128)(2,1)S(1)}, bf16[48,3072]{1,0:T(8,128)(2,1)S(1)}, u32[]{:S(2)}, u32[]{:S(2)}) collective-permute-start(bf16[48,3072]{1,0:T(8,128)(2,1)S(1)} %collective-permute-done.12.g3), channel_id=1, source_target_pairs={{0,1},{1,0},{2,3},{3,2},{4,5},{5,4},{6,7},{7,6},{8,9},{9,8},{10,11... | collective-permute-start | bytes 884744 | tf_op jit(solution)/shard_map/ppermute | solution.py:587
  51.6 4.0 %collective-permute-start.19 = (bf16[128,3072]{1,0:T(8,128)(2,1)S(1)}, bf16[128,3072]{1,0:T(8,128)(2,1)S(1)}, u32[]{:S(2)}, u32[]{:S(2)}) collective-permute-start(bf16[128,3072]{1,0:T(8,128)(2,1)S(1)} %get-tuple-element.164), channel_id=1, source_target_pairs={{0,1},{1,0},{2,3},{3,2},{4,5},{5,4},{6,7},{7,6},{8,9},{9,8},{10,11... | collective-permute-start | bytes 2359304 | tf_op jit(solution)/shard_map/ppermute | solution.py:587
  55.8 8.0 %collective-permute-start.20 = (bf16[64,3072]{1,0:T(8,128)(2,1)S(1)}, bf16[64,3072]{1,0:T(8,128)(2,1)S(1)}, u32[]{:S(2)}, u32[]{:S(2)}) collective-permute-start(bf16[64,3072]{1,0:T(8,128)(2,1)S(1)} %get-tuple-element.240), channel_id=1, source_target_pairs={{0,4},{1,9},{2,6},{3,11},{4,0},{5,13},{6,2},{7,15},{8,12},{9,1},{1... | collective-permute-start | bytes 1179656 | tf_op jit(solution)/shard_map/ppermute | solution.py:606
  57.6 6.3 %collective-permute-start.18 = (bf16[128,1920]{1,0:T(8,128)(2,1)S(1)}, bf16[128,1920]{1,0:T(8,128)(2,1)S(1)}, u32[]{:S(2)}, u32[]{:S(2)}) collective-permute-start(bf16[128,1920]{1,0:T(8,128)(2,1)S(1)} %get-tuple-element.162), channel_id=1, source_target_pairs={{0,1},{1,0},{2,3},{3,2},{4,5},{5,4},{6,7},{7,6},{8,9},{9,8},{10,11... | collective-permute-start | bytes 1474568 | tf_op jit(solution)/shard_map/ppermute | solution.py:587
  63.9 5.7 %collective-permute-start.21 = (bf16[32,3072]{1,0:T(8,128)(2,1)S(1)}, bf16[32,3072]{1,0:T(8,128)(2,1)S(1)}, u32[]{:S(2)}, u32[]{:S(2)}) collective-permute-start(bf16[32,3072]{1,0:T(8,128)(2,1)S(1)} %get-tuple-element.244), channel_id=1, source_target_pairs={{0,8},{1,5},{2,10},{3,7},{4,12},{5,1},{6,14},{7,3},{8,0},{9,13},{1... | collective-permute-start | bytes 589832 | tf_op jit(solution)/shard_map/ppermute | solution.py:606
  67.9 6.3 %collective-permute-start.23 = (bf16[64,1920]{1,0:T(8,128)(2,1)S(1)}, bf16[64,1920]{1,0:T(8,128)(2,1)S(1)}, u32[]{:S(2)}, u32[]{:S(2)}) collective-permute-start(bf16[64,1920]{1,0:T(8,128)(2,1)S(1)} %get-tuple-element.242), channel_id=1, source_target_pairs={{0,4},{1,9},{2,6},{3,11},{4,0},{5,13},{6,2},{7,15},{8,12},{9,1},{1... | collective-permute-start | bytes 737288 | tf_op jit(solution)/shard_map/ppermute | solution.py:606
  69.5 2.9 %collective-permute-start.24 = (bf16[128,1280]{1,0:T(8,128)(2,1)S(1)}, bf16[128,1280]{1,0:T(8,128)(2,1)S(1)}, u32[]{:S(2)}, u32[]{:S(2)}) collective-permute-start(bf16[128,1280]{1,0:T(8,128)(2,1)S(1)} %get-tuple-element.193), channel_id=1, source_target_pairs={{0,1},{1,0},{2,3},{3,2},{4,5},{5,4},{6,7},{7,6},{8,9},{9,8},{10,11... | collective-permute-start | bytes 983048 | tf_op jit(solution)/shard_map/ppermute | solution.py:587
  69.7 12.5 %collective-permute-start.22 = (bf16[32,3072]{1,0:T(8,128)(2,1)S(1)}, bf16[32,3072]{1,0:T(8,128)(2,1)S(1)}, u32[]{:S(2)}, u32[]{:S(2)}) collective-permute-start(bf16[32,3072]{1,0:T(8,128)(2,1)S(1)} %add_convert_fusion.6), channel_id=1, source_target_pairs={{0,16},{1,17},{2,18},{3,19},{4,20},{5,21},{6,22},{7,23},{8,24},{9,... | collective-permute-start | bytes 589832 | tf_op jit(solution)/shard_map/ppermute | solution.py:606
  74.3 8.1 %collective-permute-start.27 = (bf16[32,1920]{1,0:T(8,128)(2,1)S(1)}, bf16[32,1920]{1,0:T(8,128)(2,1)S(1)}, u32[]{:S(2)}, u32[]{:S(2)}) collective-permute-start(bf16[32,1920]{1,0:T(8,128)(2,1)S(1)} %get-tuple-element.248), channel_id=1, source_target_pairs={{0,8},{1,5},{2,10},{3,7},{4,12},{5,1},{6,14},{7,3},{8,0},{9,13},{1... | collective-permute-start | bytes 368648 | tf_op jit(solution)/shard_map/ppermute | solution.py:606
  74.7 7.7 %collective-permute-start.26 = (bf16[64,1280]{1,0:T(8,128)(2,1)S(1)}, bf16[64,1280]{1,0:T(8,128)(2,1)S(1)}, u32[]{:S(2)}, u32[]{:S(2)}) collective-permute-start(bf16[64,1280]{1,0:T(8,128)(2,1)S(1)} %get-tuple-element.246), channel_id=1, source_target_pairs={{0,4},{1,9},{2,6},{3,11},{4,0},{5,13},{6,2},{7,15},{8,12},{9,1},{1... | collective-permute-start | bytes 491528 | tf_op jit(solution)/shard_map/ppermute | solution.py:606
  82.5 4.5 %collective-permute-start.28 = (bf16[32,1280]{1,0:T(8,128)(2,1)S(1)}, bf16[32,1280]{1,0:T(8,128)(2,1)S(1)}, u32[]{:S(2)}, u32[]{:S(2)}) collective-permute-start(bf16[32,1280]{1,0:T(8,128)(2,1)S(1)} %get-tuple-element.250), channel_id=1, source_target_pairs={{0,8},{1,5},{2,10},{3,7},{4,12},{5,1},{6,14},{7,3},{8,0},{9,13},{1... | collective-permute-start | bytes 245768 | tf_op jit(solution)/shard_map/ppermute | solution.py:606
  82.8 8.2 %collective-permute-start.25 = (bf16[32,3072]{1,0:T(8,128)(2,1)S(1)}, bf16[32,3072]{1,0:T(8,128)(2,1)S(1)}, u32[]{:S(2)}, u32[]{:S(2)}) collective-permute-start(bf16[32,3072]{1,0:T(8,128)(2,1)S(1)} %add_convert_fusion.5), channel_id=1, source_target_pairs={{0,8},{1,5},{2,10},{3,7},{4,12},{5,1},{6,14},{7,3},{8,0},{9,13},{1... | collective-permute-start | bytes 589832 | tf_op jit(solution)/shard_map/ppermute | solution.py:606
  84.6 8.9 %collective-permute-start.32 = (bf16[32,1920]{1,0:T(8,128)(2,1)S(1)}, bf16[32,1920]{1,0:T(8,128)(2,1)S(1)}, u32[]{:S(2)}, u32[]{:S(2)}) collective-permute-start(bf16[32,1920]{1,0:T(8,128)(2,1)S(1)} %add_convert_fusion.9), channel_id=1, source_target_pairs={{0,16},{1,17},{2,18},{3,19},{4,20},{5,21},{6,22},{7,23},{8,24},{9,... | collective-permute-start | bytes 368648 | tf_op jit(solution)/shard_map/ppermute | solution.py:606
  87.0 10.1 %collective-permute-start.31 = (bf16[32,1280]{1,0:T(8,128)(2,1)S(1)}, bf16[32,1280]{1,0:T(8,128)(2,1)S(1)}, u32[]{:S(2)}, u32[]{:S(2)}) collective-permute-start(bf16[32,1280]{1,0:T(8,128)(2,1)S(1)} %add_convert_fusion.11), channel_id=1, source_target_pairs={{0,16},{1,17},{2,18},{3,19},{4,20},{5,21},{6,22},{7,23},{8,24},{9,... | collective-permute-start | bytes 245768 | tf_op jit(solution)/shard_map/ppermute | solution.py:606
  91.1 13.1 %collective-permute-start.37 = (bf16[64,3072]{1,0:T(8,128)(2,1)S(1)}, bf16[64,3072]{1,0:T(8,128)(2,1)S(1)}, u32[]{:S(2)}, u32[]{:S(2)}) collective-permute-start(bf16[64,3072]{1,0:T(8,128)(2,1)S(1)} %constant_dynamic-update-slice_fusion.low_ref), channel_id=1, source_target_pairs={{0,4},{1,9},{2,6},{3,11},{4,0},{5,13},{6,2},{7,15},{8,12},{9,1},{1... | collective-permute-start | bytes 1179656 | tf_op jit(solution)/shard_map/ppermute | solution.py:606
  93.5 6.0 %collective-permute-start.34 = (bf16[32,1920]{1,0:T(8,128)(2,1)S(1)}, bf16[32,1920]{1,0:T(8,128)(2,1)S(1)}, u32[]{:S(2)}, u32[]{:S(2)}) collective-permute-start(bf16[32,1920]{1,0:T(8,128)(2,1)S(1)} %add_convert_fusion.8), channel_id=1, source_target_pairs={{0,8},{1,5},{2,10},{3,7},{4,12},{5,1},{6,14},{7,3},{8,0},{9,13},{1... | collective-permute-start | bytes 368648 | tf_op jit(solution)/shard_map/ppermute | solution.py:606
  96.6 3.9 %collective-permute-start.30 = (f32[64,512]{1,0:T(8,128)S(1)}, f32[64,512]{1,0:T(8,128)S(1)}, u32[]{:S(2)}, u32[]{:S(2)}) collective-permute-start(f32[64,512]{1,0:T(8,128)S(1)} %get-tuple-element.210), channel_id=1, source_target_pairs={{0,1},{1,0},{2,3},{3,2},{4,5},{5,4},{6,7},{7,6},{8,9},{9,8},{10,11... | collective-permute-start | bytes 393224 | tf_op jit(solution)/shard_map/ppermute | solution.py:587
  96.6 6.9 %collective-permute-start.29 = (f32[128,512]{1,0:T(8,128)S(1)}, f32[128,512]{1,0:T(8,128)S(1)}, u32[]{:S(2)}, u32[]{:S(2)}) collective-permute-start(f32[128,512]{1,0:T(8,128)S(1)} %get-tuple-element.208), channel_id=1, source_target_pairs={{0,1},{1,0},{2,3},{3,2},{4,5},{5,4},{6,7},{7,6},{8,9},{9,8},{10,11... | collective-permute-start | bytes 786440 | tf_op jit(solution)/shard_map/ppermute | solution.py:587
  97.1 4.7 %collective-permute-start.33 = (bf16[32,1280]{1,0:T(8,128)(2,1)S(1)}, bf16[32,1280]{1,0:T(8,128)(2,1)S(1)}, u32[]{:S(2)}, u32[]{:S(2)}) collective-permute-start(bf16[32,1280]{1,0:T(8,128)(2,1)S(1)} %add_convert_fusion.10), channel_id=1, source_target_pairs={{0,8},{1,5},{2,10},{3,7},{4,12},{5,1},{6,14},{7,3},{8,0},{9,13},{1... | collective-permute-start | bytes 245768 | tf_op jit(solution)/shard_map/ppermute | solution.py:606
  99.5 6.5 %collective-permute-start.36 = (bf16[64,1920]{1,0:T(8,128)(2,1)S(1)}, bf16[64,1920]{1,0:T(8,128)(2,1)S(1)}, u32[]{:S(2)}, u32[]{:S(2)}) collective-permute-start(bf16[64,1920]{1,0:T(8,128)(2,1)S(1)} %constant_dynamic-update-slice_fusion.2.low_ref), channel_id=1, source_target_pairs={{0,4},{1,9},{2,6},{3,11},{4,0},{5,13},{6,2},{7,15},{8,12},{9,1},{1... | collective-permute-start | bytes 737288 | tf_op jit(solution)/shard_map/ppermute | solution.py:606
  101.8 5.7 %collective-permute-start.35 = (bf16[64,1280]{1,0:T(8,128)(2,1)S(1)}, bf16[64,1280]{1,0:T(8,128)(2,1)S(1)}, u32[]{:S(2)}, u32[]{:S(2)}) collective-permute-start(bf16[64,1280]{1,0:T(8,128)(2,1)S(1)} %constant_dynamic-update-slice_fusion.4.low_ref), channel_id=1, source_target_pairs={{0,4},{1,9},{2,6},{3,11},{4,0},{5,13},{6,2},{7,15},{8,12},{9,1},{1... | collective-permute-start | bytes 491528 | tf_op jit(solution)/shard_map/ppermute | solution.py:606
  (14 other events, 118.1 us)
